TPU v7x, 32 devices: a whole 2x2x4 slice. The times are simulated.
32 devices in a mesh: dp: 4 (over y, core), fsdp: 8 (over z, x).
Axes of the slice: x: 2, y: 2, z: 4, core: 2. Of those that a mesh axis runs over, the one named last changes fastest.
Arguments:
- target: bfloat16 [32768, 768], P(('dp', 'fsdp')), may hold values from -6 to 6
- memory: bfloat16 [128, 1024, 768], P(('dp', 'fsdp')), may hold values from -6 to 6
- cotangent: bfloat16 [32768, 768], P(('dp', 'fsdp')), may hold values from -6 to 6
- bucket: int32 [32], P(('dp', 'fsdp')), may hold values from 0 to 1
- source_len: int32 [128], P(('dp', 'fsdp')), may hold values from 256 to 1024, as said below
- self_qkv: bfloat16 [3, 768, 768], P(None, 'fsdp'), may hold values from -0.21875 to 0.21875
- self_out: bfloat16 [768, 768], P('fsdp'), may hold values from -0.875 to 0.875
- self_bias: bfloat16 [3, 768], P(None, 'fsdp'), may hold values from -3 to 3
- cross_qkv: bfloat16 [3, 768, 768], P(None, 'fsdp'), may hold values from -0.21875 to 0.21875
- cross_out: bfloat16 [768, 768], P('fsdp'), may hold values from -0.875 to 0.875
- cross_bias: bfloat16 [3, 768], P(None, 'fsdp'), may hold values from -3 to 3
- ffn_in: bfloat16 [768, 3072], P('fsdp'), may hold values from -0.21875 to 0.21875
- ffn_in_bias: bfloat16 [3072], P('fsdp'), may hold values from -3 to 3
- ffn_out: bfloat16 [3072, 768], P('fsdp'), may hold values from -0.109375 to 0.109375
- ffn_out_bias: bfloat16 [768], P('fsdp'), may hold values from -3 to 3
- norm_gain: bfloat16 [3, 768], P(None, 'fsdp'), may hold values from 0.25 to 1.75
- norm_bias: bfloat16 [3, 768], P(None, 'fsdp'), may hold values from -2 to 2
Outputs:
- output: bfloat16 [32768, 768], P(('dp', 'fsdp'))
- target_grad: float32 [32768, 768], P(('dp', 'fsdp'))
- memory_grad: float32 [128, 1024, 768], P(('dp', 'fsdp'))
- grad_self_qkv: float32 [3, 768, 768], P(None, 'fsdp')
- grad_self_out: float32 [768, 768], P('fsdp')
- grad_self_bias: float32 [3, 768], P(None, 'fsdp')
- grad_cross_qkv: float32 [3, 768, 768], P(None, 'fsdp')
- grad_cross_out: float32 [768, 768], P('fsdp')
- grad_cross_bias: float32 [3, 768], P(None, 'fsdp')
- grad_ffn_in: float32 [768, 3072], P('fsdp')
- grad_ffn_in_bias: float32 [3072], P('fsdp')
- grad_ffn_out: float32 [3072, 768], P('fsdp')
- grad_ffn_out_bias: float32 [768], P('fsdp')
- grad_norm_gain: float32 [3, 768], P(None, 'fsdp')
- grad_norm_bias: float32 [3, 768], P(None, 'fsdp')
Inputs may be any that keep to these rules, and one draw needn't show every extreme that they name: bucket 1: the device's 1024 tokens are 4 rows of 256, row r reading memory row r of the device; bucket 0: they are one row, which reads the device's first memory row. `source_len`: some memory row has all 1024 tokens valid.
All inputs are finite; a program needn't handle non-finite values.
Results may differ from a plain program's by a relative error of at most 0.024.
The roundings to bfloat16 on the way count: a program that leaves them out, or rounds other values in their place, can miss the bound.
Values may be sent and summed in bfloat16 or wider, within the bound.
No kernel may reach another device: no remote copies, remote signals or barrier semaphores. Data moves between devices by JAX's collectives and lax.ppermute only.
A program may use at most 384 MiB of HBM per device.

v0:
```python
import jax
import jax.numpy as jnp
from jax import lax
from jax.sharding import PartitionSpec as P

HEAD = 64


very_low = -1e30
epsilon = 1e-05


def layer_norm(total, norm_scale, shift):
    middle = jnp.mean(total, -1, keepdims=True)
    centred = total - middle
    variance = jnp.mean(centred * centred, -1, keepdims=True)
    return centred * lax.rsqrt(variance + epsilon) * norm_scale + shift


def gelu_exact(value):
    return jax.nn.gelu(value, approximate=False)


def inner_rows(left, right):
    return lax.dot_general(
        left, right, (((0,), (0,)), ((), ())), preferred_element_type=jnp.float32
    )


def against(left, right):
    return lax.dot_general(
        left, right, (((1,), (1,)), ((), ())), preferred_element_type=jnp.float32
    )


def attend(queries, keys, values, valid):
    scores = jnp.einsum("bqhe,bkhe->bhqk", queries, keys, preferred_element_type=jnp.float32)
    scores = jnp.where(valid[:, None], scores, very_low)
    highest = jnp.max(scores, -1, keepdims=True)
    raised = jnp.exp(scores - highest)
    summed = jnp.sum(raised, -1, keepdims=True)
    shares_low = (raised / summed).astype(jnp.bfloat16)
    context = jnp.einsum("bhqk,bkhe->bqhe", shares_low, values, preferred_element_type=jnp.float32)
    return (context, highest + jnp.log(summed))


def attend_back(queries, keys, values, valid, logsum, grad_context):
    scores = jnp.einsum("bqhe,bkhe->bhqk", queries, keys, preferred_element_type=jnp.float32)
    scores = jnp.where(valid[:, None], scores, very_low)
    shares = jnp.exp(scores - logsum)
    shares_low = shares.astype(jnp.bfloat16)
    grad_values = jnp.einsum(
        "bhqk,bqhe->bkhe", shares_low, grad_context, preferred_element_type=jnp.float32
    )
    grad_shares = jnp.einsum(
        "bqhe,bkhe->bhqk", grad_context, values, preferred_element_type=jnp.float32
    )
    inner_sum = jnp.sum(grad_shares * shares, -1, keepdims=True)
    grad_scores = (shares * (grad_shares - inner_sum)).astype(jnp.bfloat16)
    grad_queries = jnp.einsum(
        "bhqk,bkhe->bqhe", grad_scores, keys, preferred_element_type=jnp.float32
    )
    grad_keys = jnp.einsum(
        "bhqk,bqhe->bkhe", grad_scores, queries, preferred_element_type=jnp.float32
    )
    return (grad_queries, grad_keys, grad_values)


def fold_rows(grads, chosen, row_count):
    total = jnp.zeros_like(grads)
    for group in range(row_count):
        hit = (jnp.arange(row_count, dtype=jnp.int32) == chosen[group])[:, None, None, None]
        total = total + jnp.where(hit, grads[group][None], 0.0)
    return total


def spread_rows(array, axis_dim, fsdp_count, dp_count):
    layout = array.shape
    length = layout[axis_dim]
    parted = array.reshape(
        layout[:axis_dim]
        + (fsdp_count, dp_count, length // (fsdp_count * dp_count))
        + layout[axis_dim + 1 :]
    )
    return jnp.swapaxes(parted, axis_dim, axis_dim + 1).reshape(layout)


def on_device(
    target,
    memory,
    cotangent,
    bucket,
    source_len,
    self_qkv,
    self_out,
    self_bias,
    cross_qkv,
    cross_out,
    cross_bias,
    ffn_in,
    ffn_in_bias,
    ffn_out,
    ffn_out_bias,
    norm_gain,
    norm_bias,
):
    gathered = (
        lax.all_gather(self_qkv, "fsdp", axis=1, tiled=True),
        lax.all_gather(self_out, "fsdp", axis=0, tiled=True),
        lax.all_gather(self_bias, "fsdp", axis=1, tiled=True),
        lax.all_gather(cross_qkv, "fsdp", axis=1, tiled=True),
        lax.all_gather(cross_out, "fsdp", axis=0, tiled=True),
        lax.all_gather(cross_bias, "fsdp", axis=1, tiled=True),
        lax.all_gather(ffn_in, "fsdp", axis=0, tiled=True),
        lax.all_gather(ffn_in_bias, "fsdp", axis=0, tiled=True),
        lax.all_gather(ffn_out, "fsdp", axis=0, tiled=True),
        lax.all_gather(ffn_out_bias, "fsdp", axis=0, tiled=True),
        lax.all_gather(norm_gain, "fsdp", axis=1, tiled=True),
        lax.all_gather(norm_bias, "fsdp", axis=1, tiled=True),
    )
    (
        self_qkv_w,
        self_out_w,
        self_bias_w,
        cross_qkv_w,
        cross_out_w,
        cross_bias_w,
        ffn_in_w,
        ffn_in_bias_w,
        ffn_out_w,
        ffn_out_bias_w,
        gain_all,
        shift_all,
    ) = gathered
    tokens = target.shape[0]
    row_count = memory.shape[0]
    mem_len = memory.shape[1]
    model_width = target.shape[1]
    head_count = model_width // HEAD
    short_len = tokens // row_count
    block_rows = min(512, tokens)
    group_block = block_rows // short_len
    query_scale = HEAD ** (-0.5)
    bucket_id = bucket[0]
    target_full = target.astype(jnp.float32)
    index = jnp.arange(tokens, dtype=jnp.int32)
    row_of = jnp.where(bucket_id == 1, index // short_len, 0)
    place = jnp.where(bucket_id == 1, index % short_len, index)
    allowed = (row_of[:, None] == row_of[None, :]) & (place[None, :] <= place[:, None])
    query_self = (
        (jnp.dot(target, self_qkv_w[0], preferred_element_type=jnp.float32) + self_bias_w[0])
        * query_scale
    ).astype(jnp.bfloat16)
    key_self = jnp.dot(target, self_qkv_w[1], preferred_element_type=jnp.float32).astype(
        jnp.bfloat16
    )
    value_self = (
        jnp.dot(target, self_qkv_w[2], preferred_element_type=jnp.float32) + self_bias_w[1]
    ).astype(jnp.bfloat16)
    heads_query = query_self.reshape(1, tokens, head_count, HEAD)
    heads_key = key_self.reshape(1, tokens, head_count, HEAD)
    heads_value = value_self.reshape(1, tokens, head_count, HEAD)
    self_parts = []
    self_sums = []
    for part_no in range(tokens // block_rows):
        low_row = part_no * block_rows
        high_row = low_row + block_rows
        context, logsum = attend(
            heads_query[:, low_row:high_row],
            heads_key[:, :high_row],
            heads_value[:, :high_row],
            allowed[None, low_row:high_row, :high_row],
        )
        self_parts.append(context.reshape(block_rows, model_width))
        self_sums.append(logsum)
    context_self = jnp.concatenate(self_parts, 0).astype(jnp.bfloat16)
    branch_self = (
        jnp.dot(context_self, self_out_w, preferred_element_type=jnp.float32) + self_bias_w[2]
    )
    first, pull_first = jax.vjp(
        layer_norm,
        target_full + branch_self,
        gain_all[0].astype(jnp.float32),
        shift_all[0].astype(jnp.float32),
    )
    first_low = first.astype(jnp.bfloat16)
    query_cross = (
        (jnp.dot(first_low, cross_qkv_w[0], preferred_element_type=jnp.float32) + cross_bias_w[0])
        * query_scale
    ).astype(jnp.bfloat16)
    key_all = jnp.einsum(
        "rmd,de->rme", memory, cross_qkv_w[1], preferred_element_type=jnp.float32
    ).astype(jnp.bfloat16)
    value_all = (
        jnp.einsum("rmd,de->rme", memory, cross_qkv_w[2], preferred_element_type=jnp.float32)
        + cross_bias_w[1]
    ).astype(jnp.bfloat16)
    chosen = jnp.where(bucket_id == 1, jnp.arange(row_count, dtype=jnp.int32), 0)
    key_chosen = jnp.take(key_all, chosen, axis=0).reshape(row_count, mem_len, head_count, HEAD)
    value_chosen = jnp.take(value_all, chosen, axis=0).reshape(row_count, mem_len, head_count, HEAD)
    reach = jnp.arange(mem_len, dtype=jnp.int32)[None, :] < jnp.take(source_len, chosen)[:, None]
    cross_query = query_cross.reshape(row_count, short_len, head_count, HEAD)
    cross_parts = []
    cross_sums = []
    for part_no in range(row_count // group_block):
        low_group = part_no * group_block
        high_group = low_group + group_block
        valid = jnp.broadcast_to(
            reach[low_group:high_group, None, :], (group_block, short_len, mem_len)
        )
        context, logsum = attend(
            cross_query[low_group:high_group],
            key_chosen[low_group:high_group],
            value_chosen[low_group:high_group],
            valid,
        )
        cross_parts.append(context.reshape(group_block * short_len, model_width))
        cross_sums.append(logsum)
    context_cross = jnp.concatenate(cross_parts, 0).astype(jnp.bfloat16)
    branch_cross = (
        jnp.dot(context_cross, cross_out_w, preferred_element_type=jnp.float32) + cross_bias_w[2]
    )
    second, pull_second = jax.vjp(
        layer_norm,
        first + branch_cross,
        gain_all[1].astype(jnp.float32),
        shift_all[1].astype(jnp.float32),
    )
    second_low = second.astype(jnp.bfloat16)
    hidden = jnp.dot(second_low, ffn_in_w, preferred_element_type=jnp.float32) + ffn_in_bias_w
    active, pull_active = jax.vjp(gelu_exact, hidden)
    active_low = active.astype(jnp.bfloat16)
    branch_ffn = jnp.dot(active_low, ffn_out_w, preferred_element_type=jnp.float32) + ffn_out_bias_w
    final, pull_final = jax.vjp(
        layer_norm,
        second + branch_ffn,
        gain_all[2].astype(jnp.float32),
        shift_all[2].astype(jnp.float32),
    )
    output = final.astype(jnp.bfloat16)
    regathered = (
        lax.all_gather(self_qkv, "fsdp", axis=1, tiled=True),
        lax.all_gather(self_out, "fsdp", axis=0, tiled=True),
        lax.all_gather(cross_qkv, "fsdp", axis=1, tiled=True),
        lax.all_gather(cross_out, "fsdp", axis=0, tiled=True),
        lax.all_gather(ffn_in, "fsdp", axis=0, tiled=True),
        lax.all_gather(ffn_out, "fsdp", axis=0, tiled=True),
    )
    self_qkv_b, self_out_b, cross_qkv_b, cross_out_b, ffn_in_b, ffn_out_b = regathered
    grad_final, grad_gain_last, grad_shift_last = pull_final(cotangent.astype(jnp.float32))
    grad_branch = grad_final.astype(jnp.bfloat16)
    grad_ffn_out_w = inner_rows(active_low, grad_branch)
    grad_ffn_out_bias_w = jnp.sum(grad_branch.astype(jnp.float32), 0)
    grad_active = against(grad_branch, ffn_out_b)
    grad_hidden = pull_active(grad_active)[0].astype(jnp.bfloat16)
    grad_ffn_in_w = inner_rows(second_low, grad_hidden)
    grad_ffn_in_bias_w = jnp.sum(grad_hidden.astype(jnp.float32), 0)
    grad_second = grad_final + against(grad_hidden, ffn_in_b)
    grad_mid, grad_gain_mid, grad_shift_mid = pull_second(grad_second)
    grad_branch = grad_mid.astype(jnp.bfloat16)
    grad_cross_out_w = inner_rows(context_cross, grad_branch)
    grad_cross_last = jnp.sum(grad_branch.astype(jnp.float32), 0)
    grad_context = (
        against(grad_branch, cross_out_b)
        .astype(jnp.bfloat16)
        .reshape(row_count, short_len, head_count, HEAD)
    )
    query_parts = []
    key_parts = []
    value_parts = []
    for part_no in range(row_count // group_block):
        low_group = part_no * group_block
        high_group = low_group + group_block
        valid = jnp.broadcast_to(
            reach[low_group:high_group, None, :], (group_block, short_len, mem_len)
        )
        grad_queries, grad_keys, grad_values = attend_back(
            cross_query[low_group:high_group],
            key_chosen[low_group:high_group],
            value_chosen[low_group:high_group],
            valid,
            cross_sums[part_no],
            grad_context[low_group:high_group],
        )
        query_parts.append(grad_queries)
        key_parts.append(grad_keys)
        value_parts.append(grad_values)
    grad_query_low = (
        jnp.concatenate(query_parts, 0).reshape(tokens, model_width).astype(jnp.bfloat16)
    )
    grad_query_raw = (grad_query_low.astype(jnp.float32) * query_scale).astype(jnp.bfloat16)
    grad_key_low = (
        fold_rows(jnp.concatenate(key_parts, 0), chosen, row_count)
        .reshape(row_count, mem_len, model_width)
        .astype(jnp.bfloat16)
    )
    grad_value_low = (
        fold_rows(jnp.concatenate(value_parts, 0), chosen, row_count)
        .reshape(row_count, mem_len, model_width)
        .astype(jnp.bfloat16)
    )
    grad_cross_qkv_w = jnp.stack(
        [
            inner_rows(first_low, grad_query_raw),
            jnp.einsum("rmd,rme->de", memory, grad_key_low, preferred_element_type=jnp.float32),
            jnp.einsum("rmd,rme->de", memory, grad_value_low, preferred_element_type=jnp.float32),
        ]
    )
    grad_cross_bias_w = jnp.stack(
        [
            jnp.sum(grad_query_raw.astype(jnp.float32), 0),
            jnp.sum(grad_value_low.astype(jnp.float32), (0, 1)),
            grad_cross_last,
        ]
    )
    memory_grad = jnp.einsum(
        "rme,de->rmd", grad_key_low, cross_qkv_b[1], preferred_element_type=jnp.float32
    ) + jnp.einsum(
        "rme,de->rmd", grad_value_low, cross_qkv_b[2], preferred_element_type=jnp.float32
    )
    grad_first = grad_mid + against(grad_query_raw, cross_qkv_b[0])
    grad_start, grad_gain_first, grad_shift_first = pull_first(grad_first)
    grad_branch = grad_start.astype(jnp.bfloat16)
    grad_self_out_w = inner_rows(context_self, grad_branch)
    grad_self_last = jnp.sum(grad_branch.astype(jnp.float32), 0)
    grad_context = (
        against(grad_branch, self_out_b).astype(jnp.bfloat16).reshape(1, tokens, head_count, HEAD)
    )
    query_parts = []
    grad_key_total = jnp.zeros((1, tokens, head_count, HEAD), jnp.float32)
    grad_value_total = jnp.zeros((1, tokens, head_count, HEAD), jnp.float32)
    for part_no in range(tokens // block_rows):
        low_row = part_no * block_rows
        high_row = low_row + block_rows
        grad_queries, grad_keys, grad_values = attend_back(
            heads_query[:, low_row:high_row],
            heads_key[:, :high_row],
            heads_value[:, :high_row],
            allowed[None, low_row:high_row, :high_row],
            self_sums[part_no],
            grad_context[:, low_row:high_row],
        )
        query_parts.append(grad_queries)
        padding = ((0, 0), (0, tokens - high_row), (0, 0), (0, 0))
        grad_key_total = grad_key_total + jnp.pad(grad_keys, padding)
        grad_value_total = grad_value_total + jnp.pad(grad_values, padding)
    grad_query_low = (
        jnp.concatenate(query_parts, 1).reshape(tokens, model_width).astype(jnp.bfloat16)
    )
    grad_query_raw = (grad_query_low.astype(jnp.float32) * query_scale).astype(jnp.bfloat16)
    grad_key_low = grad_key_total.reshape(tokens, model_width).astype(jnp.bfloat16)
    grad_value_low = grad_value_total.reshape(tokens, model_width).astype(jnp.bfloat16)
    grad_self_qkv_w = jnp.stack(
        [
            inner_rows(target, grad_query_raw),
            inner_rows(target, grad_key_low),
            inner_rows(target, grad_value_low),
        ]
    )
    grad_self_bias_w = jnp.stack(
        [
            jnp.sum(grad_query_raw.astype(jnp.float32), 0),
            jnp.sum(grad_value_low.astype(jnp.float32), 0),
            grad_self_last,
        ]
    )
    target_grad = (
        grad_start
        + against(grad_query_raw, self_qkv_b[0])
        + against(grad_key_low, self_qkv_b[1])
        + against(grad_value_low, self_qkv_b[2])
    )
    grad_gain_w = jnp.stack([grad_gain_first, grad_gain_mid, grad_gain_last])
    grad_shift_w = jnp.stack([grad_shift_first, grad_shift_mid, grad_shift_last])
    fsdp_count = lax.axis_size("fsdp")
    dp_count = lax.axis_size("dp")
    split_dims = (1, 0, 1, 1, 0, 1, 0, 0, 0, 0, 1, 1)
    gradients = (
        grad_self_qkv_w,
        grad_self_out_w,
        grad_self_bias_w,
        grad_cross_qkv_w,
        grad_cross_out_w,
        grad_cross_bias_w,
        grad_ffn_in_w,
        grad_ffn_in_bias_w,
        grad_ffn_out_w,
        grad_ffn_out_bias_w,
        grad_gain_w,
        grad_shift_w,
    )
    moved = [
        spread_rows(gradient, axis_dim, fsdp_count, dp_count)
        for gradient, axis_dim in zip(gradients, split_dims)
    ]
    pieces = (
        lax.psum_scatter(moved[0], ("dp", "fsdp"), scatter_dimension=1, tiled=True),
        lax.psum_scatter(moved[1], ("dp", "fsdp"), scatter_dimension=0, tiled=True),
        lax.psum_scatter(moved[2], ("dp", "fsdp"), scatter_dimension=1, tiled=True),
        lax.psum_scatter(moved[3], ("dp", "fsdp"), scatter_dimension=1, tiled=True),
        lax.psum_scatter(moved[4], ("dp", "fsdp"), scatter_dimension=0, tiled=True),
        lax.psum_scatter(moved[5], ("dp", "fsdp"), scatter_dimension=1, tiled=True),
        lax.psum_scatter(moved[6], ("dp", "fsdp"), scatter_dimension=0, tiled=True),
        lax.psum_scatter(moved[7], ("dp", "fsdp"), scatter_dimension=0, tiled=True),
        lax.psum_scatter(moved[8], ("dp", "fsdp"), scatter_dimension=0, tiled=True),
        lax.psum_scatter(moved[9], ("dp", "fsdp"), scatter_dimension=0, tiled=True),
        lax.psum_scatter(moved[10], ("dp", "fsdp"), scatter_dimension=1, tiled=True),
        lax.psum_scatter(moved[11], ("dp", "fsdp"), scatter_dimension=1, tiled=True),
    )
    summed = (
        lax.all_gather(pieces[0].astype(jnp.bfloat16), "dp", axis=1, tiled=True).astype(
            jnp.float32
        ),
        lax.all_gather(pieces[1].astype(jnp.bfloat16), "dp", axis=0, tiled=True).astype(
            jnp.float32
        ),
        lax.all_gather(pieces[2].astype(jnp.bfloat16), "dp", axis=1, tiled=True).astype(
            jnp.float32
        ),
        lax.all_gather(pieces[3].astype(jnp.bfloat16), "dp", axis=1, tiled=True).astype(
            jnp.float32
        ),
        lax.all_gather(pieces[4].astype(jnp.bfloat16), "dp", axis=0, tiled=True).astype(
            jnp.float32
        ),
        lax.all_gather(pieces[5].astype(jnp.bfloat16), "dp", axis=1, tiled=True).astype(
            jnp.float32
        ),
        lax.all_gather(pieces[6].astype(jnp.bfloat16), "dp", axis=0, tiled=True).astype(
            jnp.float32
        ),
        lax.all_gather(pieces[7].astype(jnp.bfloat16), "dp", axis=0, tiled=True).astype(
            jnp.float32
        ),
        lax.all_gather(pieces[8].astype(jnp.bfloat16), "dp", axis=0, tiled=True).astype(
            jnp.float32
        ),
        lax.all_gather(pieces[9].astype(jnp.bfloat16), "dp", axis=0, tiled=True).astype(
            jnp.float32
        ),
        lax.all_gather(pieces[10].astype(jnp.bfloat16), "dp", axis=1, tiled=True).astype(
            jnp.float32
        ),
        lax.all_gather(pieces[11].astype(jnp.bfloat16), "dp", axis=1, tiled=True).astype(
            jnp.float32
        ),
    )
    return (
        output,
        target_grad,
        memory_grad,
        summed[0],
        summed[1],
        summed[2],
        summed[3],
        summed[4],
        summed[5],
        summed[6],
        summed[7],
        summed[8],
        summed[9],
        summed[10],
        summed[11],
    )


def solution(mesh):
    placed = (
        P(("dp", "fsdp"), None),
        P(("dp", "fsdp"), None, None),
        P(("dp", "fsdp"), None),
        P(("dp", "fsdp")),
        P(("dp", "fsdp")),
        P(None, "fsdp", None),
        P("fsdp", None),
        P(None, "fsdp"),
        P(None, "fsdp", None),
        P("fsdp", None),
        P(None, "fsdp"),
        P("fsdp", None),
        P("fsdp"),
        P("fsdp", None),
        P("fsdp"),
        P(None, "fsdp"),
        P(None, "fsdp"),
    )
    return jax.shard_map(
        on_device,
        mesh=mesh,
        in_specs=placed,
        out_specs=(
            P(("dp", "fsdp"), None),
            P(("dp", "fsdp"), None),
            P(("dp", "fsdp"), None, None),
            P(None, "fsdp", None),
            P("fsdp", None),
            P(None, "fsdp"),
            P(None, "fsdp", None),
            P("fsdp", None),
            P(None, "fsdp"),
            P("fsdp", None),
            P("fsdp"),
            P("fsdp", None),
            P("fsdp"),
            P(None, "fsdp"),
            P(None, "fsdp"),
        ),
        check_vma=False,
    )
```

profile of v0, /device:TPU:9, one launch (start us, length us, event | category | flops | bytes accessed | tf_op | source)
XLA Modules:
  0.0 1364.5 jit_solution(16155922407876979513)
XLA Ops:
  15.4 16.2 %all-reduce.2 = bf16[768]{0:T(1024)(128)(2,1)S(1)} all-reduce(bf16[768]{0:T(1024)(128)(2,1)S(1)} %dynamic-update-slice), channel_id=1, replica_groups=mesh['dp'=4,'fsdp'=8] {'fsdp'}, use_global_device_ids=true, to_apply=%add.2 | all-reduce | flops 768 | bytes 3072
  45.7 16.0 %all-gather.3 = bf16[8,96,3]{1,2,0:T(4,128)(2,1)S(1)} all-gather(bf16[1,96,3]{1,2,0:T(4,128)(2,1)S(1)} %bitcast.445), channel_id=1, replica_groups=mesh['dp'=4,'fsdp'=8] {'fsdp'}, dimensions={0}, use_global_device_ids=true | all-gather | bytes 5184 | tf_op jit(solution)/shard_map/all_gather | solution.py:113
  62.5 12.7 all-gather.1
  75.9 14.9 %all-gather.2 = bf16[8,96,3]{1,2,0:T(4,128)(2,1)S(1)} all-gather(bf16[1,96,3]{1,2,0:T(4,128)(2,1)S(1)} %bitcast.447), channel_id=1, replica_groups=mesh['dp'=4,'fsdp'=8] {'fsdp'}, dimensions={0}, use_global_device_ids=true | all-gather | bytes 5184 | tf_op jit(solution)/shard_map/all_gather | solution.py:119
  91.5 22.8 %all-gather.4 = bf16[8,1,384]{2,1,0:T(2,128)(2,1)S(1)} all-gather(bf16[1,1,384]{2,1,0:T(2,128)(2,1)S(1)} %reshape.719), channel_id=1, replica_groups=mesh['dp'=4,'fsdp'=8] {'fsdp'}, dimensions={0}, use_global_device_ids=true | all-gather | bytes 6912 | tf_op jit(solution)/shard_map/all_gather | solution.py:115
  238.5 12.4 fusion.64
  266.5 14.0 %select_reduce_fusion.1 = (f32[2,12,256]{2,1,0:T(8,128)S(1)}, f32[2,12,256,1024]{3,2,1,0:T(8,128)}) fusion(pred[2,1024]{1,0:T(4,128)(4,1)S(1)} %get-tuple-element.160, bf16[2,1024,12,64]{1,3,2,0:T(8,128)(2,1)} %bitcast.376, bf16[2,256,12,64]{1,0,3,2:T(2,128)(2,1)} %slice.214), kind=kOutput, calls=%fused_computation.22 | convolution fusion | flops 817883136 | bytes 29124608 | tf_op jit(solution)/shard_map/bqhe,bkhe->bhqk/dot_general | solution.py:37
  350.7 38.2 %multiply_convert_fusion.4 = (bf16[1024,3072]{1,0:T(8,128)(2,1)}, f32[1024,3072]{1,0:T(8,128)}, f32[1024,3072]{1,0:T(8,128)}) fusion(f32[3072]{0:T(1024)S(1)} %bitcast.438, bf16[768,3072]{1,0:T(8,128)(2,1)} %all-gather.24.cloned.1.call-done, f32[1024,768]{0,1:T(8,128)} %copy-done.19, f32[768]{0:T(1024)S(1)} %copy-done.105, f32[768]{0:T(1024)S(1)} %copy-done.93, ...), kind=kOutput, calls=%fused_computation.43 | convolution fusion | flops 5043388416 | bytes 39348224 | tf_op jit(solution)/shard_map/dot_general | solution.py:230
  405.9 18.1 %convert_reduce_fusion = (f32[3072]{0:T(1024)}, bf16[1024,3072]{1,0:T(8,128)(2,1)}) fusion(f32[1024,3072]{1,0:T(8,128)} %get-tuple-element.137, bf16[1024,768]{0,1:T(8,128)(2,1)S(1)} %get-tuple-element.123, bf16[3072,768]{1,0:T(8,128)(2,1)} %all-gather.26.cloned.1.call-done, f32[1024,3072]{1,0:T(8,128)} %get-tuple-element.179, f32[3072]{0:T(1024)S(1)} %bitcast.439), kind=kOutput, calls=%fused_computation.32 | convolution fusion | flops 4885312512 | bytes 37773312 | tf_op jit(solution)/shard_map/dot_general | solution.py:31
  446.0 13.6 fusion.44
  459.5 16.8 %multiply_reduce_fusion.2 = (f32[2,12,256]{2,1,0:T(8,128)S(1)}, f32[2,12,256,1024]{3,2,1,0:T(8,128)}) fusion(f32[2,12,256,1024]{3,2,1,0:T(8,128)} %get-tuple-element.174, f32[2,12,256]{2,1,0:T(8,128)S(1)} %copy-done.64, pred[2,1024]{1,0:T(4,128)(4,1)S(1)} %copy-done.69, bf16[2,1024,12,64]{1,3,2,0:T(8,128)(2,1)S(1)} %bitcast.385, ...), kind=kOutput, calls=%fused_computation.10 | convolution fusion | flops 830466048 | bytes 54315008 | tf_op jit(solution)/shard_map/bqhe,bkhe->bhqk/dot_general | solution.py:55
  476.4 22.0 %multiply_convert_fusion.2 = bf16[2,12,256,1024]{3,2,1,0:T(8,128)(2,1)} fusion(f32[2,12,256,1024]{3,2,1,0:T(8,128)} %get-tuple-element.186, f32[2,12,256,1024]{3,2,1,0:T(8,128)} %get-tuple-element.174, f32[2,12,256]{2,1,0:T(8,128)S(1)} %get-tuple-element.185, f32[2,12,256]{2,1,0:T(8,128)S(1)} %copy-done.64, pred[2,1024]{1,0:T(4,128)(4,1)S(1)} %copy-done.69), kind=kLoop, calls=%fused_computation.9 | loop fusion | flops 31457280 | bytes 62965760 | tf_op jit(solution)/shard_map/convert_element_type | solution.py:59
  519.0 13.5 fusion.47
  532.5 16.8 %multiply_reduce_fusion.1 = (f32[2,12,256]{2,1,0:T(8,128)S(1)}, f32[2,12,256,1024]{3,2,1,0:T(8,128)}) fusion(f32[2,12,256,1024]{3,2,1,0:T(8,128)} %get-tuple-element.176, f32[2,12,256]{2,1,0:T(8,128)S(1)} %copy-done.63, pred[2,1024]{1,0:T(4,128)(4,1)S(1)} %copy-done.67, bf16[2,1024,12,64]{1,3,2,0:T(8,128)(2,1)S(1)} %bitcast.383, ...), kind=kOutput, calls=%fused_computation.7 | convolution fusion | flops 830466048 | bytes 54315008 | tf_op jit(solution)/shard_map/bqhe,bkhe->bhqk/dot_general | solution.py:55
  549.2 21.8 %multiply_convert_fusion.1 = bf16[2,12,256,1024]{3,2,1,0:T(8,128)(2,1)} fusion(f32[2,12,256,1024]{3,2,1,0:T(8,128)} %get-tuple-element.184, f32[2,12,256,1024]{3,2,1,0:T(8,128)} %get-tuple-element.176, f32[2,12,256]{2,1,0:T(8,128)S(1)} %get-tuple-element.183, f32[2,12,256]{2,1,0:T(8,128)S(1)} %copy-done.63, pred[2,1024]{1,0:T(4,128)(4,1)S(1)} %copy-done.67), kind=kLoop, calls=%fused_computation.6 | loop fusion | flops 31457280 | bytes 62965760 | tf_op jit(solution)/shard_map/convert_element_type | solution.py:59
  674.3 14.2 %fusion.136 = f32[768,768,1]{0,1,2:T(8,128)} fusion(bf16[4,1024,768]{2,1,0:T(8,128)(2,1)} %param.20, f32[1024,768]{1,0:T(8,128)} %copy.301, f32[1024,768]{1,0:T(8,128)} %copy.300, f32[1024,768]{1,0:T(8,128)} %copy.298, f32[1024,768]{1,0:T(8,128)S(1)} %copy-done.47, pred[4]{0:T(512)(128)(4,1)S(1)} %copy-done.112, pred[4]{0:T(512)(128)(4,1)S(1)} %copy-done.114, ...), kind=kOutput, calls=%fused_computation.295 | convolution fusion | flops 4857004032 | bytes 21233680 | tf_op jit(solution)/shard_map/rmd,rme->de/dot_general | solution.py:305
  709.0 17.6 %multiply_reduce_fusion = (f32[12,512]{1,0:T(8,128)S(1)}, f32[12,512,1024]{2,1,0:T(8,128)}) fusion(f32[12,512,1024]{2,1,0:T(8,128)} %get-tuple-element.168, f32[12,512]{1,0:T(8,128)S(1)} %copy-done.70, pred[512,1024]{1,0:T(8,128)(4,1)S(1)} %copy-done.14, bf16[1024,12,64]{0,2,1:T(8,128)(2,1)} %bitcast.404, bf16[1,1024,12,64]{1,3,2,0:T(8,128)(2,1)} %bitcast.410), kind=kOutput, calls=%fused_computation.4 | convolution fusion | flops 830466048 | bytes 53264384 | tf_op jit(solution)/shard_map/bqhe,bkhe->bhqk/dot_general | solution.py:55
  726.8 13.7 %multiply_convert_fusion.3 = bf16[12,512,512]{1,2,0:T(8,128)(2,1)} fusion(f32[12,512,512]{1,2,0:T(8,128)} %get-tuple-element.189, f32[12,512,512]{1,2,0:T(8,128)} %copy-done.2, f32[12,512]{1,0:T(8,128)S(1)} %get-tuple-element.188, f32[12,512]{1,0:T(8,128)S(1)} %copy-done.62, pred[512,512]{0,1:T(8,128)(4,1)S(1)} %copy-done.32), kind=kLoop, calls=%fused_computation.37 | loop fusion | flops 15728640 | bytes 31768576 | tf_op jit(solution)/shard_map/convert_element_type | solution.py:59
  748.0 15.6 %multiply_convert_fusion = bf16[12,512,1024]{2,1,0:T(8,128)(2,1)} fusion(f32[12,512,1024]{2,1,0:T(8,128)} %get-tuple-element.191, f32[12,512,1024]{2,1,0:T(8,128)S(1)} %bitcast.365, f32[12,512]{1,0:T(8,128)S(1)} %get-tuple-element.190, f32[12,512]{1,0:T(8,128)S(1)} %copy-done.70, pred[512,1024]{1,0:T(8,128)(4,1)S(1)} %copy-done.14), kind=kLoop, calls=%fused_computation.3 | loop fusion | flops 31457280 | bytes 63488000 | tf_op jit(solution)/shard_map/convert_element_type | solution.py:59
  842.7 63.6 %all-reduce.11 = (bf16[3,768]{1,0:T(4,128)(2,1)S(1)}, bf16[3,768]{1,0:T(4,128)(2,1)S(1)}, bf16[3072]{0:T(1024)(128)(2,1)S(1)}, bf16[768]{0:T(1024)(128)(2,1)S(1)...) all-reduce(f32[3,768]{1,0:T(4,128)S(1)} %reshape.648, ...), channel_id=4, replica_groups=mesh['dp'=4,'fsdp'=8] {'dp','fsdp'}, use_global_device_ids=true, to_apply=%region_29.31.clone | all-reduce | flops 13056 | bytes 78336
  948.3 13.4 fusion.72
  995.5 68.1 %reduce-scatter.11.cloned.1.call-done = f32[3,24,768]{2,1,0:T(8,128)} async-done(((f32[3,768,768]{2,1,0:T(8,128)}), f32[3,24,768]{2,1,0:T(8,128)}) %reduce-scatter.11.cloned.1.call-update) | async-done | bytes 221200 | tf_op jit(solution)/shard_map/reduce_scatter | solution.py:397
  1074.6 129.6 %reduce-scatter.19.cloned.1.call-done = f32[24,3072]{1,0:T(8,128)} async-done(((f32[768,3072]{1,0:T(8,128)}), f32[24,3072]{1,0:T(8,128)}) %reduce-scatter.19.cloned.1.call-update) | async-done | bytes 294928 | tf_op jit(solution)/shard_map/reduce_scatter | solution.py:403
  1215.6 130.1 %reduce-scatter.21.cloned.1.call-done = f32[96,768]{1,0:T(8,128)} async-done(((f32[3072,768]{1,0:T(8,128)}), f32[96,768]{1,0:T(8,128)}) %reduce-scatter.21.cloned.1.call-update) | async-done | bytes 294928 | tf_op jit(solution)/shard_map/reduce_scatter | solution.py:405
  (545 shorter events, 609.7 us)
Async XLA Ops:
  7.3 117.7 %all-gather.20.cloned.1.call-start = ((), (), s32[]{:S(2)}) async-start(), calls=%async_computation.8 | async-start | bytes 3981312 | tf_op jit(solution)/shard_map/all_gather | solution.py:111
  8.0 187.4 %all-gather.16.cloned.1.call-start = ((), (), s32[]{:S(2)}) async-start(), calls=%async_computation.6 | async-start | bytes 3981312 | tf_op jit(solution)/shard_map/all_gather | solution.py:108
  8.8 242.2 %all-gather.18.cloned.1.call-start = ((), (), s32[]{:S(2)}) async-start(), calls=%async_computation.7 | async-start | bytes 1327104 | tf_op jit(solution)/shard_map/all_gather | solution.py:109
  9.5 335.1 %all-gather.22.cloned.1.call-start = ((), (), s32[]{:S(2)}) async-start(), calls=%async_computation.9 | async-start | bytes 1327104 | tf_op jit(solution)/shard_map/all_gather | solution.py:112
  10.1 340.6 %all-gather.24.cloned.1.call-start = ((), (), s32[]{:S(2)}) async-start(), calls=%async_computation.10 | async-start | bytes 5308416 | tf_op jit(solution)/shard_map/all_gather | solution.py:114
  10.7 378.3 %all-gather.26.cloned.1.call-start = ((), (), s32[]{:S(2)}) async-start(), calls=%async_computation.11 | async-start | bytes 5308416 | tf_op jit(solution)/shard_map/all_gather | solution.py:116
  11.2 961.3 %reduce-scatter.17.cloned.1.call-start = ((), (), s32[]{:S(2)}) async-start(), calls=%async_computation.15 | async-start | bytes 2433024 | tf_op jit(solution)/shard_map/reduce_scatter | solution.py:401
  13.8 197.6 %copy-start.31 = (pred[512,512]{0,1:T(8,128)(4,1)}, pred[512,512]{0,1:T(8,128)(4,1)S(1)}, u32[]{:S(2)}) copy-start(pred[512,512]{0,1:T(8,128)(4,1)S(1)} %slice.257) | copy-start | bytes 786436
  33.5 258.9 %copy-start.68 = (pred[2,1024]{1,0:T(4,128)(4,1)}, pred[2,1024]{1,0:T(4,128)(4,1)S(1)}, u32[]{:S(2)}) copy-start(pred[2,1024]{1,0:T(4,128)(4,1)S(1)} %get-tuple-element.160) | copy-start | bytes 6148
  75.9 268.7 %copy-start.80 = (f32[768]{0:T(1024)}, f32[768]{0:T(1024)S(1)}, u32[]{:S(2)}) copy-start(f32[768]{0:T(1024)S(1)} %get-tuple-element.104) | copy-start | bytes 9220
  115.9 122.6 %copy-start.13 = (pred[512,1024]{1,0:T(8,128)(4,1)}, pred[512,1024]{1,0:T(8,128)(4,1)S(1)}, u32[]{:S(2)}) copy-start(pred[512,1024]{1,0:T(8,128)(4,1)S(1)} %copy.268) | copy-start | bytes 1572868
  254.9 89.8 %copy-start.3 = (f32[1024,768]{0,1:T(8,128)}, f32[1024,768]{0,1:T(8,128)S(1)}, u32[]{:S(2)}) copy-start(f32[1024,768]{0,1:T(8,128)S(1)} %get-tuple-element.172) | copy-start | bytes 9437188
  254.9 89.7 %copy-start.71 = (f32[1024]{0:T(1024)}, f32[1024]{0:T(1024)S(1)}, u32[]{:S(2)}) copy-start(f32[1024]{0:T(1024)S(1)} %broadcast_multiply_fusion.2) | copy-start | bytes 12292
  255.3 89.3 %copy-start.78 = (f32[1024]{0:T(1024)}, f32[1024]{0:T(1024)S(1)}, u32[]{:S(2)}) copy-start(f32[1024]{0:T(1024)S(1)} %fusion.99) | copy-start | bytes 12292
  348.6 87.0 %copy-start.74 = (f32[1024]{0:T(1024)}, f32[1024]{0:T(1024)S(1)}, u32[]{:S(2)}) copy-start(f32[1024]{0:T(1024)S(1)} %broadcast_multiply_fusion.1) | copy-start | bytes 12292
  350.6 85.0 %copy-start.89 = (f32[1024]{0:T(1024)}, f32[1024]{0:T(1024)S(1)}, u32[]{:S(2)}) copy-start(f32[1024]{0:T(1024)S(1)} %fusion.100) | copy-start | bytes 12292
  592.0 387.6 %reduce-scatter.13.cloned.1.call-start = ((), (), s32[]{:S(2)}) async-start(), calls=%async_computation.13 | async-start | bytes 2433024 | tf_op jit(solution)/shard_map/reduce_scatter | solution.py:398
  695.7 291.0 %reduce-scatter.15.cloned.1.call-start = ((), (), s32[]{:S(2)}) async-start(), calls=%async_computation.14 | async-start | bytes 7299072 | tf_op jit(solution)/shard_map/reduce_scatter | solution.py:400
  726.7 336.9 %reduce-scatter.11.cloned.1.call-start = ((), (), s32[]{:S(2)}) async-start(), calls=%async_computation.12 | async-start | bytes 7299072 | tf_op jit(solution)/shard_map/reduce_scatter | solution.py:397
  809.2 395.0 %reduce-scatter.19.cloned.1.call-start = ((), (), s32[]{:S(2)}) async-start(), calls=%async_computation.16 | async-start | bytes 9732096 | tf_op jit(solution)/shard_map/reduce_scatter | solution.py:403
  822.9 522.8 %reduce-scatter.21.cloned.1.call-start = ((), (), s32[]{:S(2)}) async-start(), calls=%async_computation.17 | async-start | bytes 9732096 | tf_op jit(solution)/shard_map/reduce_scatter | solution.py:405
  836.6 102.3 %copy-start.46 = (bf16[1,512,12,64]{1,3,2,0:T(8,128)(2,1)S(1)}, bf16[1,512,12,64]{1,3,2,0:T(8,128)(2,1)}, u32[]{:S(2)}) copy-start(bf16[1,512,12,64]{1,3,2,0:T(8,128)(2,1)} %copy-done.45) | copy-start | bytes 2359300
  836.7 102.3 %copy-start.50 = (bf16[1,512,12,64]{1,3,2,0:T(8,128)(2,1)S(1)}, bf16[1,512,12,64]{1,3,2,0:T(8,128)(2,1)}, u32[]{:S(2)}) copy-start(bf16[1,512,12,64]{1,3,2,0:T(8,128)(2,1)} %copy-done.49) | copy-start | bytes 2359300
  1073.6 283.9 %copy-start.1 = (s32[4]{0:T(128)S(1)}, s32[4]{0:T(128)}, u32[]{:S(2)}) copy-start(s32[4]{0:T(128)} %param.23) | copy-start | bytes 52
  (126 other events, 969.5 us)
Sparse Core Ops, SparseCore 0:
  10.3 65.2 all-gather.19
  77.8 63.8 all-gather.15
  143.9 39.6 all-gather.17
  185.6 39.8 all-gather.21
  227.5 78.0 all-gather.23
  307.7 78.0 all-gather.25
  592.1 117.7 reduce-scatter.16
  716.1 98.1 reduce-scatter.12
  819.9 118.7 reduce-scatter.14
  945.1 118.4 reduce-scatter.10
  1069.5 134.6 reduce-scatter.18
  1211.0 134.6 reduce-scatter.20
where the time goes:
time: 1370 us; the launch traced here: 1360 us
  matrix products  446 us (33%)
  waiting for transfers between devices  332 us (24%)
  blocking collectives  232 us (17%)
  local copies, waits for them, and re-layouts  168 us (12%)
  other arithmetic  168 us (12%)
  between operations  19 us (1%)
    reduce_scatter x1, waiting for transfers between devices, on_device(): lax.psum_scatter(moved[8], ('dp', 'fsdp'), scatter_dimension=0, tiled=True)  130 us
    reduce_scatter x1, waiting for transfers between devices, on_device(): lax.psum_scatter(moved[6], ('dp', 'fsdp'), scatter_dimension=0, tiled=True)  130 us
    unnamed x3, blocking collectives  86.7 us
    convert_element_type x4, other arithmetic, attend_back(): grad_scores = (shares * (grad_shares - inner_sum)).astype(jnp.bfloat16)  73.2 us
    reduce_scatter x1, waiting for transfers between devices, on_device(): lax.psum_scatter(moved[0], ('dp', 'fsdp'), scatter_dimension=1, tiled=True)  68.1 us
    dot_general x4, matrix products, attend_back(): jnp.einsum('bqhe,bkhe->bhqk', grad_context, values, preferred_element_typ...  60.6 us
    dot_general x4, matrix products, attend_back(): jnp.einsum('bhqk,bqhe->bkhe', shares_low, grad_context, preferred_element...  45.3 us
    dot_general x8, matrix products, against(): lax.dot_general(left, right, (((1,), (1,)), ((), ())), preferred_element_...  43.8 us
  transfers between devices with their start and end apart: 12, of which 3 were waited for; matrix products, arithmetic and copies ran while one was open for 41% of the time, Pallas kernels for 0%

commit v1 on v0

v1 whole, which is shorter than its diff:
```python
import functools
import math
import jax
import jax.numpy as jnp
from jax import lax
from jax.sharding import PartitionSpec as P
from jax.experimental import pallas as pl
from jax.experimental.pallas import tpu as pltpu

HEAD = 64
PAIR = 2 * HEAD
BLOCK = 256
very_low = -1e30
VMEM_LIMIT = 60 * 2**20
f32 = jnp.float32
bf16 = jnp.bfloat16


def dot_nt(left, right):
    return lax.dot_general(left, right, (((1,), (1,)), ((), ())), preferred_element_type=f32)


def dot_nn(left, right):
    return lax.dot_general(left, right, (((1,), (0,)), ((), ())), preferred_element_type=f32)


def dot_tn(left, right):
    return lax.dot_general(left, right, (((0,), (0,)), ((), ())), preferred_element_type=f32)


def split_pair(pair):
    lane = lax.broadcasted_iota(jnp.int32, pair.shape, 1)
    none = jnp.zeros_like(pair)
    return (jnp.where(lane < HEAD, pair, none), jnp.where(lane < HEAD, none, pair))


def mask_tail(scores, valid):
    width = scores.shape[0]
    if width == BLOCK:
        return jnp.where(valid, scores, very_low)
    return jnp.concatenate(
        [scores[: width - BLOCK], jnp.where(valid, scores[width - BLOCK :], very_low)], 0
    )


def attend_tile(queries, keys, values_t, valid):
    parts = []
    stats = []
    for half, query in enumerate(split_pair(queries)):
        scores = mask_tail(dot_nt(keys, query), valid)
        highest = jnp.max(scores, 0, keepdims=True)
        raised = jnp.exp(scores - highest)
        summed = jnp.sum(raised, 0, keepdims=True)
        context = dot_nn(values_t[half * HEAD : (half + 1) * HEAD], raised.astype(bf16))
        parts.append(context * (1.0 / summed))
        stats.append(highest + jnp.log(summed))
    return jnp.concatenate(parts, 0).T, jnp.concatenate(stats, 0)


def attend_back_tile(queries, keys, values, keys_t, grads, logsum, valid):
    shares_all = []
    grads_all = []
    query_parts = []
    query_halves = split_pair(queries)
    grad_halves = split_pair(grads)
    for half in range(2):
        scores = mask_tail(dot_nt(keys, query_halves[half]), valid)
        shares = jnp.exp(scores - logsum[half : half + 1])
        grad_shares = dot_nt(values, grad_halves[half])
        inner = jnp.sum(shares * grad_shares, 0, keepdims=True)
        grad_scores = (shares * (grad_shares - inner)).astype(bf16)
        query_parts.append(dot_nn(keys_t[half * HEAD : (half + 1) * HEAD], grad_scores))
        shares_all.append(shares.astype(bf16))
        grads_all.append(grad_scores)
    grad_values = dot_nn(jnp.concatenate(shares_all, 1), jnp.concatenate(grad_halves, 0))
    grad_keys = dot_nn(jnp.concatenate(grads_all, 1), jnp.concatenate(query_halves, 0))
    return jnp.concatenate(query_parts, 0).T, grad_keys, grad_values


def causal():
    key = lax.broadcasted_iota(jnp.int32, (BLOCK, BLOCK), 0)
    query = lax.broadcasted_iota(jnp.int32, (BLOCK, BLOCK), 1)
    return key <= query


def self_kernel(info, q_ref, k_ref, v_ref, o_ref, stat_ref):
    tokens = q_ref.shape[0]
    valid = causal()
    values_t = v_ref[...].T

    def run(whole):
        for part in range(tokens // BLOCK):
            rows = pl.ds(part * BLOCK, BLOCK)
            low = 0 if whole else part * BLOCK
            high = (part + 1) * BLOCK
            context, stats = attend_tile(
                q_ref[rows, :], k_ref[low:high, :], values_t[:, low:high], valid
            )
            o_ref[rows, :] = context.astype(bf16)
            stat_ref[0, :, rows] = stats

    pl.when(info[0] == 1)(functools.partial(run, False))
    pl.when(info[0] != 1)(functools.partial(run, True))


def self_back_kernel(
    info, q_ref, k_ref, v_ref, g_ref, stat_ref, dq_ref, dk_ref, dv_ref, key_sum, value_sum
):
    tokens = q_ref.shape[0]
    valid = causal()
    keys_t = k_ref[...].T

    def run(whole):
        for part in reversed(range(tokens // BLOCK)):
            rows = pl.ds(part * BLOCK, BLOCK)
            low = 0 if whole else part * BLOCK
            high = (part + 1) * BLOCK
            grad_queries, grad_keys, grad_values = attend_back_tile(
                q_ref[rows, :],
                k_ref[low:high, :],
                v_ref[low:high, :],
                keys_t[:, low:high],
                g_ref[rows, :],
                stat_ref[0, :, rows],
                valid,
            )
            dq_ref[rows, :] = (grad_queries.astype(bf16).astype(f32) * HEAD**-0.5).astype(bf16)
            if not whole:
                dk_ref[rows, :] = grad_keys.astype(bf16)
                dv_ref[rows, :] = grad_values.astype(bf16)
            elif high == tokens:
                key_sum[...] = grad_keys
                value_sum[...] = grad_values
            else:
                key_sum[:high, :] += grad_keys
                value_sum[:high, :] += grad_values
        if whole:
            dk_ref[...] = key_sum[...].astype(bf16)
            dv_ref[...] = value_sum[...].astype(bf16)

    pl.when(info[0] == 1)(functools.partial(run, False))
    pl.when(info[0] != 1)(functools.partial(run, True))


def cross_kernel(info, q_ref, k_ref, v_ref, o_ref, stat_ref):
    row = jnp.where(info[0] == 1, pl.program_id(1), 0)
    length = info[1 + row]
    mem_len = k_ref.shape[1]
    key = lax.broadcasted_iota(jnp.int32, (BLOCK, BLOCK), 0)

    def run(width):
        valid = key < length - (width - BLOCK)
        context, stats = attend_tile(
            q_ref[...], k_ref[0, :width, :], v_ref[0, :width, :].T, valid
        )
        o_ref[...] = context.astype(bf16)
        stat_ref[0] = stats

    for width in range(BLOCK, mem_len + 1, BLOCK):
        pl.when((length > width - BLOCK) & (length <= width))(functools.partial(run, width))


def cross_back_kernel(
    info, q_ref, k_ref, v_ref, g_ref, stat_ref, dq_ref, dk_ref, dv_ref, key_sum, value_sum
):
    part = pl.program_id(1)
    short = info[0] == 1
    row = jnp.where(short, part, 0)
    length = info[1 + row]
    mem_len = k_ref.shape[1]
    key = lax.broadcasted_iota(jnp.int32, (BLOCK, BLOCK), 0)

    def run(width):
        valid = key < length - (width - BLOCK)
        grad_queries, grad_keys, grad_values = attend_back_tile(
            q_ref[...],
            k_ref[0, :width, :],
            v_ref[0, :width, :],
            k_ref[0, :width, :].T,
            g_ref[...],
            stat_ref[0],
            valid,
        )
        dq_ref[...] = (grad_queries.astype(bf16).astype(f32) * HEAD**-0.5).astype(bf16)
        if width < mem_len:
            rest = jnp.zeros((mem_len - width, PAIR), bf16)
            dk_ref[0, width:, :] = rest
            dv_ref[0, width:, :] = rest

        @pl.when(short)
        def _():
            dk_ref[0, :width, :] = grad_keys.astype(bf16)
            dv_ref[0, :width, :] = grad_values.astype(bf16)

        @pl.when(jnp.logical_not(short))
        def _():
            @pl.when(part == 0)
            def _():
                key_sum[:width, :] = grad_keys
                value_sum[:width, :] = grad_values

            @pl.when(part != 0)
            def _():
                key_sum[:width, :] += grad_keys
                value_sum[:width, :] += grad_values

            @pl.when(part == pl.num_programs(1) - 1)
            def _():
                dk_ref[0, :width, :] = key_sum[:width, :].astype(bf16)
                dv_ref[0, :width, :] = value_sum[:width, :].astype(bf16)

    for width in range(BLOCK, mem_len + 1, BLOCK):
        pl.when((length > width - BLOCK) & (length <= width))(functools.partial(run, width))


def params():
    return pltpu.CompilerParams(vmem_limit_bytes=VMEM_LIMIT)


def cost(matmuls, moved=2**23):
    flops = 2 * sum(math.prod(sizes) for sizes in matmuls)
    return pl.CostEstimate(flops=flops, bytes_accessed=moved, transcendentals=0)


def self_attend(info, queries, keys, values):
    tokens, width = queries.shape
    pairs = width // PAIR
    whole = pl.BlockSpec((tokens, PAIR), lambda pair, info: (0, pair))
    return pl.pallas_call(
        self_kernel,
        grid_spec=pltpu.PrefetchScalarGridSpec(
            num_scalar_prefetch=1,
            grid=(pairs,),
            in_specs=[whole] * 3,
            out_specs=[whole, pl.BlockSpec((1, 2, tokens), lambda pair, info: (pair, 0, 0))],
        ),
        out_shape=[
            jax.ShapeDtypeStruct((tokens, width), bf16),
            jax.ShapeDtypeStruct((pairs, 2, tokens), f32),
        ],
        compiler_params=params(),
        name="self_attend",
        cost_estimate=cost([(tokens, tokens, width)] * 8),
    )(info, queries, keys, values)


def self_attend_back(info, queries, keys, values, grads, stats):
    tokens, width = queries.shape
    pairs = width // PAIR
    whole = pl.BlockSpec((tokens, PAIR), lambda pair, info: (0, pair))
    return pl.pallas_call(
        self_back_kernel,
        grid_spec=pltpu.PrefetchScalarGridSpec(
            num_scalar_prefetch=1,
            grid=(pairs,),
            in_specs=[whole] * 4
            + [pl.BlockSpec((1, 2, tokens), lambda pair, info: (pair, 0, 0))],
            out_specs=[whole] * 3,
            scratch_shapes=[pltpu.VMEM((tokens, PAIR), f32)] * 2,
        ),
        out_shape=[jax.ShapeDtypeStruct((tokens, width), bf16)] * 3,
        compiler_params=params(),
        name="self_attend_back",
        cost_estimate=cost([(tokens, tokens, width)] * 12),
    )(info, queries, keys, values, grads, stats)


def row_of(info, part):
    return jnp.where(info[0] == 1, part, 0)


def cross_attend(info, queries, keys, values):
    tokens, width = queries.shape
    rows, mem_len, _ = keys.shape
    pairs = width // PAIR
    tile = pl.BlockSpec((BLOCK, PAIR), lambda pair, part, info: (part, pair))
    memory = pl.BlockSpec((1, mem_len, PAIR), lambda pair, part, info: (row_of(info, part), 0, pair))
    return pl.pallas_call(
        cross_kernel,
        grid_spec=pltpu.PrefetchScalarGridSpec(
            num_scalar_prefetch=1,
            grid=(pairs, tokens // BLOCK),
            in_specs=[tile, memory, memory],
            out_specs=[
                tile,
                pl.BlockSpec((1, 2, BLOCK), lambda pair, part, info: (pair, 0, part)),
            ],
        ),
        out_shape=[
            jax.ShapeDtypeStruct((tokens, width), bf16),
            jax.ShapeDtypeStruct((pairs, 2, tokens), f32),
        ],
        compiler_params=params(),
        name="cross_attend",
        cost_estimate=cost([(tokens, mem_len, width)] * 16),
    )(info, queries, keys, values)


def cross_attend_back(info, queries, keys, values, grads, stats):
    tokens, width = queries.shape
    rows, mem_len, _ = keys.shape
    pairs = width // PAIR
    tile = pl.BlockSpec((BLOCK, PAIR), lambda pair, part, info: (part, pair))
    memory = pl.BlockSpec((1, mem_len, PAIR), lambda pair, part, info: (row_of(info, part), 0, pair))
    return pl.pallas_call(
        cross_back_kernel,
        grid_spec=pltpu.PrefetchScalarGridSpec(
            num_scalar_prefetch=1,
            grid=(pairs, tokens // BLOCK),
            in_specs=[
                tile,
                memory,
                memory,
                tile,
                pl.BlockSpec((1, 2, BLOCK), lambda pair, part, info: (pair, 0, part)),
            ],
            out_specs=[tile, memory, memory],
            scratch_shapes=[pltpu.VMEM((mem_len, PAIR), f32)] * 2,
        ),
        out_shape=[jax.ShapeDtypeStruct((tokens, width), bf16)]
        + [jax.ShapeDtypeStruct(keys.shape, bf16)] * 2,
        compiler_params=params(),
        name="cross_attend_back",
        cost_estimate=cost([(tokens, mem_len, width)] * 24),
    )(info, queries, keys, values, grads, stats)


epsilon = 1e-05


def normalise(total):
    middle = jnp.mean(total, -1, keepdims=True)
    centred = total - middle
    variance = jnp.mean(centred * centred, -1, keepdims=True)
    scale = lax.rsqrt(variance + epsilon)
    return centred * scale, scale


def normalise_back(grad, gain, normal, scale):
    scaled = grad * gain
    first = jnp.mean(scaled, -1, keepdims=True)
    second = jnp.mean(scaled * normal, -1, keepdims=True)
    return (scaled - first - normal * second) * scale


def add_rows(ref, row, value):
    ref[row : row + 1, :] += jnp.sum(value, 0, keepdims=True)


def start_sums(*refs):
    @pl.when(pl.program_id(0) == 0)
    def _():
        for ref in refs:
            ref[...] = jnp.zeros_like(ref)


def full(array):
    return pl.BlockSpec(memory_space=pltpu.VMEM)


def row_block(rows, width):
    return pl.BlockSpec((rows, width), lambda part: (part, 0))


def keep_block(rows, width):
    return pl.BlockSpec((rows, width), lambda part: (0, 0))


def first_kernel(x_ref, c_ref, out_w, query_w, vec_ref, z_ref, low_ref, q_ref):
    branch = dot_nn(c_ref[...], out_w[...]) + vec_ref[0:1, :]
    total = x_ref[...].astype(f32) + branch
    normal, _ = normalise(total)
    first_low = (normal * vec_ref[2:3, :] + vec_ref[3:4, :]).astype(bf16)
    z_ref[...] = total
    low_ref[...] = first_low
    q_ref[...] = ((dot_nn(first_low, query_w[...]) + vec_ref[1:2, :]) * HEAD**-0.5).astype(bf16)


def first_norm(x, context, out_w, query_w, vectors, rows=256):
    tokens, width = x.shape
    block = row_block(rows, width)
    return pl.pallas_call(
        first_kernel,
        grid=(tokens // rows,),
        in_specs=[block, block, full(out_w), full(query_w), full(vectors)],
        out_specs=[block] * 3,
        out_shape=[
            jax.ShapeDtypeStruct((tokens, width), f32),
            jax.ShapeDtypeStruct((tokens, width), bf16),
            jax.ShapeDtypeStruct((tokens, width), bf16),
        ],
        compiler_params=params(),
        name="first_norm",
        cost_estimate=cost([(tokens, width, width)] * 4),
    )(x, context, out_w, query_w, vectors)


def ffn_kernel(
    z_ref,
    c_ref,
    cot_ref,
    out_w,
    in_w,
    ffn_w,
    vec_ref,
    bias_ref,
    out_ref,
    low_ref,
    act_ref,
    du_ref,
    df_ref,
    do_ref,
    dz_ref,
    dc_ref,
    sum_ref,
    wide_ref,
    slope_ref,
):
    start_sums(sum_ref, wide_ref)
    width = z_ref.shape[1]
    gain_first, shift_first = vec_ref[2:3, :], vec_ref[3:4, :]
    gain_mid, shift_mid = vec_ref[4:5, :], vec_ref[5:6, :]
    gain_last, shift_last = vec_ref[6:7, :], vec_ref[7:8, :]
    normal_first, _ = normalise(z_ref[...])
    first = normal_first * gain_first + shift_first
    normal_mid, scale_mid = normalise(first + dot_nn(c_ref[...], out_w[...]) + vec_ref[0:1, :])
    second = normal_mid * gain_mid + shift_mid
    second_low = second.astype(bf16)
    low_ref[...] = second_low
    total = second + vec_ref[1:2, :]
    for block in range(in_w.shape[0]):
        cols = pl.ds(block * width, width)
        value = dot_nn(second_low, in_w[block]) + bias_ref[:, cols]
        share = 0.5 * (1.0 + lax.erf(value * 0.5**0.5))
        density = jnp.exp(-0.5 * value * value) * 0.3989422804014327
        active = (value * share).astype(bf16)
        slope_ref[:, cols] = share + value * density
        act_ref[:, cols] = active
        total = total + dot_nn(active, ffn_w[block])
    normal_last, scale_last = normalise(total)
    out_ref[...] = (normal_last * gain_last + shift_last).astype(bf16)
    cot = cot_ref[...].astype(f32)
    add_rows(sum_ref, 0, cot * normal_last)
    add_rows(sum_ref, 1, cot)
    grad_last = normalise_back(cot, gain_last, normal_last, scale_last)
    grad_low = grad_last.astype(bf16)
    df_ref[...] = grad_low
    add_rows(sum_ref, 2, grad_low.astype(f32))
    grad_second = grad_last
    for block in range(in_w.shape[0]):
        cols = pl.ds(block * width, width)
        grad_hidden = (dot_nt(grad_low, ffn_w[block]) * slope_ref[:, cols]).astype(bf16)
        du_ref[:, cols] = grad_hidden
        wide_ref[:, cols] += jnp.sum(grad_hidden.astype(f32), 0, keepdims=True)
        grad_second = grad_second + dot_nt(grad_hidden, in_w[block])
    add_rows(sum_ref, 3, grad_second * normal_mid)
    add_rows(sum_ref, 4, grad_second)
    grad_mid = normalise_back(grad_second, gain_mid, normal_mid, scale_mid)
    dz_ref[...] = grad_mid
    grad_low = grad_mid.astype(bf16)
    do_ref[...] = grad_low
    add_rows(sum_ref, 5, grad_low.astype(f32))
    dc_ref[...] = dot_nt(grad_low, out_w[...]).astype(bf16)


def ffn_block(z, context, cotangent, out_w, in_w, ffn_w, vectors, bias, rows=256):
    tokens, width = z.shape
    hidden = in_w.shape[0] * width
    block = row_block(rows, width)
    wide = row_block(rows, hidden)
    narrow_shape = jax.ShapeDtypeStruct((tokens, width), bf16)
    wide_shape = jax.ShapeDtypeStruct((tokens, hidden), bf16)
    return pl.pallas_call(
        ffn_kernel,
        grid=(tokens // rows,),
        in_specs=[block] * 3 + [full(None)] * 5,
        out_specs=[block, block, wide, wide, block, block, block, block]
        + [keep_block(8, width), keep_block(1, hidden)],
        out_shape=[
            narrow_shape,
            narrow_shape,
            wide_shape,
            wide_shape,
            narrow_shape,
            narrow_shape,
            jax.ShapeDtypeStruct((tokens, width), f32),
            narrow_shape,
            jax.ShapeDtypeStruct((8, width), f32),
            jax.ShapeDtypeStruct((1, hidden), f32),
        ],
        scratch_shapes=[pltpu.VMEM((rows, hidden), f32)],
        compiler_params=params(),
        name="ffn_block",
        cost_estimate=cost([(tokens, width, hidden)] * 8),
    )(z, context, cotangent, out_w, in_w, ffn_w, vectors, bias)


def first_back_kernel(
    dz2_ref, dq_ref, z_ref, query_w, out_w, vec_ref, dz_ref, do_ref, dc_ref, sum_ref
):
    start_sums(sum_ref)
    grad_query = dq_ref[...]
    grad_first = dz2_ref[...] + dot_nt(grad_query, query_w[...])
    normal, scale = normalise(z_ref[...])
    add_rows(sum_ref, 0, grad_first * normal)
    add_rows(sum_ref, 1, grad_first)
    grad_start = normalise_back(grad_first, vec_ref[2:3, :], normal, scale)
    dz_ref[...] = grad_start
    grad_low = grad_start.astype(bf16)
    do_ref[...] = grad_low
    add_rows(sum_ref, 2, grad_low.astype(f32))
    add_rows(sum_ref, 3, grad_query.astype(f32))
    dc_ref[...] = dot_nt(grad_low, out_w[...]).astype(bf16)


def first_back(dz2, grad_query, z, query_w, out_w, vectors, rows=256):
    tokens, width = z.shape
    block = row_block(rows, width)
    return pl.pallas_call(
        first_back_kernel,
        grid=(tokens // rows,),
        in_specs=[block] * 3 + [full(None)] * 3,
        out_specs=[block] * 3 + [keep_block(8, width)],
        out_shape=[
            jax.ShapeDtypeStruct((tokens, width), f32),
            jax.ShapeDtypeStruct((tokens, width), bf16),
            jax.ShapeDtypeStruct((tokens, width), bf16),
            jax.ShapeDtypeStruct((8, width), f32),
        ],
        compiler_params=params(),
        name="first_back",
        cost_estimate=cost([(tokens, width, width)] * 4),
    )(dz2, grad_query, z, query_w, out_w, vectors)


def needed(info, row, part, rows):
    return ((info[0] == 1) | (row == 0)) & (part * rows < info[1 + row])


def needed_place(info, row, part, rows):
    used = jnp.where(info[0] == 1, row, 0)
    last = (info[1 + used] + rows - 1) // rows - 1
    return used, jnp.where(info[0] == 1, jnp.minimum(part, last), jnp.where(row == 0, jnp.minimum(part, last), last))


def project_kernel(rows, info, m_ref, w_ref, b_ref, k_ref, v_ref):
    row, part = pl.program_id(0), pl.program_id(1)

    @pl.when(needed(info, row, part, rows))
    def _():
        memory = m_ref[0]
        k_ref[0] = dot_nn(memory, w_ref[1]).astype(bf16)
        v_ref[0] = (dot_nn(memory, w_ref[2]) + b_ref[...]).astype(bf16)


def project_memory(info, memory, weights, bias, rows=256):
    count, length, width = memory.shape
    place = lambda row, part, info: needed_place(info, row, part, rows) + (0,)
    block = pl.BlockSpec((1, rows, width), place)
    return pl.pallas_call(
        functools.partial(project_kernel, rows),
        grid_spec=pltpu.PrefetchScalarGridSpec(
            num_scalar_prefetch=1,
            grid=(count, length // rows),
            in_specs=[block, full(None), full(None)],
            out_specs=[block] * 2,
        ),
        out_shape=[jax.ShapeDtypeStruct(memory.shape, bf16)] * 2,
        compiler_params=params(),
        name="project_memory",
        cost_estimate=cost([(count, length, width, width)] * 2),
    )(info, memory, weights, bias)


def memory_back_kernel(rows, info, dk_ref, dv_ref, w_ref, out_ref):
    row, part = pl.program_id(0), pl.program_id(1)
    here = needed(info, row, part, rows)

    @pl.when(here)
    def _():
        out_ref[0] = dot_nt(dk_ref[0], w_ref[1]) + dot_nt(dv_ref[0], w_ref[2])

    @pl.when(jnp.logical_not(here))
    def _():
        out_ref[...] = jnp.zeros_like(out_ref)


def memory_back(info, grad_keys, grad_values, weights, rows=256):
    count, length, width = grad_keys.shape
    block = pl.BlockSpec(
        (1, rows, width), lambda row, part, info: needed_place(info, row, part, rows) + (0,)
    )
    return pl.pallas_call(
        functools.partial(memory_back_kernel, rows),
        grid_spec=pltpu.PrefetchScalarGridSpec(
            num_scalar_prefetch=1,
            grid=(count, length // rows),
            in_specs=[block, block, full(None)],
            out_specs=pl.BlockSpec((1, rows, width), lambda row, part, info: (row, part, 0)),
        ),
        out_shape=jax.ShapeDtypeStruct(grad_keys.shape, f32),
        compiler_params=params(),
        name="memory_back",
        cost_estimate=cost([(count, length, width, width)] * 2),
    )(info, grad_keys, grad_values, weights)


def memory_weights_kernel(rows, info, m_ref, dk_ref, dv_ref, w_ref, sum_ref, key_sum, value_sum):
    row, part = pl.program_id(0), pl.program_id(1)

    @pl.when((row == 0) & (part == 0))
    def _():
        key_sum[...] = jnp.zeros_like(key_sum)
        value_sum[...] = jnp.zeros_like(value_sum)
        sum_ref[...] = jnp.zeros_like(sum_ref)

    @pl.when(needed(info, row, part, rows))
    def _():
        memory = m_ref[0]
        key_sum[...] += dot_tn(memory, dk_ref[0])
        value_sum[...] += dot_tn(memory, dv_ref[0])
        sum_ref[...] += jnp.sum(dv_ref[0].astype(f32), 0, keepdims=True)

    @pl.when((row == pl.num_programs(0) - 1) & (part == pl.num_programs(1) - 1))
    def _():
        w_ref[0] = key_sum[...].astype(bf16)
        w_ref[1] = value_sum[...].astype(bf16)


def memory_weights(info, memory, grad_keys, grad_values, rows=512):
    count, length, width = memory.shape
    block = pl.BlockSpec(
        (1, rows, width), lambda row, part, info: needed_place(info, row, part, rows) + (0,)
    )
    return pl.pallas_call(
        functools.partial(memory_weights_kernel, rows),
        grid_spec=pltpu.PrefetchScalarGridSpec(
            num_scalar_prefetch=1,
            grid=(count, length // rows),
            in_specs=[block] * 3,
            out_specs=[
                pl.BlockSpec((2, width, width), lambda row, part, info: (0, 0, 0)),
                pl.BlockSpec((1, width), lambda row, part, info: (0, 0)),
            ],
            scratch_shapes=[pltpu.VMEM((width, width), f32)] * 2,
        ),
        out_shape=[
            jax.ShapeDtypeStruct((2, width, width), bf16),
            jax.ShapeDtypeStruct((1, width), f32),
        ],
        compiler_params=params(),
        name="memory_weights",
        cost_estimate=cost([(count, length, width, width)] * 2),
    )(info, memory, grad_keys, grad_values)


def unit(ref, number, count):
    rows = ref.shape[1] // count
    return ref[:, number * rows : (number + 1) * rows, :].reshape(ref.shape[0] * rows, ref.shape[2])


def put_unit(ref, number, count, value):
    rows = ref.shape[1] // count
    ref[:, number * rows : (number + 1) * rows, :] = value.astype(bf16).reshape(
        ref.shape[0], rows, ref.shape[2]
    )


def qkv_kernel(x_ref, w_ref, b_ref, q_ref, k_ref, v_ref):
    x = x_ref[...]
    q_ref[...] = ((dot_nn(x, unit(w_ref, 0, 3)) + b_ref[0:1, :]) * HEAD**-0.5).astype(bf16)
    k_ref[...] = dot_nn(x, unit(w_ref, 1, 3)).astype(bf16)
    v_ref[...] = (dot_nn(x, unit(w_ref, 2, 3)) + b_ref[1:2, :]).astype(bf16)


def project_self(x, weights, bias, rows=256):
    tokens, width = x.shape
    block = row_block(rows, width)
    return pl.pallas_call(
        qkv_kernel,
        grid=(tokens // rows,),
        in_specs=[block, full(None), full(None)],
        out_specs=[block] * 3,
        out_shape=[jax.ShapeDtypeStruct((tokens, width), bf16)] * 3,
        compiler_params=params(),
        name="project_self",
        cost_estimate=cost([(tokens, width, width)] * 4),
    )(x, weights, bias)


def target_back_kernel(z_ref, q_ref, k_ref, v_ref, w_ref, out_ref):
    out_ref[...] = (
        z_ref[...]
        + dot_nt(q_ref[...], unit(w_ref, 0, 3))
        + dot_nt(k_ref[...], unit(w_ref, 1, 3))
        + dot_nt(v_ref[...], unit(w_ref, 2, 3))
    )


def target_back(dz, grad_queries, grad_keys, grad_values, weights, rows=256):
    tokens, width = dz.shape
    block = row_block(rows, width)
    return pl.pallas_call(
        target_back_kernel,
        grid=(tokens // rows,),
        in_specs=[block] * 4 + [full(None)],
        out_specs=block,
        out_shape=jax.ShapeDtypeStruct((tokens, width), f32),
        compiler_params=params(),
        name="target_back",
        cost_estimate=cost([(tokens, width, width)] * 4),
    )(dz, grad_queries, grad_keys, grad_values, weights)


def self_weights_kernel(x_ref, q_ref, k_ref, v_ref, w_ref, sum_ref):
    x = x_ref[...]
    sum_ref[...] = jnp.zeros_like(sum_ref)
    for number, ref in enumerate((q_ref, k_ref, v_ref)):
        grads = ref[...]
        put_unit(w_ref, number, 3, dot_tn(x, grads))
        sum_ref[number : number + 1, :] = jnp.sum(grads.astype(f32), 0, keepdims=True)


def self_weights(x, grad_queries, grad_keys, grad_values, pieces):
    tokens, width = x.shape
    return pl.pallas_call(
        self_weights_kernel,
        out_shape=[
            jax.ShapeDtypeStruct((pieces, 3 * width // pieces, width), bf16),
            jax.ShapeDtypeStruct((8, width), f32),
        ],
        compiler_params=params(),
        name="self_weights",
        cost_estimate=cost([(tokens, width, width)] * 4),
    )(x, grad_queries, grad_keys, grad_values)


def ffn_weights_kernel(h_ref, du_ref, a_ref, df_ref, w_ref):
    pieces, rows, width = w_ref.shape[1:]
    w_ref[0, :, : rows // 2, :] = (
        dot_tn(h_ref[...], du_ref[...]).astype(bf16).reshape(pieces, rows // 2, width)
    )
    w_ref[0, :, rows // 2 :, :] = (
        dot_tn(a_ref[...], df_ref[...]).astype(bf16).reshape(pieces, rows // 2, width)
    )


def ffn_weights(second_low, grad_hidden, active, grad_out, pieces):
    tokens, width = second_low.shape
    blocks = active.shape[1] // width
    whole = pl.BlockSpec((tokens, width), lambda part: (0, 0))
    part = pl.BlockSpec((tokens, width), lambda part: (0, part))
    return pl.pallas_call(
        ffn_weights_kernel,
        grid=(blocks,),
        in_specs=[whole, part, part, whole],
        out_specs=pl.BlockSpec(
            (1, pieces, 2 * width // pieces, width), lambda part: (part, 0, 0, 0)
        ),
        out_shape=jax.ShapeDtypeStruct((blocks, pieces, 2 * width // pieces, width), bf16),
        compiler_params=params(),
        name="ffn_weights",
        cost_estimate=cost([(tokens, width, blocks * width)] * 2),
    )(second_low, grad_hidden, active, grad_out)


def wide(array):
    return array.astype(f32)


def weight_grad(left, right):
    return dot_tn(left, right).astype(bf16)


def forward_back(
    target, memory, cotangent, info, pieces, self_qkv, self_out, cross_qkv, cross_out, ffn, small
):
    self_bias, cross_bias, ffn_in_bias, ffn_out_bias, gain, shift = [wide(item) for item in small]
    queries, keys, values = project_self(target, self_qkv, self_bias)
    context_self, stats_self = self_attend(info, queries, keys, values)
    vec_first = jnp.stack([self_bias[2], cross_bias[0], gain[0], shift[0]])
    total_first, first_low, query_cross = first_norm(
        target, context_self, self_out, cross_qkv[0], vec_first
    )
    key_cross, value_cross = project_memory(info, memory, cross_qkv, cross_bias[1:2])
    context_cross, stats_cross = cross_attend(info, query_cross, key_cross, value_cross)
    vec_ffn = jnp.stack(
        [cross_bias[2], ffn_out_bias, gain[0], shift[0], gain[1], shift[1], gain[2], shift[2]]
    )
    output, second_low, active, du, df, do_cross, dz2, dc_cross, sums_ffn, sums_wide = ffn_block(
        total_first, context_cross, cotangent, cross_out, ffn[0], ffn[1], vec_ffn, ffn_in_bias[None]
    )
    grad_ffn = ffn_weights(second_low, du, active, df, pieces)
    grad_cross_out = weight_grad(context_cross, do_cross)
    dq_cross, dk_cross, dv_cross = cross_attend_back(
        info, query_cross, key_cross, value_cross, dc_cross, stats_cross
    )
    grad_cross_kv, sum_value_cross = memory_weights(info, memory, dk_cross, dv_cross)
    grad_cross_q = weight_grad(first_low, dq_cross)
    dz1, do_self, dc_self, sums_first = first_back(
        dz2, dq_cross, total_first, cross_qkv[0], self_out, vec_first
    )
    grad_self_out = weight_grad(context_self, do_self)
    grad_mid = jnp.concatenate(
        [
            item.reshape(pieces, item.shape[0] // pieces, item.shape[1])
            for item in (grad_cross_q, grad_cross_kv[0], grad_cross_kv[1], grad_cross_out, grad_self_out)
        ],
        1,
    )
    dq_self, dk_self, dv_self = self_attend_back(
        info, queries, keys, values, dc_self, stats_self
    )
    grad_self, sums_self = self_weights(target, dq_self, dk_self, dv_self, pieces)
    target_grad = target_back(dz1, dq_self, dk_self, dv_self, self_qkv)
    memory_grad = memory_back(info, dk_cross, dv_cross, cross_qkv)
    grad_small = (
        jnp.stack([sums_self[0], sums_self[2], sums_first[2]]),
        jnp.stack([sums_first[3], sum_value_cross[0], sums_ffn[5]]),
        sums_wide[0],
        sums_ffn[2],
        jnp.stack([sums_first[0], sums_ffn[3], sums_ffn[0]]),
        jnp.stack([sums_first[1], sums_ffn[4], sums_ffn[1]]),
    )
    return (output, target_grad, memory_grad), grad_ffn, grad_mid, grad_self, grad_small


def pair_swap(array, axis, bit):
    count = lax.axis_size(axis)
    return lax.ppermute(array, axis, [(place, place ^ bit) for place in range(count)])


def ring(array, axis, shift):
    count = lax.axis_size(axis)
    return lax.ppermute(array, axis, [(place, (place + shift) % count) for place in range(count)])


def pick(array, axis, index):
    return lax.dynamic_index_in_dim(array, index, axis, keepdims=False)


def places():
    dp, fsdp = lax.axis_index("dp"), lax.axis_index("fsdp")
    return dp // 2, dp % 2, fsdp // 2, fsdp % 2


def add_half(array, axis, mine, mesh_axis, bit):
    got = pair_swap(pick(array, axis, 1 - mine), mesh_axis, bit)
    return (wide(pick(array, axis, mine)) + wide(got)).astype(bf16)


def add_depth(array, depth):
    total = wide(pick(array, 0, depth))
    for step in (1, 2, 3):
        total = total + wide(ring(pick(array, 0, (depth + step) % 4), "fsdp", 2 * step))
    return total.astype(bf16)


def reduce_pieces(grads):
    high, core, depth, side = places()
    pieces, rows, width = grads.shape
    parts = grads.reshape(4, 2, 2, 2, rows // 4, width)
    parts = add_half(parts, 3, core, "dp", 1)
    half = rows // 8 // 8 * 8
    one, two = parts[:, :, :, :half], parts[:, :, :, half:]
    one, two = add_half(one, 2, high, "dp", 2), add_half(two, 1, side, "fsdp", 1)
    one, two = lax.optimization_barrier((one, two))
    one, two = add_half(one, 1, side, "fsdp", 1), add_half(two, 1, high, "dp", 2)
    one, two = lax.optimization_barrier((one, two))
    return jnp.concatenate([add_depth(one, depth), add_depth(two, depth)], 0)


def join_pair(array, axis, mine, mesh_axis, bit):
    got = pair_swap(array, mesh_axis, bit)
    first = jnp.where(mine == 0, array, got)
    second = jnp.where(mine == 0, got, array)
    return jnp.stack([first, second], axis)


def share_dp(array):
    high, core, _, _ = places()
    both = join_pair(array, 0, high, "dp", 2)
    return join_pair(both, 1, core, "dp", 1).reshape((4,) + array.shape)


def join_depth(array, depth):
    parts = [array] + [ring(array, "fsdp", 2 * step) for step in (1, 2, 3)]
    out = jnp.zeros((4,) + array.shape, array.dtype)
    for step, part in enumerate(parts):
        out = lax.dynamic_update_index_in_dim(out, part, (depth - step) % 4, 0)
    return out


def gather_pieces(array):
    high, core, depth, side = places()
    half = array.shape[0] // 2 // 8 * 8
    one, two = join_depth(array[:half], depth), join_depth(array[half:], depth)
    one, two = lax.optimization_barrier((one, two))
    one, two = join_pair(one, 1, side, "fsdp", 1), join_pair(two, 1, high, "dp", 2)
    one, two = lax.optimization_barrier((one, two))
    one, two = join_pair(one, 2, high, "dp", 2), join_pair(two, 1, side, "fsdp", 1)
    both = jnp.concatenate([one, two], 3)
    return join_pair(both, 3, core, "dp", 1).reshape((8, 4) + array.shape)


def split_small(rows, unit_rows):
    take = lambda low, count: rows[:, low * unit_rows : (low + count) * unit_rows]
    three = lambda low: jnp.swapaxes(
        take(low, 3).reshape(rows.shape[0], 3, unit_rows), 0, 1
    ).reshape(3, -1)
    return three(0), three(3), take(6, 4), take(10, 1).reshape(-1), three(11), three(14)


def fast_layer(
    target, memory, cotangent, bucket, source_len, self_qkv, self_out, self_bias, cross_qkv,
    cross_out, cross_bias, ffn_in, ffn_in_bias, ffn_out, ffn_out_bias, norm_gain, norm_bias,
):
    dp = lax.axis_index("dp")
    width = target.shape[1]
    own = self_out.shape[0]
    pieces = width // own
    info = jnp.concatenate([bucket, source_len])
    vectors = jnp.concatenate(
        [item.reshape(-1) for item in (self_bias, cross_bias, ffn_in_bias, ffn_out_bias, norm_gain, norm_bias)]
    )
    vectors = jnp.pad(vectors, (0, 8 * width - vectors.shape[0])).reshape(8, width)
    quarter = 3 * own // 4
    head = jnp.concatenate(
        [lax.dynamic_slice_in_dim(self_qkv.reshape(3 * own, width), dp * quarter, quarter, 0), vectors], 0
    )
    head = gather_pieces(head)
    self_qkv_w = head[:, :, :quarter].reshape(pieces, 3 * own, width)
    small = split_small(head[:, 0, quarter:].reshape(pieces, -1), own)
    small = list(small)
    small[2] = jnp.swapaxes(small[2].reshape(pieces, 4, own), 0, 1).reshape(-1)
    units = jnp.concatenate([self_out[None], cross_qkv], 0)
    mid = lax.all_gather(pick(units, 0, dp), ("dp", "fsdp"), axis=0, tiled=True)
    mid = mid.reshape(4, width, width)
    cross_rows = lax.dynamic_slice_in_dim(cross_out, dp * (own // 4), own // 4, 0)
    in_cols = pick(ffn_in.reshape(own, pieces, 4, own), 2, dp).reshape(own, width)
    out_rows = pick(ffn_out.reshape(4, own, width), 0, dp)
    tail = lax.all_gather(
        jnp.concatenate([in_cols, out_rows, cross_rows], 0), ("dp", "fsdp"), axis=0, tiled=False
    ).reshape(4, pieces, 2 * own + own // 4, width)
    ffn = (
        tail[:, :, :own].reshape(4, width, width),
        tail[:, :, own : 2 * own].reshape(4, width, width),
    )
    cross_out_w = jnp.swapaxes(tail[:, :, 2 * own :], 0, 1).reshape(width, width)
    outs, grad_ffn, grad_mid, grad_self, grad_small = forward_back(
        target, memory, cotangent, info, pieces, self_qkv_w, mid[0], mid[1:], cross_out_w, ffn, small
    )
    sum_ffn = lax.psum_scatter(
        grad_ffn.reshape(-1, width), ("dp", "fsdp"), scatter_dimension=0, tiled=True
    )
    sum_mid = reduce_pieces(grad_mid)
    grad_small = list(grad_small)
    grad_small[2] = jnp.swapaxes(grad_small[2].reshape(4, pieces, own), 0, 1).reshape(-1)
    per_owner = jnp.concatenate(
        [
            jnp.swapaxes(item.reshape(item.shape[0], pieces, -1), 0, 1).reshape(pieces, -1)
            if item.ndim == 2
            else item.reshape(pieces, -1)
            for item in grad_small
        ],
        1,
    )
    per_owner = jnp.pad(per_owner, ((0, 0), (0, 4 * width - per_owner.shape[1])))
    per_owner = jnp.pad(per_owner.reshape(pieces, 4, 1, width), ((0, 0), (0, 0), (0, 7), (0, 0)))
    grad_self = jnp.concatenate(
        [grad_self.reshape(pieces, 4, quarter, width), per_owner.astype(bf16)], 2
    )
    sum_self = reduce_pieces(grad_self.reshape(pieces, -1, width))
    everything = share_dp(jnp.concatenate([sum_ffn, sum_mid, sum_self], 0))
    everything = everything.astype(f32)
    low = 0
    parts = []
    for count in (own, own, 5 * own // 4, quarter, 8):
        parts.append(everything[:, low : low + count])
        low += count
    grad_in = jnp.moveaxis(parts[0].reshape(4, own, pieces, own), 0, 2).reshape(own, 4 * width)
    grad_out = parts[1].reshape(4 * own, width)
    mid_rows = parts[2].reshape(5, own, width)
    self_rows = parts[3].reshape(3, own, width)
    flat = parts[4][:, 0].reshape(-1)
    bias_self = flat[: 3 * own].reshape(3, own)
    bias_cross = flat[3 * own : 6 * own].reshape(3, own)
    bias_in = flat[6 * own : 10 * own]
    bias_out = flat[10 * own : 11 * own]
    gain = flat[11 * own : 14 * own].reshape(3, own)
    shift = flat[14 * own : 17 * own].reshape(3, own)
    return outs + (
        self_rows, mid_rows[4], bias_self, mid_rows[:3], mid_rows[3], bias_cross, grad_in, bias_in,
        grad_out, bias_out, gain, shift,
    )


def plain_layer(
    target, memory, cotangent, bucket, source_len, self_qkv, self_out, self_bias, cross_qkv,
    cross_out, cross_bias, ffn_in, ffn_in_bias, ffn_out, ffn_out_bias, norm_gain, norm_bias,
):
    gather = lambda item, axis: lax.all_gather(item, "fsdp", axis=axis, tiled=True)
    info = jnp.concatenate([bucket, source_len])
    width = target.shape[1]
    blocks = ffn_out.shape[0] * lax.axis_size("fsdp") // width
    ffn_in_w = jnp.swapaxes(gather(ffn_in, 0).reshape(width, blocks, width), 0, 1)
    ffn_out_w = gather(ffn_out, 0).reshape(blocks, width, width)
    small = (
        gather(self_bias, 1), gather(cross_bias, 1), gather(ffn_in_bias, 0), gather(ffn_out_bias, 0),
        gather(norm_gain, 1), gather(norm_bias, 1),
    )
    outs, grad_ffn, grad_mid, grad_self, grad_small = forward_back(
        target, memory, cotangent, info, 1, gather(self_qkv, 1).reshape(1, 3 * width, width),
        gather(self_out, 0), gather(cross_qkv, 1), gather(cross_out, 0), (ffn_in_w, ffn_out_w), small,
    )

    def reduce(grad, axis):
        piece = lax.psum_scatter(wide(grad), "fsdp", scatter_dimension=axis, tiled=True)
        return lax.psum(piece, "dp")

    grad_in = jnp.swapaxes(grad_ffn[:, 0, :width], 0, 1).reshape(width, blocks * width)
    grad_out = grad_ffn[:, 0, width:].reshape(blocks * width, width)
    mid = grad_mid.reshape(5, width, width)
    return outs + (
        reduce(grad_self.reshape(3, width, width), 1),
        reduce(mid[4], 0),
        reduce(grad_small[0], 1),
        reduce(mid[:3], 1),
        reduce(mid[3], 0),
        reduce(grad_small[1], 1),
        reduce(grad_in, 0),
        reduce(grad_small[2], 0),
        reduce(grad_out, 0),
        reduce(grad_small[3], 0),
        reduce(grad_small[4], 1),
        reduce(grad_small[5], 1),
    )


def solution(mesh):
    rows = P(("dp", "fsdp"))
    first = P("fsdp")
    second = P(None, "fsdp")
    weights = (second, first, second, second, first, second, first, first, first, first, second, second)
    layer = fast_layer if (mesh.shape["dp"], mesh.shape["fsdp"]) == (4, 8) else plain_layer
    return jax.shard_map(
        layer,
        mesh=mesh,
        in_specs=(rows,) * 5 + weights,
        out_specs=(rows,) * 3 + weights,
        check_vma=False,
    )
```

time: 1370 us -> 539 us (0.39)
  the two profiles are of different devices: /device:TPU:9 before, /device:TPU:23 now
where the time goes in v1:
time: 539 us; the launch traced here: 531 us
  Pallas kernels  272 us (50%)
  waiting for transfers between devices  85.3 us (16%)
  local copies, waits for them, and re-layouts  63.9 us (12%)
  starting transfers between devices  63.4 us (12%)
  other arithmetic  26.1 us (5%)
  between operations  15.6 us (3%)
    ppermute x17, waiting for transfers between devices, pair_swap(): lax.ppermute(array, axis, [(place, place ^ bit) for place in range(count)])  66.8 us
    pallas_call x1, Pallas kernels, cross_attend_back(): pl.pallas_call(cross_back_kernel, grid_spec=pltpu.PrefetchScalarGridSpec(...  46 us
    ppermute x17, starting transfers between devices, pair_swap(): lax.ppermute(array, axis, [(place, place ^ bit) for place in range(count)])  39.2 us
    pallas_call x1, Pallas kernels, ffn_block(): pl.pallas_call(ffn_kernel, grid=(tokens // rows,), in_specs=[block] * 3 +...  37.1 us
    pallas_call x1, Pallas kernels, cross_attend(): pl.pallas_call(cross_kernel, grid_spec=pltpu.PrefetchScalarGridSpec(num_s...  35.1 us
    ppermute x18, starting transfers between devices, ring(): lax.ppermute(array, axis, [(place, (place + shift) % count) for place in...  24 us
    pallas_call x1, Pallas kernels, self_attend_back(): pl.pallas_call(self_back_kernel, grid_spec=pltpu.PrefetchScalarGridSpec(n...  21.5 us
    pallas_call x1, Pallas kernels, memory_back(): pl.pallas_call(functools.partial(memory_back_kernel, rows), grid_spec=plt...  21.3 us
  transfers between devices with their start and end apart: 38, of which 19 were waited for; matrix products, arithmetic and copies ran while one was open for 11% of the time, Pallas kernels for 41%

profile of v1, /device:TPU:23, one launch (start us, length us, event | category | flops | bytes accessed | tf_op | source)
XLA Modules:
  0.0 530.8 jit_solution(17851096259659846609)
XLA Ops:
  30.0 5.7 %collective-permute-done.6 = bf16[4,40,768]{2,1,0:T(8,128)(2,1)S(1)} collective-permute-done((bf16[4,40,768]{2,1,0:T(8,128)(2,1)S(1)}, bf16[4,40,768]{2,1,0:T(8,128)(2,1)S(1)}, u32[]{:S(2)}, u32[]{:S(2)}) %collective-permute-start.6) | collective-permute-done | bytes 245792 | tf_op jit(solution)/shard_map/ppermute | solution.py:830
  37.2 11.8 %collective-permute-done.8 = bf16[4,2,40,768]{3,2,0,1:T(8,128)(2,1)S(1)} collective-permute-done((bf16[4,2,40,768]{3,2,0,1:T(8,128)(2,1)S(1)}, bf16[4,2,40,768]{3,2,0,1:T(8,128)(2,1)S(1)}, u32[]{:S(2)}, u32[]{:S(2)}) %collective-permute-start.8) | collective-permute-done | bytes 491552 | tf_op jit(solution)/shard_map/ppermute | solution.py:830
  68.8 7.3 %project_self.1 = (bf16[1024,768]{1,0:T(8,128)(2,1)}, bf16[1024,768]{1,0:T(8,128)(2,1)}, bf16[1024,768]{1,0:T(8,128)(2,1)}) custom-call(bf16[1024,768]{1,0:T(8,128)(2,1)} %x_ref.5, bf16[8,288,768]{2,1,0:T(8,128)(2,1)} %bitcast.225, f32[3,768]{1,0:T(4,128)} %convert_element_type.288.b_ref), custom_call_target="tpu_custom_call" | custom-call | flops 4831838208 | bytes 8388608 | tf_op jit(solution)/shard_map/project_self/pallas_call | solution.py:679
  76.2 17.8 %self_attend.1 = (bf16[1024,768]{1,0:T(8,128)(2,1)}, f32[6,2,1024]{2,1,0:T(2,128)}) custom-call(s32[5]{0:T(128)} %pad_add_fusion.info, bf16[1024,768]{1,0:T(8,128)(2,1)} %get-tuple-element.67.q_ref, bf16[1024,768]{1,0:T(8,128)(2,1)} %get-tuple-element.68.k_ref, bf16[1024,768]{1,0:T(8,128)(2,1)} %get-tuple-element.69.v_ref), custom_call_target="tpu_custom_call" | custom-call | flops 12884901888 | bytes 8388608 | tf_op jit(solution)/shard_map/self_attend/pallas_call | solution.py:229
  94.0 4.3 slice.318
  99.8 8.0 %first_norm.1 = (f32[1024,768]{1,0:T(8,128)}, bf16[1024,768]{1,0:T(8,128)(2,1)}, bf16[1024,768]{1,0:T(8,128)(2,1)}) custom-call(bf16[1024,768]{1,0:T(8,128)(2,1)} %x_ref.5, bf16[1024,768]{1,0:T(8,128)(2,1)} %get-tuple-element.70.c_ref, bf16[768,768]{1,0:T(8,128)(2,1)} %get-tuple-element.131.out_w, bf16[768,768]{1,0:T(8,128)(2,1)} %get-tuple-element.130.query_w, ...), custom_call_target="tpu_custom_call" | custom-call | flops 4831838208 | bytes 8388608 | tf_op jit(solution)/shard_map/first_norm/pallas_call | solution.py:382
  107.8 19.3 %project_memory.1 = (bf16[4,1024,768]{2,1,0:T(8,128)(2,1)}, bf16[4,1024,768]{2,1,0:T(8,128)(2,1)}) custom-call(s32[5]{0:T(128)} %pad_add_fusion.info, bf16[4,1024,768]{2,1,0:T(8,128)(2,1)} %m_ref.3, bf16[3,768,768]{2,1,0:T(8,128)(2,1)} %bitcast.227, f32[1,768]{1,0:T(1,128)} %slice.254.b_ref), custom_call_target="tpu_custom_call" | custom-call | flops 9663676416 | bytes 8388608 | tf_op jit(solution)/shard_map/project_memory/pallas_call | solution.py:560
  127.1 35.1 %cross_attend.1 = (bf16[1024,768]{1,0:T(8,128)(2,1)}, f32[6,2,1024]{2,1,0:T(2,128)}) custom-call(s32[5]{0:T(128)} %pad_add_fusion.info, bf16[1024,768]{1,0:T(8,128)(2,1)} %get-tuple-element.72.q_ref, bf16[4,1024,768]{2,1,0:T(8,128)(2,1)} %get-tuple-element.73.k_ref, bf16[4,1024,768]{2,1,0:T(8,128)(2,1)} %get-tuple-element.74.v_ref), custom_call_target="tpu_custom_call" | custom-call | flops 25769803776 | bytes 8388608 | tf_op jit(solution)/shard_map/cross_attend/pallas_call | solution.py:278
  162.2 6.7 %all-gather.7.cloned.1.call-done = bf16[6912,768]{1,0:T(8,128)(2,1)} async-done(((bf16[216,768]{1,0:T(8,128)(2,1)}), bf16[6912,768]{1,0:T(8,128)(2,1)}) %all-gather.7.cloned.1.call-update) | async-done | bytes 10616848 | tf_op jit(solution)/shard_map/all_gather | solution.py:942
  170.2 8.2 %fusion.27 = (bf16[4,8,96,768]{3,2,1,0:T(8,128)(2,1)}, bf16[4,8,96,768]{3,2,1,0:T(8,128)(2,1)}) fusion(bf16[4,8,216,768]{3,2,1,0:T(8,128)(2,1)} %bitcast.214), kind=kLoop, calls=%fused_computation.150 | loop fusion | bytes 18874368 | tf_op jit(solution)/shard_map/slice | solution.py:947
  179.6 37.1 %ffn_block.1 = (bf16[1024,768]{1,0:T(8,128)(2,1)}, bf16[1024,768]{1,0:T(8,128)(2,1)}, bf16[1024,3072]{1,0:T(8,128)(2,1)}, bf16[1024,3072]{1,0:T(8,128)(2,1)}, bf...) custom-call(f32[1024,768]{1,0:T(8,128)} %get-tuple-element.71.z_ref,, ...), custom_call_target="tpu_custom_call" | custom-call | flops 38654705664 | bytes 8388608 | tf_op jit(solution)/shard_map/ffn_block/pallas_call | solution.py:473
  217.6 15.0 %ffn_weights.1 = bf16[4,8,192,768]{3,2,1,0:T(8,128)(2,1)} custom-call(bf16[1024,768]{1,0:T(8,128)(2,1)} %get-tuple-element.89.h_ref, bf16[1024,3072]{1,0:T(8,128)(2,1)} %get-tuple-element.90.du_ref, bf16[1024,3072]{1,0:T(8,128)(2,1)} %get-tuple-element.91.a_ref, bf16[1024,768]{1,0:T(8,128)(2,1)} %get-tuple-element.92.df_ref), custom_call_target="tpu_custom_call" | custom-call | flops 9663676416 | bytes 8388608 | tf_op jit(solution)/shard_map/ffn_weights/pallas_call | solution.py:753
  232.6 46.0 %cross_attend_back.1 = (bf16[1024,768]{1,0:T(8,128)(2,1)}, bf16[4,1024,768]{2,1,0:T(8,128)(2,1)}, bf16[4,1024,768]{2,1,0:T(8,128)(2,1)}) custom-call(s32[5]{0:T(128)} %pad_add_fusion.info, bf16[1024,768]{1,0:T(8,128)(2,1)} %get-tuple-element.72.q_ref, bf16[4,1024,768]{2,1,0:T(8,128)(2,1)} %get-tuple-element.73.k_ref, ...), custom_call_target="tpu_custom_call" | custom-call | flops 38654705664 | bytes 8388608 | tf_op jit(solution)/shard_map/cross_attend_back/pallas_call | solution.py:305
  278.6 8.7 %first_back.1 = (f32[1024,768]{1,0:T(8,128)}, bf16[1024,768]{1,0:T(8,128)(2,1)}, bf16[1024,768]{1,0:T(8,128)(2,1)}, f32[8,768]{1,0:T(8,128)}) custom-call(f32[1024,768]{1,0:T(8,128)} %get-tuple-element.77.dz2_ref, bf16[1024,768]{1,0:T(8,128)(2,1)} %get-tuple-element.80.dq_ref, f32[1024,768]{1,0:T(8,128)} %get-tuple-element.71.z_ref, ...), custom_call_target="tpu_custom_call" | custom-call | flops 4831838208 | bytes 8388608 | tf_op jit(solution)/shard_map/first_back/pallas_call | solution.py:519
  287.3 21.5 %self_attend_back.1 = (bf16[1024,768]{1,0:T(8,128)(2,1)}, bf16[1024,768]{1,0:T(8,128)(2,1)}, bf16[1024,768]{1,0:T(8,128)(2,1)}) custom-call(s32[5]{0:T(128)} %pad_add_fusion.info, bf16[1024,768]{1,0:T(8,128)(2,1)} %get-tuple-element.67.q_ref, bf16[1024,768]{1,0:T(8,128)(2,1)} %get-tuple-element.68.k_ref, bf16[1024,768]{1,0:T(8,128)(2,1)} %get-tuple-element.69.v_ref, ...), custom_call_target="tpu_custom_call" | custom-call | flops 19327352832 | bytes 8388608 | tf_op jit(solution)/shard_map/self_attend_back/pallas_call | solution.py:251
  308.8 8.6 %self_weights.1 = (bf16[8,288,768]{2,1,0:T(8,128)(2,1)}, f32[8,768]{1,0:T(8,128)}) custom-call(bf16[1024,768]{1,0:T(8,128)(2,1)} %x_ref.5, bf16[1024,768]{1,0:T(8,128)(2,1)} %get-tuple-element.84.q_ref, bf16[1024,768]{1,0:T(8,128)(2,1)} %get-tuple-element.85.k_ref, bf16[1024,768]{1,0:T(8,128)(2,1)} %get-tuple-element.86.v_ref), custom_call_target="tpu_custom_call" | custom-call | flops 4831838208 | bytes 8388608 | tf_op jit(solution)/shard_map/self_weights/pallas_call | solution.py:726
  319.0 17.4 %memory_weights.1 = (bf16[2,768,768]{2,1,0:T(8,128)(2,1)}, f32[1,768]{1,0:T(1,128)}) custom-call(s32[5]{0:T(128)} %pad_add_fusion.info, bf16[4,1024,768]{2,1,0:T(8,128)(2,1)} %m_ref.3, bf16[4,1024,768]{2,1,0:T(8,128)(2,1)} %get-tuple-element.87.dk_ref, bf16[4,1024,768]{2,1,0:T(8,128)(2,1)} %get-tuple-element.88.dv_ref), custom_call_target="tpu_custom_call" | custom-call | flops 9663676416 | bytes 8388608 | tf_op jit(solution)/shard_map/memory_weights/pallas_call | solution.py:635
  360.0 18.6 %collective-permute-start.23 = (bf16[4,2,40,768]{3,2,0,1:T(8,128)(2,1)S(1)}, bf16[4,2,40,768]{3,2,0,1:T(8,128)(2,1)S(1)}, u32[]{:S(2)}, u32[]{:S(2)}) collective-permute-start(bf16[4,2,40,768]{3,2,0,1:T(8,128)(2,1)S(1)} %dynamic-slice_bitcast_fusion.5), channel_id=1, source_target_pairs={{0,16},{8,24},{16,0},{24,8},{1,17},{9,25},{17,1},{25,9},{2,18},{10... | collective-permute-start | bytes 1474568 | tf_op jit(solution)/shard_map/ppermute | solution.py:830
  379.3 11.0 %collective-permute-done.23 = bf16[4,2,40,768]{3,2,0,1:T(8,128)(2,1)S(1)} collective-permute-done((bf16[4,2,40,768]{3,2,0,1:T(8,128)(2,1)S(1)}, bf16[4,2,40,768]{3,2,0,1:T(8,128)(2,1)S(1)}, u32[]{:S(2)}, u32[]{:S(2)}) %collective-permute-start.23) | collective-permute-done | bytes 491552 | tf_op jit(solution)/shard_map/ppermute | solution.py:830
  403.7 19.6 %collective-permute-done.25 = bf16[4,40,768]{2,1,0:T(8,128)(2,1)} collective-permute-done((bf16[4,40,768]{2,1,0:T(8,128)(2,1)}, bf16[4,40,768]{2,1,0:T(8,128)(2,1)}, u32[]{:S(2)}, u32[]{:S(2)}) %collective-permute-start.25) | collective-permute-done | bytes 245792 | tf_op jit(solution)/shard_map/ppermute | solution.py:830
  460.6 8.0 %collective-permute-done.33 = bf16[392,768]{1,0:T(8,128)(2,1)S(1)} collective-permute-done((bf16[392,768]{1,0:T(8,128)(2,1)S(1)}, bf16[392,768]{1,0:T(8,128)(2,1)S(1)}, u32[]{:S(2)}, u32[]{:S(2)}) %collective-permute-start.33) | collective-permute-done | bytes 602144 | tf_op jit(solution)/shard_map/ppermute | solution.py:830
  469.9 10.3 %collective-permute-start.34 = (bf16[2,392,768]{2,1,0:T(8,128)(2,1)}, bf16[2,392,768]{2,1,0:T(8,128)(2,1)S(1)}, u32[]{:S(2)}, u32[]{:S(2)}) collective-permute-start(bf16[2,392,768]{2,1,0:T(8,128)(2,1)} %pad_maximum_fusion.2), channel_id=1, source_target_pairs={{0,8},{8,0},{16,24},{24,16},{1,9},{9,1},{17,25},{25,17},{2,10},{10... | collective-permute-start | bytes 3612680 | tf_op jit(solution)/shard_map/ppermute | solution.py:830
  480.2 8.9 %target_back.1 = f32[1024,768]{1,0:T(8,128)} custom-call(f32[1024,768]{1,0:T(8,128)} %get-tuple-element.81.z_ref, bf16[1024,768]{1,0:T(8,128)(2,1)} %get-tuple-element.84.q_ref, bf16[1024,768]{1,0:T(8,128)(2,1)} %get-tuple-element.85.k_ref, bf16[1024,768]{1,0:T(8,128)(2,1)} %get-tuple-element.86.v_ref, bf16[8,288,768]{2,1,0:T(8,128)(2,1)} %bitcast.226), custom_call_target="tpu_custom_call" | custom-call | flops 4831838208 | bytes 8388608 | tf_op jit(solution)/shard_map/target_back/pallas_call | solution.py:703
  489.1 21.3 %memory_back.1 = f32[4,1024,768]{2,1,0:T(8,128)} custom-call(s32[5]{0:T(128)} %pad_add_fusion.info, bf16[4,1024,768]{2,1,0:T(8,128)(2,1)} %get-tuple-element.87.dk_ref, bf16[4,1024,768]{2,1,0:T(8,128)(2,1)} %get-tuple-element.88.dv_ref, bf16[3,768,768]{2,1,0:T(8,128)(2,1)} %bitcast.228), custom_call_target="tpu_custom_call" | custom-call | flops 9663676416 | bytes 8388608 | tf_op jit(solution)/shard_map/memory_back/pallas_call | solution.py:593
  (281 shorter events, 138.8 us)
Async XLA Ops:
  7.2 86.8 %all-gather.5.cloned.1.call-start = ((), (), s32[]{:S(2)}) async-start(), calls=%async_computation.2 | async-start | bytes 4866048 | tf_op jit(solution)/shard_map/all_gather | solution.py:937
  9.0 159.9 %all-gather.7.cloned.1.call-start = ((), (), s32[]{:S(2)}) async-start(), calls=%async_computation.3 | async-start | bytes 10948608 | tf_op jit(solution)/shard_map/all_gather | solution.py:942
  14.4 425.0 %reduce-scatter.2.cloned.1.call-start = ((), (), s32[]{:S(2)}) async-start(), calls=%async_computation.1 | async-start | bytes 9732096 | tf_op jit(solution)/shard_map/reduce_scatter | solution.py:953
  15.4 11.3 %collective-permute-start.1 = (bf16[40,768]{1,0:T(8,128)(2,1)S(1)}, bf16[40,768]{1,0:T(8,128)(2,1)S(1)}, u32[]{:S(2)}, u32[]{:S(2)}) collective-permute-start(bf16[40,768]{1,0:T(8,128)(2,1)S(1)} %get-tuple-element.123), channel_id=1, source_target_pairs={{0,4},{1,5},{2,6},{3,7},{4,0},{5,1},{6,2},{7,3},{8,12},{9,13},{10,... | collective-permute-start | bytes 184328 | tf_op jit(solution)/shard_map/ppermute | solution.py:835
  15.5 7.7 %collective-permute-start = (bf16[40,768]{1,0:T(8,128)(2,1)S(1)}, bf16[40,768]{1,0:T(8,128)(2,1)S(1)}, u32[]{:S(2)}, u32[]{:S(2)}) collective-permute-start(bf16[40,768]{1,0:T(8,128)(2,1)S(1)} %get-tuple-element.123), channel_id=1, source_target_pairs={{0,2},{1,3},{2,4},{3,5},{4,6},{5,7},{6,0},{7,1},{8,10},{9,11},{10,... | collective-permute-start | bytes 184328 | tf_op jit(solution)/shard_map/ppermute | solution.py:835
  16.8 10.6 %collective-permute-start.2 = (bf16[40,768]{1,0:T(8,128)(2,1)S(1)}, bf16[40,768]{1,0:T(8,128)(2,1)S(1)}, u32[]{:S(2)}, u32[]{:S(2)}) collective-permute-start(bf16[40,768]{1,0:T(8,128)(2,1)S(1)} %get-tuple-element.123), channel_id=1, source_target_pairs={{0,6},{1,7},{2,0},{3,1},{4,2},{5,3},{6,4},{7,5},{8,14},{9,15},{10,... | collective-permute-start | bytes 184328 | tf_op jit(solution)/shard_map/ppermute | solution.py:835
  35.9 13.0 %collective-permute-start.8 = (bf16[4,2,40,768]{3,2,0,1:T(8,128)(2,1)S(1)}, bf16[4,2,40,768]{3,2,0,1:T(8,128)(2,1)S(1)}, u32[]{:S(2)}, u32[]{:S(2)}) collective-permute-start(bf16[4,2,40,768]{3,2,0,1:T(8,128)(2,1)S(1)} %pad_maximum_fusion.4), channel_id=1, source_target_pairs={{0,16},{8,24},{16,0},{24,8},{1,17},{9,25},{17,1},{25,9},{2,18},{10... | collective-permute-start | bytes 1474568 | tf_op jit(solution)/shard_map/ppermute | solution.py:830
  36.0 14.9 %collective-permute-start.9 = (bf16[4,2,40,768]{3,2,1,0:T(8,128)(2,1)S(1)}, bf16[4,2,40,768]{3,2,1,0:T(8,128)(2,1)S(1)}, u32[]{:S(2)}, u32[]{:S(2)}) collective-permute-start(bf16[4,2,40,768]{3,2,1,0:T(8,128)(2,1)S(1)} %pad_maximum_fusion.5), channel_id=1, source_target_pairs={{0,1},{1,0},{2,3},{3,2},{4,5},{5,4},{6,7},{7,6},{8,9},{9,8},{10,11... | collective-permute-start | bytes 1474568 | tf_op jit(solution)/shard_map/ppermute | solution.py:830
  343.3 14.5 %collective-permute-start.22 = (bf16[4,2,2,80,768]{4,3,0,2,1:T(8,128)(2,1)}, bf16[4,2,2,80,768]{4,3,0,2,1:T(8,128)(2,1)S(1)}, u32[]{:S(2)}, u32[]{:S(2)}) collective-permute-start(bf16[4,2,2,80,768]{4,3,0,2,1:T(8,128)(2,1)} %dynamic-slice_bitcast_fusion.1), channel_id=1, source_target_pairs={{0,8},{8,0},{16,24},{24,16},{1,9},{9,1},{17,25},{25,17},{2,10},{10... | collective-permute-start | bytes 5898248 | tf_op jit(solution)/shard_map/ppermute | solution.py:830
  357.8 36.0 %collective-permute-start.11 = (bf16[4,2,2,120,768]{4,3,2,1,0:T(8,128)(2,1)}, bf16[4,2,2,120,768]{4,3,2,1,0:T(8,128)(2,1)}, u32[]{:S(2)}, u32[]{:S(2)}) collective-permute-start(bf16[4,2,2,120,768]{4,3,2,1,0:T(8,128)(2,1)} %dynamic-slice_bitcast_fusion), channel_id=1, source_target_pairs={{0,8},{8,0},{16,24},{24,16},{1,9},{9,1},{17,25},{25,17},{2,10},{10... | collective-permute-start | bytes 8847368 | tf_op jit(solution)/shard_map/ppermute | solution.py:830
  360.0 30.3 %collective-permute-start.23 = (bf16[4,2,40,768]{3,2,0,1:T(8,128)(2,1)S(1)}, bf16[4,2,40,768]{3,2,0,1:T(8,128)(2,1)S(1)}, u32[]{:S(2)}, u32[]{:S(2)}) collective-permute-start(bf16[4,2,40,768]{3,2,0,1:T(8,128)(2,1)S(1)} %dynamic-slice_bitcast_fusion.5), channel_id=1, source_target_pairs={{0,16},{8,24},{16,0},{24,8},{1,17},{9,25},{17,1},{25,9},{2,18},{10... | collective-permute-start | bytes 1474568 | tf_op jit(solution)/shard_map/ppermute | solution.py:830
  378.7 12.7 %collective-permute-start.24 = (bf16[4,2,40,768]{3,2,0,1:T(8,128)(2,1)S(1)}, bf16[4,2,40,768]{3,2,0,1:T(8,128)(2,1)}, u32[]{:S(2)}, u32[]{:S(2)}) collective-permute-start(bf16[4,2,40,768]{3,2,0,1:T(8,128)(2,1)S(1)} %dynamic-slice_bitcast_fusion.4), channel_id=1, source_target_pairs={{0,1},{1,0},{2,3},{3,2},{4,5},{5,4},{6,7},{7,6},{8,9},{9,8},{10,11... | collective-permute-start | bytes 1474568 | tf_op jit(solution)/shard_map/ppermute | solution.py:830
  393.4 9.2 %collective-permute-start.26 = (bf16[4,40,768]{2,1,0:T(8,128)(2,1)}, bf16[4,40,768]{2,1,0:T(8,128)(2,1)}, u32[]{:S(2)}, u32[]{:S(2)}) collective-permute-start(bf16[4,40,768]{2,1,0:T(8,128)(2,1)} %dynamic-slice_bitcast_fusion.8), channel_id=1, source_target_pairs={{0,16},{8,24},{16,0},{24,8},{1,17},{9,25},{17,1},{25,9},{2,18},{10... | collective-permute-start | bytes 737288 | tf_op jit(solution)/shard_map/ppermute | solution.py:830
  398.3 26.0 %collective-permute-start.12 = (bf16[4,2,56,768]{3,2,1,0:T(8,128)(2,1)}, bf16[4,2,56,768]{3,2,1,0:T(8,128)(2,1)}, u32[]{:S(2)}, u32[]{:S(2)}) collective-permute-start(bf16[4,2,56,768]{3,2,1,0:T(8,128)(2,1)} %dynamic-slice_bitcast_fusion.3), channel_id=1, source_target_pairs={{0,16},{8,24},{16,0},{24,8},{1,17},{9,25},{17,1},{25,9},{2,18},{10... | collective-permute-start | bytes 2064392 | tf_op jit(solution)/shard_map/ppermute | solution.py:830
  400.4 25.4 %collective-permute-start.13 = (bf16[4,2,64,768]{3,2,1,0:T(8,128)(2,1)}, bf16[4,2,64,768]{3,2,1,0:T(8,128)(2,1)}, u32[]{:S(2)}, u32[]{:S(2)}) collective-permute-start(bf16[4,2,64,768]{3,2,1,0:T(8,128)(2,1)} %dynamic-slice_bitcast_fusion.2), channel_id=1, source_target_pairs={{0,1},{1,0},{2,3},{3,2},{4,5},{5,4},{6,7},{7,6},{8,9},{9,8},{10,11... | collective-permute-start | bytes 2359304 | tf_op jit(solution)/shard_map/ppermute | solution.py:830
  401.7 21.7 %collective-permute-start.25 = (bf16[4,40,768]{2,1,0:T(8,128)(2,1)}, bf16[4,40,768]{2,1,0:T(8,128)(2,1)}, u32[]{:S(2)}, u32[]{:S(2)}) collective-permute-start(bf16[4,40,768]{2,1,0:T(8,128)(2,1)} %dynamic-slice_bitcast_fusion.9), channel_id=1, source_target_pairs={{0,1},{1,0},{2,3},{3,2},{4,5},{5,4},{6,7},{7,6},{8,9},{9,8},{10,11... | collective-permute-start | bytes 737288 | tf_op jit(solution)/shard_map/ppermute | solution.py:830
  427.8 7.8 %collective-permute-start.15 = (bf16[4,64,768]{2,1,0:T(8,128)(2,1)S(1)}, bf16[4,64,768]{2,1,0:T(8,128)(2,1)S(1)}, u32[]{:S(2)}, u32[]{:S(2)}) collective-permute-start(bf16[4,64,768]{2,1,0:T(8,128)(2,1)S(1)} %dynamic-slice_bitcast_fusion.6), channel_id=1, source_target_pairs={{0,16},{8,24},{16,0},{24,8},{1,17},{9,25},{17,1},{25,9},{2,18},{10... | collective-permute-start | bytes 1179656 | tf_op jit(solution)/shard_map/ppermute | solution.py:830
  428.7 23.6 %collective-permute-start.27 = (bf16[40,768]{1,0:T(8,128)(2,1)S(1)}, bf16[40,768]{1,0:T(8,128)(2,1)S(1)}, u32[]{:S(2)}, u32[]{:S(2)}) collective-permute-start(bf16[40,768]{1,0:T(8,128)(2,1)S(1)} %get-tuple-element.161), channel_id=1, source_target_pairs={{0,2},{1,3},{2,4},{3,5},{4,6},{5,7},{6,0},{7,1},{8,10},{9,11},{10,... | collective-permute-start | bytes 184328 | tf_op jit(solution)/shard_map/ppermute | solution.py:835
  429.5 26.0 %collective-permute-start.29 = (bf16[40,768]{1,0:T(8,128)(2,1)S(1)}, bf16[40,768]{1,0:T(8,128)(2,1)S(1)}, u32[]{:S(2)}, u32[]{:S(2)}) collective-permute-start(bf16[40,768]{1,0:T(8,128)(2,1)S(1)} %get-tuple-element.162), channel_id=1, source_target_pairs={{0,6},{1,7},{2,0},{3,1},{4,2},{5,3},{6,4},{7,5},{8,14},{9,15},{10,... | collective-permute-start | bytes 184328 | tf_op jit(solution)/shard_map/ppermute | solution.py:835
  442.2 10.1 %collective-permute-start.20 = (bf16[64,768]{1,0:T(8,128)(2,1)S(1)}, bf16[64,768]{1,0:T(8,128)(2,1)S(1)}, u32[]{:S(2)}, u32[]{:S(2)}) collective-permute-start(bf16[64,768]{1,0:T(8,128)(2,1)S(1)} %get-tuple-element.154), channel_id=1, source_target_pairs={{0,4},{1,5},{2,6},{3,7},{4,0},{5,1},{6,2},{7,3},{8,12},{9,13},{10,... | collective-permute-start | bytes 294920 | tf_op jit(solution)/shard_map/ppermute | solution.py:835
  445.6 9.9 %collective-permute-start.28 = (bf16[40,768]{1,0:T(8,128)(2,1)S(1)}, bf16[40,768]{1,0:T(8,128)(2,1)S(1)}, u32[]{:S(2)}, u32[]{:S(2)}) collective-permute-start(bf16[40,768]{1,0:T(8,128)(2,1)S(1)} %get-tuple-element.163), channel_id=1, source_target_pairs={{0,4},{1,5},{2,6},{3,7},{4,0},{5,1},{6,2},{7,3},{8,12},{9,13},{10,... | collective-permute-start | bytes 184328 | tf_op jit(solution)/shard_map/ppermute | solution.py:835
  446.9 9.6 %collective-permute-start.30 = (bf16[40,768]{1,0:T(8,128)(2,1)S(1)}, bf16[40,768]{1,0:T(8,128)(2,1)S(1)}, u32[]{:S(2)}, u32[]{:S(2)}) collective-permute-start(bf16[40,768]{1,0:T(8,128)(2,1)S(1)} %get-tuple-element.158), channel_id=1, source_target_pairs={{0,2},{1,3},{2,4},{3,5},{4,6},{5,7},{6,0},{7,1},{8,10},{9,11},{10,... | collective-permute-start | bytes 184328 | tf_op jit(solution)/shard_map/ppermute | solution.py:835
  459.7 8.9 %collective-permute-start.33 = (bf16[392,768]{1,0:T(8,128)(2,1)S(1)}, bf16[392,768]{1,0:T(8,128)(2,1)S(1)}, u32[]{:S(2)}, u32[]{:S(2)}) collective-permute-start(bf16[392,768]{1,0:T(8,128)(2,1)S(1)} %fusion.26), channel_id=1, source_target_pairs={{0,16},{8,24},{16,0},{24,8},{1,17},{9,25},{17,1},{25,9},{2,18},{10... | collective-permute-start | bytes 1806344 | tf_op jit(solution)/shard_map/ppermute | solution.py:830
  469.9 40.6 %collective-permute-start.34 = (bf16[2,392,768]{2,1,0:T(8,128)(2,1)}, bf16[2,392,768]{2,1,0:T(8,128)(2,1)S(1)}, u32[]{:S(2)}, u32[]{:S(2)}) collective-permute-start(bf16[2,392,768]{2,1,0:T(8,128)(2,1)} %pad_maximum_fusion.2), channel_id=1, source_target_pairs={{0,8},{8,0},{16,24},{24,16},{1,9},{9,1},{17,25},{25,17},{2,10},{10... | collective-permute-start | bytes 3612680 | tf_op jit(solution)/shard_map/ppermute | solution.py:830
  (38 other events, 230.6 us)
Sparse Core Ops, SparseCore 0:
  11.6 67.4 all-gather.4
  82.7 86.1 all-gather.6
  232.7 134.1 reduce-scatter.1

commit v2 on v1

v2 whole, which is shorter than its diff:
```python
import functools
import math
import jax
import jax.numpy as jnp
from jax import lax
from jax.sharding import PartitionSpec as P
from jax.experimental import pallas as pl
from jax.experimental.pallas import tpu as pltpu

HEAD = 64
PAIR = 2 * HEAD
BLOCK = 256
very_low = -1e30
VMEM_LIMIT = 60 * 2**20
f32 = jnp.float32
bf16 = jnp.bfloat16


def dot_nt(left, right):
    return lax.dot_general(left, right, (((1,), (1,)), ((), ())), preferred_element_type=f32)


def dot_nn(left, right):
    return lax.dot_general(left, right, (((1,), (0,)), ((), ())), preferred_element_type=f32)


def dot_tn(left, right):
    return lax.dot_general(left, right, (((0,), (0,)), ((), ())), preferred_element_type=f32)


def split_pair(pair):
    lane = lax.broadcasted_iota(jnp.int32, pair.shape, 1)
    none = jnp.zeros_like(pair)
    return (jnp.where(lane < HEAD, pair, none), jnp.where(lane < HEAD, none, pair))


def mask_tail(scores, valid):
    width = scores.shape[0]
    if width == BLOCK:
        return jnp.where(valid, scores, very_low)
    return jnp.concatenate(
        [scores[: width - BLOCK], jnp.where(valid, scores[width - BLOCK :], very_low)], 0
    )


def stacked(pair):
    return jnp.concatenate(split_pair(pair), 0)


def score_tile(queries, keys, valid):
    return mask_tail(dot_nt(keys, stacked(queries)), valid)


def attend_tile(scores, values):
    count = scores.shape[1] // 2
    values_t = values.T
    highest = jnp.max(scores, 0, keepdims=True)
    raised = jnp.exp(scores - highest)
    summed = jnp.sum(raised, 0, keepdims=True)
    raised = raised.astype(bf16)
    context = jnp.concatenate(
        [
            dot_nn(values_t[half * HEAD : (half + 1) * HEAD], raised[:, half * count : (half + 1) * count])
            / summed[:, half * count : (half + 1) * count]
            for half in range(2)
        ],
        0,
    )
    return context.T.astype(bf16), highest + jnp.log(summed)


def head_sums(pair):
    turned = pair.T
    return jnp.concatenate(
        [jnp.sum(turned[half * HEAD : (half + 1) * HEAD], 0, keepdims=True) for half in range(2)], 1
    )


def back_tile(scores, queries, keys, values, grads, contexts, logsum):
    count = scores.shape[1] // 2
    grad_rows = stacked(grads)
    grad_shares = dot_nt(values, grad_rows)
    inner = head_sums(grads.astype(f32) * contexts.astype(f32))
    keys_t = keys.T
    shares = jnp.exp(scores - logsum)
    grad_scores = (shares * (grad_shares - inner)).astype(bf16)
    grad_values = dot_nn(shares.astype(bf16), grad_rows)
    grad_keys = dot_nn(grad_scores, stacked(queries))
    grad_queries = jnp.concatenate(
        [
            dot_nn(keys_t[half * HEAD : (half + 1) * HEAD], grad_scores[:, half * count : (half + 1) * count])
            for half in range(2)
        ],
        0,
    ).T
    grad_queries = (grad_queries.astype(bf16).astype(f32) * HEAD**-0.5).astype(bf16)
    return grad_queries, grad_keys, grad_values


def causal(columns):
    key = lax.broadcasted_iota(jnp.int32, (BLOCK, columns), 0)
    query = lax.broadcasted_iota(jnp.int32, (BLOCK, columns), 1) % BLOCK
    return key <= query


def key_spans(tokens, whole):
    return [
        (0 if whole else low, low, low + BLOCK) for low in range(0, tokens, BLOCK)
    ]


def self_kernel(skip, info, q_ref, k_ref, v_ref, o_ref, stat_ref):
    tokens = q_ref.shape[0]
    valid = causal(2 * BLOCK)

    def run(whole):
        spans = key_spans(tokens, whole)
        score = lambda span: score_tile(q_ref[span[1] : span[2], :], k_ref[span[0] : span[2], :], valid)
        ahead = score(spans[0])
        for part, (low, start, stop) in enumerate(spans):
            scores = ahead
            if part + 1 < len(spans):
                ahead = score(spans[part + 1])
            o_ref[start:stop, :], stat_ref[0, part] = attend_tile(scores, v_ref[low:stop, :])

    pl.when(info[0] == 1)(functools.partial(run, False))
    pl.when(info[0] != 1)(functools.partial(run, True))


def self_back_kernel(skip, info, q_ref, k_ref, v_ref, g_ref, o_ref, stat_ref, *refs):
    dq_ref, dk_ref, dv_ref, key_sum, value_sum = refs[skip:]
    tokens = q_ref.shape[0]
    valid = causal(2 * BLOCK)

    def run(whole):
        spans = key_spans(tokens, whole)[::-1]
        score = lambda span: score_tile(q_ref[span[1] : span[2], :], k_ref[span[0] : span[2], :], valid)
        ahead = score(spans[0])
        for step, (low, start, stop) in enumerate(spans):
            scores = ahead
            if step + 1 < len(spans):
                ahead = score(spans[step + 1])
            dq_ref[start:stop, :], grad_keys, grad_values = back_tile(
                scores,
                q_ref[start:stop, :],
                k_ref[low:stop, :],
                v_ref[low:stop, :],
                g_ref[start:stop, :],
                o_ref[start:stop, :],
                stat_ref[0, start // BLOCK],
            )
            if not whole:
                dk_ref[start:stop, :] = grad_keys.astype(bf16)
                dv_ref[start:stop, :] = grad_values.astype(bf16)
            elif stop == tokens:
                key_sum[...] = grad_keys
                value_sum[...] = grad_values
            else:
                key_sum[:stop, :] += grad_keys
                value_sum[:stop, :] += grad_values
        if whole:
            dk_ref[...] = key_sum[...].astype(bf16)
            dv_ref[...] = value_sum[...].astype(bf16)

    pl.when(info[0] == 1)(functools.partial(run, False))
    pl.when(info[0] != 1)(functools.partial(run, True))


def by_length(info, row, mem_len, run):
    length = info[1 + row]
    for width in range(BLOCK, mem_len + 1, BLOCK):

        @pl.when((length > width - BLOCK) & (length <= width))
        def _(width=width):
            run(width, lambda columns: lax.broadcasted_iota(jnp.int32, (BLOCK, columns), 0) < length - (width - BLOCK))


def cross_kernel(skip, info, q_ref, k_ref, v_ref, o_ref, stat_ref):
    tokens = q_ref.shape[0]
    count, mem_len, _ = k_ref.shape
    parts = tokens // BLOCK

    @pl.when(info[0] == 1)
    def _():
        def step(row, none):
            rows = pl.ds(pl.multiple_of(row * BLOCK, BLOCK), BLOCK)

            def run(width, valid):
                scores = score_tile(q_ref[rows, :], k_ref[row, :width, :], valid(2 * BLOCK))
                o_ref[rows, :], stat_ref[0, row] = attend_tile(scores, v_ref[row, :width, :])

            by_length(info, row, mem_len, run)
            return none

        lax.fori_loop(0, count, step, None)

    @pl.when(info[0] != 1)
    def _():
        def run(width, valid):
            scores = score_tile(q_ref[...], k_ref[0, :width, :], valid(2 * tokens))
            o_ref[...], stats = attend_tile(scores, v_ref[0, :width, :])
            for part in range(parts):
                low = part * BLOCK
                stat_ref[0, part] = jnp.concatenate(
                    [stats[:, low : low + BLOCK], stats[:, tokens + low : tokens + low + BLOCK]], 1
                )

        by_length(info, 0, mem_len, run)


def cross_back_kernel(skip, info, q_ref, k_ref, v_ref, g_ref, o_ref, stat_ref, *refs):
    dq_ref, dk_ref, dv_ref = refs[skip:]
    tokens = q_ref.shape[0]
    count, mem_len, _ = k_ref.shape
    parts = tokens // BLOCK

    def store(row, width, grad_keys, grad_values):
        dk_ref[row, :width, :] = grad_keys.astype(bf16)
        dv_ref[row, :width, :] = grad_values.astype(bf16)
        if width < mem_len:
            rest = jnp.zeros((mem_len - width, PAIR), bf16)
            dk_ref[row, width:, :] = rest
            dv_ref[row, width:, :] = rest

    @pl.when(info[0] == 1)
    def _():
        def step(row, none):
            rows = pl.ds(pl.multiple_of(row * BLOCK, BLOCK), BLOCK)

            def run(width, valid):
                keys = k_ref[row, :width, :]
                scores = score_tile(q_ref[rows, :], keys, valid(2 * BLOCK))
                dq_ref[rows, :], grad_keys, grad_values = back_tile(
                    scores, q_ref[rows, :], keys, v_ref[row, :width, :], g_ref[rows, :], o_ref[rows, :],
                    stat_ref[0, row],
                )
                store(row, width, grad_keys, grad_values)

            by_length(info, row, mem_len, run)
            return none

        lax.fori_loop(0, count, step, None)

    @pl.when(info[0] != 1)
    def _():
        def run(width, valid):
            keys = k_ref[0, :width, :]
            scores = score_tile(q_ref[...], keys, valid(2 * tokens))
            stats = jnp.concatenate(
                [stat_ref[0, part][:, half * BLOCK : (half + 1) * BLOCK] for half in range(2) for part in range(parts)],
                1,
            )
            dq_ref[...], grad_keys, grad_values = back_tile(
                scores, q_ref[...], keys, v_ref[0, :width, :], g_ref[...], o_ref[...], stats
            )
            store(0, width, grad_keys, grad_values)

        by_length(info, 0, mem_len, run)


def params():
    return pltpu.CompilerParams(vmem_limit_bytes=VMEM_LIMIT)


def cost(matmuls, moved=2**23):
    flops = 2 * sum(math.prod(sizes) for sizes in matmuls)
    return pl.CostEstimate(flops=flops, bytes_accessed=moved, transcendentals=0)


def attend_call(kernel, name, info, queries, keys, values, rest=None, first=0, count=None, start=()):
    tokens, width = queries.shape
    pairs = width // PAIR
    count = count or pairs
    parts = tokens // BLOCK
    back = rest is not None
    own = pl.BlockSpec((tokens, PAIR), lambda pair, info: (0, pair + first))
    stat = pl.BlockSpec((1, parts, 1, 2 * BLOCK), lambda pair, info: (pair + first, 0, 0, 0))
    if keys.ndim == 2:
        other = own
        scratch = [pltpu.VMEM((tokens, PAIR), f32)] * 2 if back else []
    else:
        other = pl.BlockSpec(keys.shape[:2] + (PAIR,), lambda pair, info: (0, 0, pair + first))
        scratch = []
    queries_shape = jax.ShapeDtypeStruct((tokens, width), bf16)
    keys_shape = jax.ShapeDtypeStruct(keys.shape, bf16)
    stat_shape = jax.ShapeDtypeStruct((pairs, parts, 1, 2 * BLOCK), f32)
    inputs = (queries, keys, values) + (rest or ())
    return pl.pallas_call(
        functools.partial(kernel, len(start)),
        grid_spec=pltpu.PrefetchScalarGridSpec(
            num_scalar_prefetch=1,
            grid=(count,),
            in_specs=[own, other, other]
            + ([own, own, stat] if back else [])
            + [pl.BlockSpec(memory_space=pl.ANY)] * len(start),
            out_specs=[own, other, other] if back else [own, stat],
            scratch_shapes=scratch,
        ),
        out_shape=[queries_shape, keys_shape, keys_shape] if back else [queries_shape, stat_shape],
        input_output_aliases={1 + len(inputs) + place: place for place in range(len(start))},
        compiler_params=params(),
        name=name,
        cost_estimate=cost([(tokens, tokens, width)] * (24 if back else 12)),
    )(info, *inputs, *start)


def self_attend(info, queries, keys, values):
    return attend_call(self_kernel, "self_attend", info, queries, keys, values)


def cross_attend(info, queries, keys, values):
    return attend_call(cross_kernel, "cross_attend", info, queries, keys, values)


def self_attend_back(info, queries, keys, values, *rest, **span):
    return attend_call(self_back_kernel, "self_attend_back", info, queries, keys, values, rest, **span)


def cross_attend_back(info, queries, keys, values, *rest, **span):
    return attend_call(cross_back_kernel, "cross_attend_back", info, queries, keys, values, rest, **span)


epsilon = 1e-05
VECTORS = 32


def normalise(total):
    middle = jnp.mean(total, -1, keepdims=True)
    centred = total - middle
    variance = jnp.mean(centred * centred, -1, keepdims=True)
    scale = lax.rsqrt(variance + epsilon)
    return centred * scale, scale


def normalise_back(grad, gain, normal, scale):
    scaled = grad * gain
    first = jnp.mean(scaled, -1, keepdims=True)
    second = jnp.mean(scaled * normal, -1, keepdims=True)
    return (scaled - first - normal * second) * scale


def add_rows(ref, row, value):
    ref[row : row + 1, :] += jnp.sum(value, 0, keepdims=True)


def start_sums(*refs):
    @pl.when(pl.program_id(0) == 0)
    def _():
        for ref in refs:
            ref[...] = jnp.zeros_like(ref)


def full(array):
    return pl.BlockSpec(memory_space=pltpu.VMEM)


def row_block(rows, width):
    return pl.BlockSpec((rows, width), lambda part, *info: (part, 0))


def keep_block(rows, width):
    return pl.BlockSpec((rows, width), lambda part, *info: (0, 0))


def unit(ref, high=0):
    return ref[:, high].reshape(ref.shape[0] * ref.shape[2], ref.shape[3])


def by_core(info, mine, got, run):
    core = info[info.shape[0] - 1]
    pl.when(core == 0)(lambda: run(mine, got))
    pl.when(core != 0)(lambda: run(got, mine))


def unit_block(array, high):
    return pl.BlockSpec(
        array.shape[:1] + (1,) + array.shape[2:],
        lambda *place: (0, high, 0, 0),
        pipeline_mode=pl.Buffered(1),
    )


def first_kernel(info, x_ref, c_ref, mine, got, vec_ref, z_ref, low_ref, q_ref):
    def run(even, odd):
        total = x_ref[...].astype(f32) + dot_nn(c_ref[...], unit(even)) + vec_ref[2 : 3, :]
        normal, _ = normalise(total)
        first_low = (normal * vec_ref[32 : 33, :] + vec_ref[40 : 41, :]).astype(bf16)
        z_ref[...] = total
        low_ref[...] = first_low
        q_ref[...] = ((dot_nn(first_low, unit(odd)) + vec_ref[8 : 9, :]) * HEAD**-0.5).astype(bf16)

    by_core(info, mine, got, run)


def row_call(kernel, name, info, grid, in_specs, out_specs, out_shape, matmuls, inputs, scratch=(), aliases=None):
    return pl.pallas_call(
        kernel,
        grid_spec=pltpu.PrefetchScalarGridSpec(
            num_scalar_prefetch=1,
            grid=grid,
            in_specs=in_specs,
            out_specs=out_specs,
            scratch_shapes=scratch,
        ),
        out_shape=out_shape,
        input_output_aliases=aliases or {},
        compiler_params=params(),
        name=name,
        cost_estimate=cost(matmuls),
    )(info, *inputs)


def first_norm(info, x, context, mid, vectors, rows=256):
    tokens, width = x.shape
    block = row_block(rows, width)
    low = jax.ShapeDtypeStruct((tokens, width), bf16)
    return row_call(
        first_kernel, "first_norm", info, (tokens // rows,),
        [block, block, unit_block(mid[0], 0), unit_block(mid[1], 0), full(vectors)],
        [block] * 3, [jax.ShapeDtypeStruct((tokens, width), f32), low, low],
        [(tokens, width, width)] * 4, (x, context, *mid, vectors),
    )


def chunks(blocks, pieces, block):
    return [divmod(number, blocks) for number in range(block * pieces, (block + 1) * pieces)]


def ffn_kernel(
    info,
    z_ref,
    c_ref,
    cot_ref,
    mine,
    got,
    tail_ref,
    vec_ref,
    out_ref,
    low_ref,
    act_ref,
    du_ref,
    df_ref,
    do_ref,
    dz_ref,
    dc_ref,
    sum_ref,
    wide_ref,
    slope_ref,
    out_w,
):
    start_sums(sum_ref, wide_ref)

    @pl.when(pl.program_id(0) == 0)
    def _():
        def load(even, odd):
            out_w[...] = unit(odd)

        by_core(info, mine, got, load)

    width = z_ref.shape[1]
    blocks, pieces, both = tail_ref.shape[:3]
    in_w = lambda block: tail_ref[block, :, : both // 2].reshape(width, width)
    ffn_w = lambda block: jnp.concatenate(
        [tail_ref[d, f, both // 2 :, :] for f, d in chunks(blocks, pieces, block)], 0
    )
    gain_first, gain_mid, gain_last = [vec_ref[row : row + 1, :] for row in (32, 33, 34)]
    shift_first, shift_mid, shift_last = [vec_ref[row : row + 1, :] for row in (40, 41, 42)]
    normal_first, _ = normalise(z_ref[...])
    first = normal_first * gain_first + shift_first
    normal_mid, scale_mid = normalise(first + dot_nn(c_ref[...], out_w[...]) + vec_ref[10 : 11, :])
    second = normal_mid * gain_mid + shift_mid
    second_low = second.astype(bf16)
    low_ref[...] = second_low
    total = second + vec_ref[24 : 25, :]
    ahead = dot_nn(second_low, in_w(0))
    for block in range(blocks):
        cols = pl.ds(block * width, width)
        value = ahead + vec_ref[16 + block : 17 + block, :]
        if block + 1 < blocks:
            ahead = dot_nn(second_low, in_w(block + 1))
        share = 0.5 * (1.0 + lax.erf(value * 0.5**0.5))
        density = jnp.exp(-0.5 * value * value) * 0.3989422804014327
        active = (value * share).astype(bf16)
        slope_ref[:, cols] = share + value * density
        act_ref[:, cols] = active
        total = total + dot_nn(active, ffn_w(block))
    normal_last, scale_last = normalise(total)
    out_ref[...] = (normal_last * gain_last + shift_last).astype(bf16)
    cot = cot_ref[...].astype(f32)
    add_rows(sum_ref, 0, cot * normal_last)
    add_rows(sum_ref, 1, cot)
    grad_last = normalise_back(cot, gain_last, normal_last, scale_last)
    grad_low = grad_last.astype(bf16)
    df_ref[...] = grad_low
    add_rows(sum_ref, 2, grad_low.astype(f32))
    grad_second = grad_last
    ahead = dot_nt(grad_low, ffn_w(0))
    for block in range(blocks):
        cols = pl.ds(block * width, width)
        grad_hidden = (ahead * slope_ref[:, cols]).astype(bf16)
        if block + 1 < blocks:
            ahead = dot_nt(grad_low, ffn_w(block + 1))
        du_ref[:, cols] = grad_hidden
        wide_ref[:, cols] += jnp.sum(grad_hidden.astype(f32), 0, keepdims=True)
        grad_second = grad_second + dot_nt(grad_hidden, in_w(block))
    add_rows(sum_ref, 3, grad_second * normal_mid)
    add_rows(sum_ref, 4, grad_second)
    grad_mid = normalise_back(grad_second, gain_mid, normal_mid, scale_mid)
    dz_ref[...] = grad_mid
    grad_low = grad_mid.astype(bf16)
    do_ref[...] = grad_low
    add_rows(sum_ref, 5, grad_low.astype(f32))
    dc_ref[...] = dot_nt(grad_low, out_w[...]).astype(bf16)


def ffn_block(info, z, context, cotangent, head, tail, vectors, rows=256):
    tokens, width = z.shape
    hidden = tail.shape[0] * width
    block = row_block(rows, width)
    wide = row_block(rows, hidden)
    narrow_shape = jax.ShapeDtypeStruct((tokens, width), bf16)
    wide_shape = jax.ShapeDtypeStruct((tokens, hidden), bf16)
    return row_call(
        ffn_kernel, "ffn_block", info, (tokens // rows,),
        [block] * 3 + [unit_block(head[0], 1), unit_block(head[1], 1), full(tail), full(vectors)],
        [block, block, wide, wide, block, block, block, block, keep_block(8, width), keep_block(1, hidden)],
        [
            narrow_shape, narrow_shape, wide_shape, wide_shape, narrow_shape, narrow_shape,
            jax.ShapeDtypeStruct((tokens, width), f32), narrow_shape,
            jax.ShapeDtypeStruct((8, width), f32), jax.ShapeDtypeStruct((1, hidden), f32),
        ],
        [(tokens, width, hidden)] * 8, (z, context, cotangent, *head, tail, vectors),
        [pltpu.VMEM((rows, hidden), f32), pltpu.VMEM((width, width), bf16)],
    )


def first_back_kernel(info, dz2_ref, dq_ref, z_ref, mine, got, vec_ref, dz_ref, do_ref, dc_ref, sum_ref):
    start_sums(sum_ref)

    def run(even, odd):
        grad_query = dq_ref[...]
        grad_first = dz2_ref[...] + dot_nt(grad_query, unit(odd))
        normal, scale = normalise(z_ref[...])
        add_rows(sum_ref, 0, grad_first * normal)
        add_rows(sum_ref, 1, grad_first)
        grad_start = normalise_back(grad_first, vec_ref[32 : 33, :], normal, scale)
        dz_ref[...] = grad_start
        grad_low = grad_start.astype(bf16)
        do_ref[...] = grad_low
        add_rows(sum_ref, 2, grad_low.astype(f32))
        add_rows(sum_ref, 3, grad_query.astype(f32))
        dc_ref[...] = dot_nt(grad_low, unit(even)).astype(bf16)

    by_core(info, mine, got, run)


def first_back(info, dz2, grad_query, z, mid, vectors, rows=256):
    tokens, width = z.shape
    block = row_block(rows, width)
    low = jax.ShapeDtypeStruct((tokens, width), bf16)
    return row_call(
        first_back_kernel, "first_back", info, (tokens // rows,),
        [block] * 3 + [unit_block(mid[0], 0), unit_block(mid[1], 0), full(vectors)],
        [block] * 3 + [keep_block(8, width)],
        [jax.ShapeDtypeStruct((tokens, width), f32), low, low, jax.ShapeDtypeStruct((8, width), f32)],
        [(tokens, width, width)] * 4, (dz2, grad_query, z, *mid, vectors),
    )


def needed(info, row, part, rows):
    return ((info[0] == 1) | (row == 0)) & (part * rows < info[1 + row])


def needed_place(info, row, part, rows):
    used = jnp.where(info[0] == 1, row, 0)
    last = (info[1 + used] + rows - 1) // rows - 1
    return used, jnp.where(info[0] == 1, jnp.minimum(part, last), jnp.where(row == 0, jnp.minimum(part, last), last))


def project_kernel(rows, info, m_ref, mine, got, b_ref, k_ref, v_ref):
    @pl.when(needed(info, pl.program_id(0), pl.program_id(1), rows))
    def _():
        def run(even, odd):
            memory = m_ref[0]
            k_ref[0] = dot_nn(memory, unit(even)).astype(bf16)
            v_ref[0] = (dot_nn(memory, unit(odd)) + b_ref[9 : 10, :]).astype(bf16)

        by_core(info, mine, got, run)


def memory_block(rows, width, first=0):
    return pl.BlockSpec(
        (1, rows, width), lambda row, part, info: needed_place(info, row + first, part, rows) + (0,)
    )


def project_memory(info, memory, mid, vectors, rows=512):
    count, length, width = memory.shape
    block = memory_block(rows, width)
    return row_call(
        functools.partial(project_kernel, rows), "project_memory", info, (count, length // rows),
        [block, unit_block(mid[0], 1), unit_block(mid[1], 1), full(vectors)], [block] * 2,
        [jax.ShapeDtypeStruct(memory.shape, bf16)] * 2,
        [(count, length, width, width)] * 2, (memory, *mid, vectors),
    )


def memory_back_kernel(rows, first, info, dk_ref, dv_ref, mine, got, *refs):
    out_ref = refs[-1]
    here = needed(info, pl.program_id(0) + first, pl.program_id(1), rows)

    @pl.when(here)
    def _():
        def run(even, odd):
            out_ref[0] = dot_nt(dk_ref[0], unit(even)) + dot_nt(dv_ref[0], unit(odd))

        by_core(info, mine, got, run)

    @pl.when(jnp.logical_not(here))
    def _():
        out_ref[...] = jnp.zeros_like(out_ref)


def memory_back(info, grad_keys, grad_values, mid, first, count, start=(), rows=512):
    length, width = grad_keys.shape[1:]
    block = memory_block(rows, width, first)
    return row_call(
        functools.partial(memory_back_kernel, rows, first), "memory_back", info, (count, length // rows),
        [block, block, unit_block(mid[0], 1), unit_block(mid[1], 1)]
        + [pl.BlockSpec(memory_space=pl.ANY)] * len(start),
        pl.BlockSpec((1, rows, width), lambda row, part, info: (row + first, part, 0)),
        jax.ShapeDtypeStruct(grad_keys.shape, f32),
        [(count, length, width, width)] * 2, (grad_keys, grad_values, *mid, *start),
        aliases={5: 0} if start else {},
    )


def unit_copy(info, stage, sent, mine, other, number, act):
    width = stage.shape[1]
    here = info[info.shape[0] - 1] == number % 2
    for ref, chosen in ((mine, here), (other, jnp.logical_not(here))):

        @pl.when(chosen)
        def _(ref=ref):
            rows = ref.at[pl.ds(number // 2 * width, width), :]
            act(pltpu.make_async_copy(stage.at[number], rows, sent.at[number]))


def put_unit(info, stage, sent, mine, other, number, value):
    stage[number] = value.astype(bf16)
    unit_copy(info, stage, sent, mine, other, number, lambda copy: copy.start())


def end_units(info, stage, sent, mine, other):
    for number in range(4):
        unit_copy(info, stage, sent, mine, other, number, lambda copy: copy.wait())


def unit_scratch(width):
    return [pltpu.VMEM((4, width, width), bf16), pltpu.SemaphoreType.DMA((4,))]


def mid_weights_kernel(
    rows, info, m_ref, dk_ref, dv_ref, first_ref, dq_ref, self_ref, dself_ref,
    mine, other, sum_ref, key_sum, value_sum, stage, sent,
):
    row, part = pl.program_id(0), pl.program_id(1)
    out = (info, stage, sent, mine, other)

    @pl.when((row == 0) & (part == 0))
    def _():
        put_unit(*out, 0, dot_tn(self_ref[...], dself_ref[...]))
        put_unit(*out, 1, dot_tn(first_ref[...], dq_ref[...]))
        key_sum[...] = jnp.zeros_like(key_sum)
        value_sum[...] = jnp.zeros_like(value_sum)
        sum_ref[...] = jnp.zeros_like(sum_ref)

    @pl.when(needed(info, row, part, rows))
    def _():
        memory = m_ref[0]
        key_sum[...] += dot_tn(memory, dk_ref[0])
        value_sum[...] += dot_tn(memory, dv_ref[0])
        sum_ref[...] += jnp.sum(dv_ref[0].astype(f32), 0, keepdims=True)

    @pl.when((row == pl.num_programs(0) - 1) & (part == pl.num_programs(1) - 1))
    def _():
        put_unit(*out, 2, key_sum[...])
        put_unit(*out, 3, value_sum[...])
        end_units(*out)


def mid_weights(info, memory, grad_keys, grad_values, pairs):
    count, rows, width = memory.shape
    block = memory_block(rows, width)
    half = jax.ShapeDtypeStruct((2 * width, width), bf16)
    return row_call(
        functools.partial(mid_weights_kernel, rows), "mid_weights", info, (count, 1),
        [block] * 3 + [full(None)] * 4,
        [pl.BlockSpec(memory_space=pl.ANY)] * 2 + [pl.BlockSpec((1, width), lambda row, part, info: (0, 0))],
        [half, half, jax.ShapeDtypeStruct((1, width), f32)],
        [(count, rows, width, width)] * 2, (memory, grad_keys, grad_values, *pairs),
        [pltpu.VMEM((width, width), f32)] * 2 + unit_scratch(width),
    )


def qkv_kernel(info, x_ref, mine, got, vec_ref, q_ref, k_ref, v_ref):
    def run(even, odd):
        x = x_ref[...]
        q_ref[...] = ((dot_nn(x, unit(even, 0)) + vec_ref[0 : 1, :]) * HEAD**-0.5).astype(bf16)
        k_ref[...] = dot_nn(x, unit(odd, 0)).astype(bf16)
        v_ref[...] = (dot_nn(x, unit(even, 1)) + vec_ref[1 : 2, :]).astype(bf16)

    by_core(info, mine, got, run)


def project_self(info, x, head, vectors, rows=512):
    tokens, width = x.shape
    block = row_block(rows, width)
    return row_call(
        qkv_kernel, "project_self", info, (tokens // rows,),
        [block, full(None), full(None), full(None)], [block] * 3,
        [jax.ShapeDtypeStruct((tokens, width), bf16)] * 3,
        [(tokens, width, width)] * 4, (x, *head, vectors),
    )


def target_back_kernel(info, z_ref, q_ref, k_ref, v_ref, mine, got, out_ref):
    def run(even, odd):
        out_ref[...] = (
            z_ref[...]
            + dot_nt(q_ref[...], unit(even, 0))
            + dot_nt(k_ref[...], unit(odd, 0))
            + dot_nt(v_ref[...], unit(even, 1))
        )

    by_core(info, mine, got, run)


def target_back(info, dz, grads, head, rows=256):
    tokens, width = dz.shape
    block = row_block(rows, width)
    return row_call(
        target_back_kernel, "target_back", info, (tokens // rows,),
        [block] * 4 + [full(None)] * 2, block, jax.ShapeDtypeStruct((tokens, width), f32),
        [(tokens, width, width)] * 4, (dz, *grads, *head),
    )


def self_weights_kernel(
    info, x_hbm, q_hbm, k_hbm, v_hbm, cross_hbm, dcross_hbm, first_ref, value_ref, ffn_ref, wide_ref,
    mine, other, held, arrived, stage, sent, vectors, vectors_sent,
):
    sources = (cross_hbm, dcross_hbm, x_hbm, q_hbm, k_hbm, v_hbm)
    copies = [
        pltpu.make_async_copy(source, held.at[place], arrived.at[place])
        for place, source in enumerate(sources)
    ]
    for copy in copies:
        copy.start()
    width = x_hbm.shape[1]
    out = (info, stage, sent, mine, other)
    copies[0].wait()
    copies[1].wait()
    put_unit(*out, 3, dot_tn(held[0], held[1]))
    copies[2].wait()
    sums = []
    for number in range(3):
        copies[3 + number].wait()
        put_unit(*out, number, dot_tn(held[2], held[3 + number]))
        sums.append(jnp.sum(held[3 + number].astype(f32), 0, keepdims=True))
    row = lambda ref, number: ref[number : number + 1, :]
    vectors[...] = jnp.concatenate(
        [sums[0], sums[2], row(first_ref, 2), row(first_ref, 3), value_ref[...], row(ffn_ref, 5)]
        + [wide_ref[:, low : low + width] for low in range(0, wide_ref.shape[1], width)]
        + [
            row(ffn_ref, 2), row(first_ref, 0), row(ffn_ref, 3), row(ffn_ref, 0), row(first_ref, 1),
            row(ffn_ref, 4), row(ffn_ref, 1), jnp.zeros((VECTORS - 17, width), f32),
        ],
        0,
    ).astype(bf16)
    ends = [
        pltpu.make_async_copy(vectors, ref.at[pl.ds(2 * width, VECTORS), :], vectors_sent.at[place])
        for place, ref in enumerate((mine, other))
    ]
    for copy in ends:
        copy.start()
    end_units(*out)
    for copy in ends:
        copy.wait()


def self_weights(info, x, grads, cross, sums):
    tokens, width = x.shape
    half = jax.ShapeDtypeStruct((2 * width + VECTORS, width), bf16)
    return row_call(
        self_weights_kernel, "self_weights", info, (),
        [pl.BlockSpec(memory_space=pl.ANY)] * 6 + [full(None)] * 4, [pl.BlockSpec(memory_space=pl.ANY)] * 2,
        [half, half],
        [(tokens, width, width)] * 4, (x, *grads, *cross, *sums),
        [pltpu.VMEM((6, tokens, width), bf16), pltpu.SemaphoreType.DMA((6,))]
        + unit_scratch(width)
        + [pltpu.VMEM((VECTORS, width), bf16), pltpu.SemaphoreType.DMA((2,))],
    )


def ffn_weights_kernel(h_ref, du_ref, a_ref, df_ref, w_hbm, into, outof, sent):
    part = pl.program_id(0)
    blocks, pieces, rows, width = w_hbm.shape
    half = rows // 2
    owners = pieces // blocks if pieces >= blocks else 1
    slot = part % 2

    def copies(part, slot):
        if pieces >= blocks:
            rows_out = w_hbm.at[:, pl.ds(part * owners, owners), pl.ds(half, half), :]
        else:
            rows_out = w_hbm.at[pl.ds(part, 1), :, pl.ds(half, half), :]
        return (
            pltpu.make_async_copy(into.at[slot], w_hbm.at[part, :, pl.ds(0, half), :], sent.at[slot, 0]),
            pltpu.make_async_copy(outof.at[slot], rows_out, sent.at[slot, 1]),
        )

    @pl.when(part >= 2)
    def _():
        for copy in copies(part - 2, slot):
            copy.wait()

    into[slot] = dot_tn(h_ref[...], du_ref[...]).astype(bf16).reshape(pieces, half, width)
    grad_out = dot_tn(a_ref[...], df_ref[...]).astype(bf16)
    for place in range(pieces):
        piece = grad_out[place * half : (place + 1) * half]
        if pieces >= blocks:
            outof[slot, place % blocks, place // blocks] = piece
        else:
            outof[slot, 0, place] = piece
    for copy in copies(part, slot):
        copy.start()

    @pl.when(part == pl.num_programs(0) - 1)
    def _():
        for copy in copies(part - 1, 1 - slot) + copies(part, slot):
            copy.wait()


def ffn_weights(second_low, grad_hidden, active, grad_out, pieces):
    tokens, width = second_low.shape
    blocks = active.shape[1] // width
    whole = pl.BlockSpec((tokens, width), lambda part: (0, 0), pipeline_mode=pl.Buffered(1))
    part = pl.BlockSpec((tokens, width), lambda part: (0, part))
    shape = (blocks, pieces, 2 * width // pieces, width)
    out_shape = (blocks, pieces // blocks) if pieces >= blocks else (1, pieces)
    return pl.pallas_call(
        ffn_weights_kernel,
        grid=(blocks,),
        in_specs=[whole, part, part, whole],
        out_specs=pl.BlockSpec(memory_space=pl.ANY),
        out_shape=jax.ShapeDtypeStruct(shape, bf16),
        scratch_shapes=[
            pltpu.VMEM((2, pieces, width // pieces, width), bf16),
            pltpu.VMEM((2,) + out_shape + (width // pieces, width), bf16),
            pltpu.SemaphoreType.DMA((2, 2)),
        ],
        compiler_params=params(),
        name="ffn_weights",
        cost_estimate=cost([(tokens, width, blocks * width)] * 2),
    )(second_low, grad_hidden, active, grad_out)


def wide(array):
    return array.astype(f32)


def weight_grad(left, right):
    return dot_tn(left, right).astype(bf16)


def forward(
    target, memory, cotangent, info, pieces, head, mid, tail, vectors,
    mid_step=lambda *same: same, mid_last=lambda *same: same,
):
    queries, keys, values = project_self(info, target, head, vectors)
    queries, mid = mid_step(queries, mid)
    context_self, stats_self = self_attend(info, queries, keys, values)
    context_self, mid = mid_last(context_self, mid)
    total_first, first_low, query_cross = first_norm(info, target, context_self, mid, vectors)
    key_cross, value_cross = project_memory(info, memory, mid, vectors)
    context_cross, stats_cross = cross_attend(info, query_cross, key_cross, value_cross)
    output, second_low, active, du, df, do_cross, dz2, dc_cross, sums_ffn, sums_wide = ffn_block(
        info, total_first, context_cross, cotangent, head, tail, vectors
    )
    grad_ffn = ffn_weights(second_low, du, active, df, pieces)
    dq_cross, dk_cross, dv_cross = cross_attend_back(
        info, query_cross, key_cross, value_cross, dc_cross, context_cross, stats_cross
    )
    dz1, do_self, dc_self, sums_first = first_back(info, dz2, dq_cross, total_first, mid, vectors)
    *grad_mid, sum_value = mid_weights(
        info, memory, dk_cross, dv_cross, (first_low, dq_cross, context_self, do_self)
    )
    self_inputs = (queries, keys, values, dc_self, context_self, stats_self)
    cross = (context_cross, do_cross)
    sums = (sums_first, sum_value, sums_ffn, sums_wide)
    return output, grad_ffn, grad_mid, dz1, self_inputs, dk_cross, dv_cross, cross, sums, mid


def forward_back(target, memory, cotangent, info, pieces, head, mid, tail, vectors):
    output, grad_ffn, grad_mid, dz1, self_inputs, dk_cross, dv_cross, cross, sums, mid = forward(
        target, memory, cotangent, info, pieces, head, mid, tail, vectors
    )
    grads = self_attend_back(info, *self_inputs)
    grad_self = self_weights(info, target, grads, cross, sums)
    target_grad = target_back(info, dz1, grads, head)
    memory_grad = memory_back(info, dk_cross, dv_cross, mid, 0, memory.shape[0])
    return (output, target_grad, memory_grad), grad_ffn, grad_mid, grad_self


def pair_swap(array, axis, bit):
    count = lax.axis_size(axis)
    return lax.ppermute(array, axis, [(place, place ^ bit) for place in range(count)])


def ring(array, axis, shift):
    count = lax.axis_size(axis)
    return lax.ppermute(array, axis, [(place, (place + shift) % count) for place in range(count)])


def pick(array, axis, index):
    return lax.dynamic_index_in_dim(array, index, axis, keepdims=False)


def places():
    dp, fsdp = lax.axis_index("dp"), lax.axis_index("fsdp")
    return dp // 2, dp % 2, fsdp // 2, fsdp % 2


def add_half(array, axis, mine, mesh_axis, bit):
    got = pair_swap(pick(array, axis, 1 - mine), mesh_axis, bit)
    return (wide(pick(array, axis, mine)) + wide(got)).astype(bf16)


def add_depth(array, depth):
    total = wide(pick(array, 0, depth))
    for step in (1, 2, 3):
        total = total + wide(ring(pick(array, 0, (depth + step) % 4), "fsdp", 2 * step))
    return total.astype(bf16)


def fence(*arrays):
    return lax.optimization_barrier(arrays)


def add(mine, got):
    return (wide(mine) + wide(got)).astype(bf16)


def cut(array):
    half = array.shape[-2] // 2 // 8 * 8
    return array[..., :half, :], array[..., half:, :]


def join_pair(array, axis, mine, mesh_axis, bit):
    return join(array, pair_swap(array, mesh_axis, bit), axis, mine)


def join(array, got, axis, mine):
    first = jnp.where(mine == 0, array, got)
    second = jnp.where(mine == 0, got, array)
    return jnp.stack([first, second], axis)


def share_dp(array):
    high, core, _, _ = places()
    both = join_pair(array, 0, high, "dp", 2)
    return join_pair(both, 1, core, "dp", 1).reshape((4,) + array.shape)


def join_depth(array, depth):
    parts = [array] + [ring(array, "fsdp", 2 * step) for step in (1, 2, 3)]
    out = jnp.zeros((4,) + array.shape, array.dtype)
    for step, part in enumerate(parts):
        out = lax.dynamic_update_index_in_dim(out, part, (depth - step) % 4, 0)
    return out


def lay_vectors(items, width):
    rows = [jnp.pad(item, ((0, 8 - item.shape[0]), (0, 0))) for item in items]
    row = jnp.concatenate(rows, 1)
    return jnp.pad(row, ((0, 0), (0, width - row.shape[1])))


def gather_vectors(rows, own):
    pieces, _, width = rows.shape
    groups = width // own
    rows = rows.reshape(pieces, 8, groups, own)
    hidden = rows[:, :4, 2].reshape(4, pieces * own)
    rows = jnp.transpose(rows, (2, 1, 0, 3)).reshape(groups * 8, pieces * own)
    return wide(jnp.concatenate([rows[:16], hidden, rows[20:]], 0))


def fast_layer(
    target, memory, cotangent, bucket, source_len, self_qkv, self_out, self_bias, cross_qkv,
    cross_out, cross_bias, ffn_in, ffn_in_bias, ffn_out, ffn_out_bias, norm_gain, norm_bias,
):
    dp = lax.axis_index("dp")
    high, core, depth, side = places()
    count, width = memory.shape[0], target.shape[1]
    own = self_out.shape[0]
    pieces = width // own
    info = jnp.concatenate([bucket, source_len, core[None]])
    vectors = lay_vectors(
        (self_bias, cross_bias, ffn_in_bias.reshape(4, own), ffn_out_bias[None], norm_gain, norm_bias), width
    )
    head = jnp.concatenate([pick(jnp.concatenate([self_qkv, cross_out[None]], 0), 0, dp), vectors], 0)
    mid = pick(jnp.concatenate([self_out[None], cross_qkv], 0), 0, dp)
    head, mid = fence(join_depth(head, depth), mid)
    one, two = cut(head)
    one, two = join_pair(one, 1, side, "fsdp", 1), join_pair(two, 1, high, "dp", 2)
    one, two, mid, ffn_in, ffn_out = fence(one, two, mid, ffn_in, ffn_out)
    one, two = join_pair(one, 2, high, "dp", 2), join_pair(two, 1, side, "fsdp", 1)
    in_cols = pick(ffn_in.reshape(own, 4, width), 1, dp)
    out_rows = pick(ffn_out.reshape(4, own, width), 0, dp)
    tail = lax.all_gather(
        jnp.concatenate([in_cols, out_rows], 0), ("dp", "fsdp"), axis=0, tiled=True
    ).reshape(4, pieces, 2 * own, width)
    half = own // 2
    mine = jnp.concatenate([one, two[:, :, :, :half]], 3).reshape(pieces, 2, own, width)
    mine, mid = fence(mine, join_depth(mid, depth))
    got = pair_swap(mine, "dp", 1)
    vectors = gather_vectors(two[:, :, 0, half:].reshape(pieces, 8, width), own)
    three, four = cut(mid)
    parts = (three, pair_swap(three, "fsdp", 1), four, pair_swap(four, "dp", 2))

    def mid_step(queries, parts):
        queries, three, got_three, four, got_four = fence(queries, *parts)
        three, four = join(three, got_three, 1, side), join(four, got_four, 1, high)
        return queries, (three, pair_swap(three, "dp", 2), four, pair_swap(four, "fsdp", 1))

    def mid_last(context, parts):
        context, three, got_three, four, got_four = fence(context, *parts)
        three, four = join(three, got_three, 2, high), join(four, got_four, 1, side)
        mine = jnp.concatenate([three, four], 3).reshape(pieces, 2, own, width)
        return context, (mine, pair_swap(mine, "dp", 1))

    head = (mine, got)
    output, grad_ffn, grad_mid, dz1, self_inputs, dk_cross, dv_cross, cross, sums, mid = forward(
        target, memory, cotangent, info, pieces, head, parts, tail, vectors, mid_step, mid_last
    )
    sum_ffn = lax.psum_scatter(
        grad_ffn.reshape(-1, width), ("dp", "fsdp"), scatter_dimension=0, tiled=True
    )
    pairs = width // PAIR
    by_owner = lambda rows: rows[: 2 * width].reshape(2, 4, 2, own, width)
    mine, other, queries = fence(*grad_mid, self_inputs[0])
    got = pair_swap(other, "dp", 1)
    grads = self_attend_back(info, queries, *self_inputs[1:], first=0, count=pairs // 2)
    got, *grads = fence(got, *grads)
    one, two = cut(by_owner(add(mine, got)))
    one, two, queries = fence(one, two, queries)
    got_one = pair_swap(pick(one, 0, 1 - high), "dp", 2)
    got_two = pair_swap(pick(two, 2, 1 - side), "fsdp", 1)
    grads = self_attend_back(
        info, queries, *self_inputs[1:], first=pairs // 2, count=pairs // 2, start=tuple(grads)
    )
    got_one, got_two, *grads = fence(got_one, got_two, *grads)
    one, two = add(pick(one, 0, high), got_one), add(pick(two, 2, side), got_two)
    one, two, target_late = fence(one, two, target)
    got_one = pair_swap(pick(one, 1, 1 - side), "fsdp", 1)
    got_two = pair_swap(pick(two, 0, 1 - high), "dp", 2)
    mine, other = self_weights(info, target_late, grads, cross, sums)
    got_one, got_two, mine, other = fence(got_one, got_two, mine, other)
    one, two = add(pick(one, 1, side), got_one), add(pick(two, 0, high), got_two)
    both = jnp.concatenate([one, two], 1)
    both, other, dz1 = fence(both, other, dz1)
    got = pair_swap(other, "dp", 1)
    rings = [ring(pick(both, 0, (depth + step) % 4), "fsdp", 2 * step) for step in (1, 2, 3)]
    target_grad = target_back(info, dz1, grads, head)
    got, *rings, target_grad = fence(got, *rings, target_grad)
    sum_mid = wide(pick(both, 0, depth))
    for item in rings:
        sum_mid = sum_mid + wide(item)
    total = add(mine, got)
    one, two = cut(by_owner(total))
    shape = one.shape
    flat = lambda item: item.reshape(-1, width)
    vectors = total[2 * width :]
    keep, send, vectors, two, dk_cross = fence(
        flat(pick(one, 0, high)), flat(pick(one, 0, 1 - high)), vectors, two, dk_cross
    )
    got_one = pair_swap(jnp.concatenate([send, vectors], 0), "dp", 2)
    got_two = pair_swap(pick(two, 2, 1 - side), "fsdp", 1)
    memory_grad = memory_back(info, dk_cross, dv_cross, mid, 0, count // 2)
    got_one, got_two, memory_grad = fence(got_one, got_two, memory_grad)
    one = add(keep, got_one[:-VECTORS]).reshape(4, 2, -1, width)
    vectors = add(vectors, got_one[-VECTORS:])
    two = add(pick(two, 2, side), got_two)
    keep, send, vectors, two, dk_cross = fence(
        flat(pick(one, 1, side)), flat(pick(one, 1, 1 - side)), vectors, two, dk_cross
    )
    got_one = pair_swap(jnp.concatenate([send, vectors], 0), "fsdp", 1)
    got_two = pair_swap(pick(two, 0, 1 - high), "dp", 2)
    memory_grad = memory_back(
        info, dk_cross, dv_cross, mid, count // 2, count - count // 2, start=(memory_grad,)
    )
    got_one, got_two, memory_grad = fence(got_one, got_two, memory_grad)
    one = add(keep, got_one[:-VECTORS]).reshape(4, -1, width)
    vectors = add(vectors, got_one[-VECTORS:])
    two = add(pick(two, 0, high), got_two)
    both = jnp.concatenate([one, two], 1)
    early = jnp.concatenate([sum_ffn, sum_mid.astype(bf16)], 0)
    both, vectors, early = fence(both, vectors, early)
    rings = [
        ring(jnp.concatenate([pick(both, 0, (depth + step) % 4), vectors], 0), "fsdp", 2 * step)
        for step in (1, 2, 3)
    ]
    early = join_pair(early, 0, high, "dp", 2)
    early, *rings = fence(early, *rings)
    late = jnp.concatenate([pick(both, 0, depth), vectors], 0)
    late = wide(late)
    for item in rings:
        late = late + wide(item)
    vectors = late[-VECTORS:][:17]
    late = join_pair(late[:-VECTORS].astype(bf16), 0, high, "dp", 2)
    early = join_pair(early, 1, core, "dp", 1)
    early, late = fence(early, late)
    late = join_pair(late, 1, core, "dp", 1)
    early = wide(early.reshape((4,) + early.shape[2:]))
    late = wide(late.reshape((4,) + late.shape[2:]))
    grad_in = jnp.swapaxes(early[:, :own], 0, 1).reshape(own, 4 * width)
    grad_out = early[:, own : 2 * own].reshape(4 * own, width)
    mid = early[:, 2 * own :]
    place = lax.axis_index("fsdp")
    hidden = pick(vectors[6:10].reshape(pieces, 4 * own), 0, place)
    vectors = lax.dynamic_slice_in_dim(vectors, place * own, own, 1)
    return (
        output, target_grad, memory_grad, late[:3], mid[0], vectors[:3], mid[1:], late[3], vectors[3:6],
        grad_in, hidden, grad_out, vectors[10], vectors[11:14], vectors[14:17],
    )


def plain_layer(
    target, memory, cotangent, bucket, source_len, self_qkv, self_out, self_bias, cross_qkv,
    cross_out, cross_bias, ffn_in, ffn_in_bias, ffn_out, ffn_out_bias, norm_gain, norm_bias,
):
    gather = lambda item, axis: lax.all_gather(item, "fsdp", axis=axis, tiled=True)
    info = jnp.concatenate([bucket, source_len, jnp.zeros_like(bucket)])
    width = target.shape[1]
    blocks = ffn_out.shape[0] * lax.axis_size("fsdp") // width
    split = lambda units: (units[None, 0::2], units[None, 1::2])
    head = split(jnp.concatenate([gather(self_qkv, 1), gather(cross_out, 0)[None]], 0))
    mid = split(jnp.concatenate([gather(self_out, 0)[None], gather(cross_qkv, 1)], 0))
    ffn_in_w = jnp.swapaxes(gather(ffn_in, 0).reshape(width, blocks, width), 0, 1)
    tail = jnp.concatenate([ffn_in_w, gather(ffn_out, 0).reshape(blocks, width, width)], 1)[:, None]
    vectors = (
        gather(self_bias, 1), gather(cross_bias, 1), gather(ffn_in_bias, 0).reshape(blocks, width),
        gather(ffn_out_bias, 0)[None], gather(norm_gain, 1), gather(norm_bias, 1),
    )
    vectors = wide(
        jnp.concatenate([jnp.pad(item, ((0, 8 - item.shape[0]), (0, 0))) for item in vectors], 0)
    )
    outs, grad_ffn, grad_mid, grad_self = forward_back(
        target, memory, cotangent, info, 1, head, mid, tail, vectors
    )

    def reduce(grad, axis):
        piece = lax.psum_scatter(wide(grad), "fsdp", scatter_dimension=axis, tiled=True)
        return lax.psum(piece, "dp")

    def units(mine, other):
        both = [item[: 2 * width].reshape(2, width, width) for item in (mine, other)]
        return jnp.stack(both, 1).reshape(4, width, width)

    grad_in = jnp.swapaxes(grad_ffn[:, 0, :width], 0, 1).reshape(width, blocks * width)
    grad_out = grad_ffn[:, 0, width:].reshape(blocks * width, width)
    vectors = grad_self[0][2 * width :]
    grad_self, grad_mid = units(*grad_self), units(*grad_mid)
    return outs + (
        reduce(grad_self[:3], 1),
        reduce(grad_mid[0], 0),
        reduce(vectors[:3], 1),
        reduce(grad_mid[1:], 1),
        reduce(grad_self[3], 0),
        reduce(vectors[3:6], 1),
        reduce(grad_in, 0),
        reduce(vectors[6 : 6 + blocks].reshape(-1), 0),
        reduce(grad_out, 0),
        reduce(vectors[10], 0),
        reduce(vectors[11:14], 1),
        reduce(vectors[14:17], 1),
    )


def solution(mesh):
    rows = P(("dp", "fsdp"))
    first = P("fsdp")
    second = P(None, "fsdp")
    weights = (second, first, second, second, first, second, first, first, first, first, second, second)
    layer = fast_layer if (mesh.shape["dp"], mesh.shape["fsdp"]) == (4, 8) else plain_layer
    return jax.shard_map(
        layer,
        mesh=mesh,
        in_specs=(rows,) * 5 + weights,
        out_specs=(rows,) * 3 + weights,
        check_vma=False,
    )
```

time: 539 us -> 432 us (0.80)
  the two profiles are of different devices: /device:TPU:23 before, /device:TPU:9 now
where the time goes in v2:
time: 432 us; the launch traced here: 425 us
  Pallas kernels  249 us (58%)
  waiting for transfers between devices  81.9 us (19%)
  starting transfers between devices  44.4 us (10%)
  local copies, waits for them, and re-layouts  17.8 us (4%)
  other arithmetic  16 us (4%)
  between operations  15.9 us (4%)
    pallas_call x10, Pallas kernels, row_call(): pl.pallas_call(kernel, grid_spec=pltpu.PrefetchScalarGridSpec(num_scalar_...  149 us
    pallas_call x5, Pallas kernels, attend_call(): pl.pallas_call(functools.partial(kernel, len(start)), grid_spec=pltpu.Pre...  85.7 us
    ppermute x12, waiting for transfers between devices, ring(): lax.ppermute(array, axis, [(place, (place + shift) % count) for place in...  40.9 us
    ppermute x24, waiting for transfers between devices, pair_swap(): lax.ppermute(array, axis, [(place, place ^ bit) for place in range(count)])  40.9 us
    ppermute x24, starting transfers between devices, pair_swap(): lax.ppermute(array, axis, [(place, place ^ bit) for place in range(count)])  31 us
    pallas_call x1, Pallas kernels, ffn_weights(): pl.pallas_call(ffn_weights_kernel, grid=(blocks,), in_specs=[whole, part,...  14.5 us
    ppermute x12, starting transfers between devices, ring(): lax.ppermute(array, axis, [(place, (place + shift) % count) for place in...  13.2 us
  transfers between devices with their start and end apart: 38, of which 23 were waited for; matrix products, arithmetic and copies ran while one was open for 5% of the time, Pallas kernels for 46%

profile of v2, /device:TPU:9, one launch (start us, length us, event | category | flops | bytes accessed | tf_op | source)
XLA Modules:
  0.0 425.1 jit_solution(4986629618503703530)
XLA Ops:
  17.6 9.3 %collective-permute-done.1 = bf16[104,768]{1,0:T(8,128)(2,1)S(1)} collective-permute-done((bf16[104,768]{1,0:T(8,128)(2,1)S(1)}, bf16[104,768]{1,0:T(8,128)(2,1)S(1)}, u32[]{:S(2)}, u32[]{:S(2)}) %collective-permute-start.1) | collective-permute-done | bytes 159776 | tf_op jit(solution)/shard_map/ppermute | solution.py:923
  32.4 5.5 %collective-permute-done.3 = bf16[4,48,768]{2,1,0:T(8,128)(2,1)S(1)} collective-permute-done((bf16[4,48,768]{2,1,0:T(8,128)(2,1)S(1)}, bf16[4,48,768]{2,1,0:T(8,128)(2,1)S(1)}, u32[]{:S(2)}, u32[]{:S(2)}) %collective-permute-start.3) | collective-permute-done | bytes 294944 | tf_op jit(solution)/shard_map/ppermute | solution.py:918
  48.7 10.9 %collective-permute-done.9 = bf16[96,768]{1,0:T(8,128)(2,1)S(1)} collective-permute-done((bf16[96,768]{1,0:T(8,128)(2,1)S(1)}, bf16[96,768]{1,0:T(8,128)(2,1)S(1)}, u32[]{:S(2)}, u32[]{:S(2)}) %collective-permute-start.9) | collective-permute-done | bytes 147488 | tf_op jit(solution)/shard_map/ppermute | solution.py:923
  69.8 9.0 %project_self.1 = (bf16[1024,768]{1,0:T(8,128)(2,1)}, bf16[1024,768]{1,0:T(8,128)(2,1)}, bf16[1024,768]{1,0:T(8,128)(2,1)}) custom-call(s32[6]{0:T(128)} %pad_add_fusion.info, bf16[1024,768]{1,0:T(8,128)(2,1)} %x_hbm, bf16[8,2,96,768]{3,2,1,0:T(8,128)(2,1)} %bitcast.22.mine, bf16[8,2,96,768]{3,2,1,0:T(8,128)(2,1)} %collective-permute-done.10.got, ...), custom_call_target="tpu_custom_call" | custom-call | flops 4831838208 | bytes 8388608 | tf_op jit(solution)/shard_map/project_self/pallas_call | solution.py:396
  83.3 9.5 %self_attend.1 = (bf16[1024,768]{1,0:T(8,128)(2,1)}, f32[6,4,1,512]{3,2,1,0:T(1,128)}) custom-call(s32[6]{0:T(128)} %pad_add_fusion.info, bf16[1024,768]{1,0:T(8,128)(2,1)} %get-tuple-element.179.q_ref, bf16[1024,768]{1,0:T(8,128)(2,1)} %get-tuple-element.138.k_ref, bf16[1024,768]{1,0:T(8,128)(2,1)} %get-tuple-element.139.v_ref), custom_call_target="tpu_custom_call" | custom-call | flops 19327352832 | bytes 8388608 | tf_op jit(solution)/shard_map/self_attend/pallas_call | solution.py:288
  100.6 4.3 %collective-permute-done.15.got = bf16[8,2,96,768]{3,2,1,0:T(8,128)(2,1)} collective-permute-done((bf16[8,2,96,768]{3,2,1,0:T(8,128)(2,1)S(1)}, bf16[8,2,96,768]{3,2,1,0:T(8,128)(2,1)}, u32[]{:S(2)}, u32[]{:S(2)}) %collective-permute-start.15) | collective-permute-done | bytes 2359328 | tf_op jit(solution)/shard_map/ppermute | solution.py:918
  104.9 9.4 %first_norm.1 = (f32[1024,768]{1,0:T(8,128)}, bf16[1024,768]{1,0:T(8,128)(2,1)}, bf16[1024,768]{1,0:T(8,128)(2,1)}) custom-call(s32[6]{0:T(128)} %pad_add_fusion.info, bf16[1024,768]{1,0:T(8,128)(2,1)} %x_hbm, bf16[1024,768]{1,0:T(8,128)(2,1)} %get-tuple-element.145.c_ref.self_ref.o_ref, bf16[8,2,96,768]{3,2,1,0:T(8,128)(2,1)} %bitcast.181, ...), custom_call_target="tpu_custom_call" | custom-call | flops 4831838208 | bytes 8388608 | tf_op jit(solution)/shard_map/first_norm/pallas_call | solution.py:396
  114.4 16.2 %project_memory.1 = (bf16[4,1024,768]{2,1,0:T(8,128)(2,1)}, bf16[4,1024,768]{2,1,0:T(8,128)(2,1)}) custom-call(s32[6]{0:T(128)} %pad_add_fusion.info, bf16[4,1024,768]{2,1,0:T(8,128)(2,1)} %m_ref.3, bf16[8,2,96,768]{3,2,1,0:T(8,128)(2,1)} %bitcast.182, bf16[8,2,96,768]{3,2,1,0:T(8,128)(2,1)} %collective-permute-done.15.got, ...), custom_call_target="tpu_custom_call" | custom-call | flops 9663676416 | bytes 8388608 | tf_op jit(solution)/shard_map/project_memory/pallas_call | solution.py:396
  130.6 26.3 %cross_attend.1 = (bf16[1024,768]{1,0:T(8,128)(2,1)}, f32[6,4,1,512]{3,2,1,0:T(1,128)}) custom-call(s32[6]{0:T(128)} %pad_add_fusion.info, bf16[1024,768]{1,0:T(8,128)(2,1)} %get-tuple-element.151.q_ref, bf16[4,1024,768]{2,1,0:T(8,128)(2,1)} %get-tuple-element.152.k_ref, bf16[4,1024,768]{2,1,0:T(8,128)(2,1)} %get-tuple-element.153.v_ref), custom_call_target="tpu_custom_call" | custom-call | flops 19327352832 | bytes 8388608 | tf_op jit(solution)/shard_map/cross_attend/pallas_call | solution.py:288
  156.9 38.9 %ffn_block.1 = (bf16[1024,768]{1,0:T(8,128)(2,1)}, bf16[1024,768]{1,0:T(8,128)(2,1)}, bf16[1024,3072]{1,0:T(8,128)(2,1)}, bf16[1024,3072]{1,0:T(8,128)(2,1)}, bf...) custom-call(s32[6]{0:T(128)} %pad_add_fusion.info, ...), custom_call_target="tpu_custom_call" | custom-call | flops 38654705664 | bytes 8388608 | tf_op jit(solution)/shard_map/ffn_block/pallas_call | solution.py:396
  195.9 14.5 %ffn_weights.1 = bf16[4,8,192,768]{3,2,1,0:T(8,128)(2,1)} custom-call(bf16[1024,768]{1,0:T(8,128)(2,1)} %get-tuple-element.227.h_ref, bf16[1024,3072]{1,0:T(8,128)(2,1)} %get-tuple-element.228.du_ref, bf16[1024,3072]{1,0:T(8,128)(2,1)} %get-tuple-element.229.a_ref, bf16[1024,768]{1,0:T(8,128)(2,1)} %get-tuple-element.230.df_ref), custom_call_target="tpu_custom_call" | custom-call | flops 9663676416 | bytes 8388608 | tf_op jit(solution)/shard_map/ffn_weights/pallas_call | solution.py:852
  210.4 33.8 %cross_attend_back.1 = (bf16[1024,768]{1,0:T(8,128)(2,1)}, bf16[4,1024,768]{2,1,0:T(8,128)(2,1)}, bf16[4,1024,768]{2,1,0:T(8,128)(2,1)}) custom-call(s32[6]{0:T(128)} %pad_add_fusion.info, bf16[1024,768]{1,0:T(8,128)(2,1)} %get-tuple-element.151.q_ref, bf16[4,1024,768]{2,1,0:T(8,128)(2,1)} %get-tuple-element.152.k_ref, ...), custom_call_target="tpu_custom_call" | custom-call | flops 38654705664 | bytes 8388608 | tf_op jit(solution)/shard_map/cross_attend_back/pallas_call | solution.py:288
  244.3 10.5 %first_back.1 = (f32[1024,768]{1,0:T(8,128)}, bf16[1024,768]{1,0:T(8,128)(2,1)}, bf16[1024,768]{1,0:T(8,128)(2,1)}, f32[8,768]{1,0:T(8,128)}) custom-call(s32[6]{0:T(128)} %pad_add_fusion.info, f32[1024,768]{1,0:T(8,128)} %get-tuple-element.164.dz2_ref, bf16[1024,768]{1,0:T(8,128)(2,1)} %get-tuple-element.163.dq_ref, f32[1024,768]{1,0:T(8,128)} %get-tuple-element.150.z_ref, ...), custom_call_target="tpu_custom_call" | custom-call | flops 4831838208 | bytes 8388608 | tf_op jit(solution)/shard_map/first_back/pallas_call | solution.py:396
  254.8 21.7 %mid_weights.1 = (bf16[1536,768]{1,0:T(8,128)(2,1)}, bf16[1536,768]{1,0:T(8,128)(2,1)}, f32[1,768]{1,0:T(1,128)}) custom-call(s32[6]{0:T(128)} %pad_add_fusion.info, bf16[4,1024,768]{2,1,0:T(8,128)(2,1)} %m_ref.3, bf16[4,1024,768]{2,1,0:T(8,128)(2,1)} %get-tuple-element.221.dk_ref, bf16[4,1024,768]{2,1,0:T(8,128)(2,1)} %get-tuple-element.161.dv_ref, ...), custom_call_target="tpu_custom_call" | custom-call | flops 9663676416 | bytes 8388608 | tf_op jit(solution)/shard_map/mid_weights/pallas_call | solution.py:396
  276.6 8.2 %self_attend_back.2 = (bf16[1024,768]{1,0:T(8,128)(2,1)}, bf16[1024,768]{1,0:T(8,128)(2,1)}, bf16[1024,768]{1,0:T(8,128)(2,1)}) custom-call(s32[6]{0:T(128)} %pad_add_fusion.info, bf16[1024,768]{1,0:T(8,128)(2,1)} %get-tuple-element.179.q_ref, bf16[1024,768]{1,0:T(8,128)(2,1)} %get-tuple-element.138.k_ref, bf16[1024,768]{1,0:T(8,128)(2,1)} %get-tuple-element.139.v_ref, ...), custom_call_target="tpu_custom_call" | custom-call | flops 38654705664 | bytes 8388608 | tf_op jit(solution)/shard_map/self_attend_back/pallas_call | solution.py:288
  287.7 5.8 %collective-permute-start.17 = (bf16[4,2,48,768]{3,2,0,1:T(8,128)(2,1)S(1)}, bf16[4,2,48,768]{3,2,0,1:T(8,128)(2,1)}, u32[]{:S(2)}, u32[]{:S(2)}) collective-permute-start(bf16[4,2,48,768]{3,2,0,1:T(8,128)(2,1)S(1)} %dynamic-slice_bitcast_fusion.2), channel_id=1, source_target_pairs={{0,16},{8,24},{16,0},{24,8},{1,17},{9,25},{17,1},{25,9},{2,18},{10... | collective-permute-start | bytes 1769480 | tf_op jit(solution)/shard_map/ppermute | solution.py:918
  293.5 7.8 %self_attend_back.3 = (bf16[1024,768]{1,0:T(8,128)(2,1)}, bf16[1024,768]{1,0:T(8,128)(2,1)}, bf16[1024,768]{1,0:T(8,128)(2,1)}) custom-call(s32[6]{0:T(128)} %pad_add_fusion.info, bf16[1024,768]{1,0:T(8,128)(2,1)} %get-tuple-element.179.q_ref, ...), custom_call_target="tpu_custom_call", output_to_operand_aliasing={{0}: (7, {}), {1}: (8, {}), {2}: (9, {})} | custom-call | flops 38654705664 | bytes 8388608 | tf_op jit(solution)/shard_map/self_attend_back/pallas_call | solution.py:288
  301.4 6.4 %collective-permute-done.18 = bf16[2,4,48,768]{3,2,1,0:T(8,128)(2,1)S(1)} collective-permute-done((bf16[2,4,48,768]{3,2,1,0:T(8,128)(2,1)S(1)}, bf16[2,4,48,768]{3,2,1,0:T(8,128)(2,1)S(1)}, u32[]{:S(2)}, u32[]{:S(2)}) %collective-permute-start.18) | collective-permute-done | bytes 589856 | tf_op jit(solution)/shard_map/ppermute | solution.py:918
  313.2 11.8 %self_weights.1 = (bf16[1568,768]{1,0:T(8,128)(2,1)}, bf16[1568,768]{1,0:T(8,128)(2,1)}) custom-call(s32[6]{0:T(128)} %pad_add_fusion.info, bf16[1024,768]{1,0:T(8,128)(2,1)} %x_hbm, bf16[1024,768]{1,0:T(8,128)(2,1)} %get-tuple-element.191.q_hbm.q_ref, bf16[1024,768]{1,0:T(8,128)(2,1)} %get-tuple-element.192.k_hbm.k_ref, ...), custom_call_target="tpu_custom_call" | custom-call | flops 4831838208 | bytes 8388608 | tf_op jit(solution)/shard_map/self_weights/pallas_call | solution.py:396
  327.6 4.9 %collective-permute-start.23 = (bf16[96,768]{1,0:T(8,128)(2,1)S(1)}, bf16[96,768]{1,0:T(8,128)(2,1)S(1)}, u32[]{:S(2)}, u32[]{:S(2)}) collective-permute-start(bf16[96,768]{1,0:T(8,128)(2,1)S(1)} %get-tuple-element.274), channel_id=1, source_target_pairs={{0,4},{1,5},{2,6},{3,7},{4,0},{5,1},{6,2},{7,3},{8,12},{9,13},{10,... | collective-permute-start | bytes 442376 | tf_op jit(solution)/shard_map/ppermute | solution.py:923
  332.6 10.4 %target_back.1 = f32[1024,768]{1,0:T(8,128)} custom-call(s32[6]{0:T(128)} %pad_add_fusion.info, f32[1024,768]{1,0:T(8,128)} %get-tuple-element.207.z_ref, bf16[1024,768]{1,0:T(8,128)(2,1)} %get-tuple-element.191.q_hbm.q_ref, bf16[1024,768]{1,0:T(8,128)(2,1)} %get-tuple-element.192.k_hbm.k_ref, bf16[1024,768]{1,0:T(8,128)(2,1)} %get-tuple-element.193.v_hbm.v_ref, ...), custom_call_target="tpu_custom_call" | custom-call | flops 4831838208 | bytes 8388608 | tf_op jit(solution)/shard_map/target_back/pallas_call | solution.py:396
  356.5 10.5 %memory_back.2.refs_0_ = f32[4,1024,768]{2,1,0:T(8,128)} custom-call(s32[6]{0:T(128)} %pad_add_fusion.info, bf16[4,1024,768]{2,1,0:T(8,128)(2,1)} %get-tuple-element.221.dk_ref, bf16[4,1024,768]{2,1,0:T(8,128)(2,1)} %get-tuple-element.161.dv_ref, bf16[8,2,96,768]{3,2,1,0:T(8,128)(2,1)} %bitcast.184, bf16[8,2,96,768]{3,2,1,0:T(8,128)(2,1)} %collective-permute-done.15.got), custom_call_target="tpu_custom_call" | custom-call | flops 4831838208 | bytes 8388608 | tf_op jit(solution)/shard_map/memory_back/pallas_call | solution.py:396
  373.8 10.4 %memory_back.3 = f32[4,1024,768]{2,1,0:T(8,128)} custom-call(s32[6]{0:T(128)} %pad_add_fusion.info, bf16[4,1024,768]{2,1,0:T(8,128)(2,1)} %get-tuple-element.221.dk_ref, bf16[4,1024,768]{2,1,0:T(8,128)(2,1)} %get-tuple-element.161.dv_ref, bf16[8,2,96,768]{3,2,1,0:T(8,128)(2,1)} %bitcast.185, ...), custom_call_target="tpu_custom_call", output_to_operand_aliasing={{}: (5, {})} | custom-call | flops 4831838208 | bytes 8388608 | tf_op jit(solution)/shard_map/memory_back/pallas_call | solution.py:396
  387.4 9.8 %collective-permute-done.29 = bf16[288,768]{1,0:T(8,128)(2,1)S(1)} collective-permute-done((bf16[288,768]{1,0:T(8,128)(2,1)S(1)}, bf16[288,768]{1,0:T(8,128)(2,1)S(1)}, u32[]{:S(2)}, u32[]{:S(2)}) %collective-permute-start.29) | collective-permute-done | bytes 442400 | tf_op jit(solution)/shard_map/ppermute | solution.py:918
  (205 shorter events, 103.0 us)
Async XLA Ops:
  7.2 149.7 %all-gather.2.cloned.1.call-start = ((), (), s32[]{:S(2)}) async-start(), calls=%async_computation.1 | async-start | bytes 9732096 | tf_op jit(solution)/shard_map/all_gather | solution.py:1021
  13.9 13.0 %collective-permute-start.1 = (bf16[104,768]{1,0:T(8,128)(2,1)S(1)}, bf16[104,768]{1,0:T(8,128)(2,1)S(1)}, u32[]{:S(2)}, u32[]{:S(2)}) collective-permute-start(bf16[104,768]{1,0:T(8,128)(2,1)S(1)} %fusion.12), channel_id=1, source_target_pairs={{0,4},{1,5},{2,6},{3,7},{4,0},{5,1},{6,2},{7,3},{8,12},{9,13},{10,... | collective-permute-start | bytes 479240 | tf_op jit(solution)/shard_map/ppermute | solution.py:923
  15.0 14.8 %collective-permute-start.2 = (bf16[104,768]{1,0:T(8,128)(2,1)S(1)}, bf16[104,768]{1,0:T(8,128)(2,1)S(1)}, u32[]{:S(2)}, u32[]{:S(2)}) collective-permute-start(bf16[104,768]{1,0:T(8,128)(2,1)S(1)} %fusion.12), channel_id=1, source_target_pairs={{0,6},{1,7},{2,0},{3,1},{4,2},{5,3},{6,4},{7,5},{8,14},{9,15},{10,... | collective-permute-start | bytes 479240 | tf_op jit(solution)/shard_map/ppermute | solution.py:923
  41.7 342.8 %reduce-scatter.2.cloned.1.call-start = ((), (), s32[]{:S(2)}) async-start(), calls=%async_computation.2 | async-start | bytes 9732096 | tf_op jit(solution)/shard_map/reduce_scatter | solution.py:1047
  41.9 17.7 %collective-permute-start.9 = (bf16[96,768]{1,0:T(8,128)(2,1)S(1)}, bf16[96,768]{1,0:T(8,128)(2,1)S(1)}, u32[]{:S(2)}, u32[]{:S(2)}) collective-permute-start(bf16[96,768]{1,0:T(8,128)(2,1)S(1)} %fusion.14), channel_id=1, source_target_pairs={{0,6},{1,7},{2,0},{3,1},{4,2},{5,3},{6,4},{7,5},{8,14},{9,15},{10,... | collective-permute-start | bytes 442376 | tf_op jit(solution)/shard_map/ppermute | solution.py:923
  43.3 16.4 %collective-permute-start.6 = (bf16[4,2,56,768]{3,2,0,1:T(8,128)(2,1)S(1)}, bf16[4,2,56,768]{3,2,0,1:T(8,128)(2,1)S(1)}, u32[]{:S(2)}, u32[]{:S(2)}) collective-permute-start(bf16[4,2,56,768]{3,2,0,1:T(8,128)(2,1)S(1)} %pad_maximum_fusion.3), channel_id=1, source_target_pairs={{0,1},{1,0},{2,3},{3,2},{4,5},{5,4},{6,7},{7,6},{8,9},{9,8},{10,11... | collective-permute-start | bytes 2064392 | tf_op jit(solution)/shard_map/ppermute | solution.py:918
  43.5 16.1 %collective-permute-start.5 = (bf16[4,2,48,768]{3,2,1,0:T(8,128)(2,1)S(1)}, bf16[4,2,48,768]{3,2,1,0:T(8,128)(2,1)S(1)}, u32[]{:S(2)}, u32[]{:S(2)}) collective-permute-start(bf16[4,2,48,768]{3,2,1,0:T(8,128)(2,1)S(1)} %pad_maximum_fusion.5), channel_id=1, source_target_pairs={{0,16},{8,24},{16,0},{24,8},{1,17},{9,25},{17,1},{25,9},{2,18},{10... | collective-permute-start | bytes 1769480 | tf_op jit(solution)/shard_map/ppermute | solution.py:918
  67.4 12.8 %collective-permute-start.11 = (bf16[4,48,768]{2,1,0:T(8,128)(2,1)S(1)}, bf16[4,48,768]{2,1,0:T(8,128)(2,1)S(1)}, u32[]{:S(2)}, u32[]{:S(2)}) collective-permute-start(bf16[4,48,768]{2,1,0:T(8,128)(2,1)S(1)} %get-tuple-element.141), channel_id=1, source_target_pairs={{0,1},{1,0},{2,3},{3,2},{4,5},{5,4},{6,7},{7,6},{8,9},{9,8},{10,11... | collective-permute-start | bytes 884744 | tf_op jit(solution)/shard_map/ppermute | solution.py:918
  67.7 12.5 %collective-permute-start.12 = (bf16[4,48,768]{2,1,0:T(8,128)(2,1)S(1)}, bf16[4,48,768]{2,1,0:T(8,128)(2,1)S(1)}, u32[]{:S(2)}, u32[]{:S(2)}) collective-permute-start(bf16[4,48,768]{2,1,0:T(8,128)(2,1)S(1)} %get-tuple-element.143), channel_id=1, source_target_pairs={{0,16},{8,24},{16,0},{24,8},{1,17},{9,25},{17,1},{25,9},{2,18},{10... | collective-permute-start | bytes 884744 | tf_op jit(solution)/shard_map/ppermute | solution.py:918
  80.3 16.6 %collective-permute-start.14 = (bf16[4,2,48,768]{3,2,0,1:T(8,128)(2,1)S(1)}, bf16[4,2,48,768]{3,2,0,1:T(8,128)(2,1)S(1)}, u32[]{:S(2)}, u32[]{:S(2)}) collective-permute-start(bf16[4,2,48,768]{3,2,0,1:T(8,128)(2,1)S(1)} %pad_maximum_fusion.7), channel_id=1, source_target_pairs={{0,1},{1,0},{2,3},{3,2},{4,5},{5,4},{6,7},{7,6},{8,9},{9,8},{10,11... | collective-permute-start | bytes 1769480 | tf_op jit(solution)/shard_map/ppermute | solution.py:918
  81.7 15.2 %collective-permute-start.13 = (bf16[4,2,48,768]{3,2,0,1:T(8,128)(2,1)S(1)}, bf16[4,2,48,768]{3,2,0,1:T(8,128)(2,1)S(1)}, u32[]{:S(2)}, u32[]{:S(2)}) collective-permute-start(bf16[4,2,48,768]{3,2,0,1:T(8,128)(2,1)S(1)} %pad_maximum_fusion.6), channel_id=1, source_target_pairs={{0,16},{8,24},{16,0},{24,8},{1,17},{9,25},{17,1},{25,9},{2,18},{10... | collective-permute-start | bytes 1769480 | tf_op jit(solution)/shard_map/ppermute | solution.py:918
  287.6 20.2 %collective-permute-start.18 = (bf16[2,4,48,768]{3,2,1,0:T(8,128)(2,1)S(1)}, bf16[2,4,48,768]{3,2,1,0:T(8,128)(2,1)S(1)}, u32[]{:S(2)}, u32[]{:S(2)}) collective-permute-start(bf16[2,4,48,768]{3,2,1,0:T(8,128)(2,1)S(1)} %dynamic-slice_bitcast_fusion.1), channel_id=1, source_target_pairs={{0,1},{1,0},{2,3},{3,2},{4,5},{5,4},{6,7},{7,6},{8,9},{9,8},{10,11... | collective-permute-start | bytes 1769480 | tf_op jit(solution)/shard_map/ppermute | solution.py:918
  287.7 21.5 %collective-permute-start.17 = (bf16[4,2,48,768]{3,2,0,1:T(8,128)(2,1)S(1)}, bf16[4,2,48,768]{3,2,0,1:T(8,128)(2,1)}, u32[]{:S(2)}, u32[]{:S(2)}) collective-permute-start(bf16[4,2,48,768]{3,2,0,1:T(8,128)(2,1)S(1)} %dynamic-slice_bitcast_fusion.2), channel_id=1, source_target_pairs={{0,16},{8,24},{16,0},{24,8},{1,17},{9,25},{17,1},{25,9},{2,18},{10... | collective-permute-start | bytes 1769480 | tf_op jit(solution)/shard_map/ppermute | solution.py:918
  310.7 14.3 %collective-permute-start.20 = (bf16[4,48,768]{2,1,0:T(8,128)(2,1)S(1)}, bf16[4,48,768]{2,1,0:T(8,128)(2,1)S(1)}, u32[]{:S(2)}, u32[]{:S(2)}) collective-permute-start(bf16[4,48,768]{2,1,0:T(8,128)(2,1)S(1)} %dynamic-slice_bitcast_fusion.4), channel_id=1, source_target_pairs={{0,16},{8,24},{16,0},{24,8},{1,17},{9,25},{17,1},{25,9},{2,18},{10... | collective-permute-start | bytes 884744 | tf_op jit(solution)/shard_map/ppermute | solution.py:918
  312.6 12.4 %collective-permute-start.19 = (bf16[4,48,768]{2,1,0:T(8,128)(2,1)S(1)}, bf16[4,48,768]{2,1,0:T(8,128)(2,1)S(1)}, u32[]{:S(2)}, u32[]{:S(2)}) collective-permute-start(bf16[4,48,768]{2,1,0:T(8,128)(2,1)S(1)} %dynamic-slice_bitcast_fusion.5), channel_id=1, source_target_pairs={{0,1},{1,0},{2,3},{3,2},{4,5},{5,4},{6,7},{7,6},{8,9},{9,8},{10,11... | collective-permute-start | bytes 884744 | tf_op jit(solution)/shard_map/ppermute | solution.py:918
  325.2 24.9 %collective-permute-start.21 = (bf16[1568,768]{1,0:T(8,128)(2,1)}, bf16[1568,768]{1,0:T(8,128)(2,1)}, u32[]{:S(2)}, u32[]{:S(2)}) collective-permute-start(bf16[1568,768]{1,0:T(8,128)(2,1)} %get-tuple-element.205), channel_id=1, source_target_pairs={{0,8},{8,0},{16,24},{24,16},{1,9},{9,1},{17,25},{25,17},{2,10},{10... | collective-permute-start | bytes 7225352 | tf_op jit(solution)/shard_map/ppermute | solution.py:918
  326.4 16.6 %collective-permute-start.22 = (bf16[96,768]{1,0:T(8,128)(2,1)S(1)}, bf16[96,768]{1,0:T(8,128)(2,1)S(1)}, u32[]{:S(2)}, u32[]{:S(2)}) collective-permute-start(bf16[96,768]{1,0:T(8,128)(2,1)S(1)} %get-tuple-element.275), channel_id=1, source_target_pairs={{0,2},{1,3},{2,4},{3,5},{4,6},{5,7},{6,0},{7,1},{8,10},{9,11},{10,... | collective-permute-start | bytes 442376 | tf_op jit(solution)/shard_map/ppermute | solution.py:923
  327.6 19.1 %collective-permute-start.23 = (bf16[96,768]{1,0:T(8,128)(2,1)S(1)}, bf16[96,768]{1,0:T(8,128)(2,1)S(1)}, u32[]{:S(2)}, u32[]{:S(2)}) collective-permute-start(bf16[96,768]{1,0:T(8,128)(2,1)S(1)} %get-tuple-element.274), channel_id=1, source_target_pairs={{0,4},{1,5},{2,6},{3,7},{4,0},{5,1},{6,2},{7,3},{8,12},{9,13},{10,... | collective-permute-start | bytes 442376 | tf_op jit(solution)/shard_map/ppermute | solution.py:923
  332.6 17.5 %collective-permute-start.24 = (bf16[96,768]{1,0:T(8,128)(2,1)S(1)}, bf16[96,768]{1,0:T(8,128)(2,1)S(1)}, u32[]{:S(2)}, u32[]{:S(2)}) collective-permute-start(bf16[96,768]{1,0:T(8,128)(2,1)S(1)} %get-tuple-element.273), channel_id=1, source_target_pairs={{0,6},{1,7},{2,0},{3,1},{4,2},{5,3},{6,4},{7,5},{8,14},{9,15},{10,... | collective-permute-start | bytes 442376 | tf_op jit(solution)/shard_map/ppermute | solution.py:923
  353.8 14.7 %collective-permute-start.26 = (bf16[2,4,48,768]{3,2,1,0:T(8,128)(2,1)}, bf16[2,4,48,768]{3,2,1,0:T(8,128)(2,1)}, u32[]{:S(2)}, u32[]{:S(2)}) collective-permute-start(bf16[2,4,48,768]{3,2,1,0:T(8,128)(2,1)} %dynamic-slice_bitcast_fusion), channel_id=1, source_target_pairs={{0,1},{1,0},{2,3},{3,2},{4,5},{5,4},{6,7},{7,6},{8,9},{9,8},{10,11... | collective-permute-start | bytes 1769480 | tf_op jit(solution)/shard_map/ppermute | solution.py:918
  355.4 15.2 %collective-permute-start.25 = (bf16[416,768]{1,0:T(8,128)(2,1)}, bf16[416,768]{1,0:T(8,128)(2,1)S(1)}, u32[]{:S(2)}, u32[]{:S(2)}) collective-permute-start(bf16[416,768]{1,0:T(8,128)(2,1)} %pad_maximum_fusion.4), channel_id=1, source_target_pairs={{0,16},{8,24},{16,0},{24,8},{1,17},{9,25},{17,1},{25,9},{2,18},{10... | collective-permute-start | bytes 1916936 | tf_op jit(solution)/shard_map/ppermute | solution.py:918
  372.1 12.2 %collective-permute-start.28 = (bf16[4,48,768]{2,1,0:T(8,128)(2,1)S(1)}, bf16[4,48,768]{2,1,0:T(8,128)(2,1)S(1)}, u32[]{:S(2)}, u32[]{:S(2)}) collective-permute-start(bf16[4,48,768]{2,1,0:T(8,128)(2,1)S(1)} %dynamic-slice_bitcast_fusion.3), channel_id=1, source_target_pairs={{0,16},{8,24},{16,0},{24,8},{1,17},{9,25},{17,1},{25,9},{2,18},{10... | collective-permute-start | bytes 884744 | tf_op jit(solution)/shard_map/ppermute | solution.py:918
  385.8 14.8 %collective-permute-start.31 = (bf16[128,768]{1,0:T(8,128)(2,1)S(1)}, bf16[128,768]{1,0:T(8,128)(2,1)S(1)}, u32[]{:S(2)}, u32[]{:S(2)}) collective-permute-start(bf16[128,768]{1,0:T(8,128)(2,1)S(1)} %get-tuple-element.289), channel_id=1, source_target_pairs={{0,4},{1,5},{2,6},{3,7},{4,0},{5,1},{6,2},{7,3},{8,12},{9,13},{10,... | collective-permute-start | bytes 589832 | tf_op jit(solution)/shard_map/ppermute | solution.py:923
  386.3 18.0 %collective-permute-start.32 = (bf16[128,768]{1,0:T(8,128)(2,1)S(1)}, bf16[128,768]{1,0:T(8,128)(2,1)S(1)}, u32[]{:S(2)}, u32[]{:S(2)}) collective-permute-start(bf16[128,768]{1,0:T(8,128)(2,1)S(1)} %get-tuple-element.288), channel_id=1, source_target_pairs={{0,6},{1,7},{2,0},{3,1},{4,2},{5,3},{6,4},{7,5},{8,14},{9,15},{10,... | collective-permute-start | bytes 589832 | tf_op jit(solution)/shard_map/ppermute | solution.py:923
  (23 other events, 189.8 us)
Sparse Core Ops, SparseCore 0:
  41.8 88.9 all-gather.1
  210.6 152.9 reduce-scatter.1

commit v3 on v2

--- a/solution.py
+++ b/solution.py
@@ -392,7 +392,9 @@
     by_core(info, mine, got, run)
 
 
-def row_call(kernel, name, info, grid, in_specs, out_specs, out_shape, matmuls, inputs, scratch=(), aliases=None):
+def row_call(
+    kernel, name, info, grid, in_specs, out_specs, out_shape, matmuls, inputs, scratch=(), aliases=None, limit=VMEM_LIMIT
+):
     return pl.pallas_call(
         kernel,
         grid_spec=pltpu.PrefetchScalarGridSpec(
@@ -404,7 +406,7 @@
         ),
         out_shape=out_shape,
         input_output_aliases=aliases or {},
-        compiler_params=params(),
+        compiler_params=pltpu.CompilerParams(vmem_limit_bytes=limit),
         name=name,
         cost_estimate=cost(matmuls),
     )(info, *inputs)
@@ -866,6 +868,163 @@
     )(second_low, grad_hidden, active, grad_out)
 
 
+def fold_call(kernel, name, spot, inputs, outs):
+    return row_call(
+        kernel, name, spot, (), [full(None)] * len(inputs), [full(None)] * len(outs),
+        [jax.ShapeDtypeStruct(shape, kind) for shape, kind in outs], [], inputs, limit=12 * 2**20,
+    )
+
+
+def added(*parts):
+    total = parts[0].astype(f32)
+    for part in parts[1:]:
+        total = total + part.astype(f32)
+    return total
+
+
+def fold_first_kernel(own, extra, spot, mine, got, keep_one, send_one, keep_two, send_two):
+    high, side = spot[0], spot[3]
+    half = own // 2
+    slots = keep_one.shape[0] // half
+
+    def take(place, low):
+        rows = pl.ds(pl.multiple_of(place * own + low, 16), half)
+        return added(mine[rows, :], got[rows, :]).astype(bf16)
+
+    for slot in range(slots):
+        rows = pl.ds(slot * half, half)
+        keep_one[rows, :] = take(high * slots + slot, 0)
+        send_one[rows, :] = take((1 - high) * slots + slot, 0)
+        keep_two[rows, :] = take(2 * slot + side, half)
+        send_two[rows, :] = take(2 * slot + 1 - side, half)
+    if extra:
+        vectors = added(mine[2 * slots * own :, :], got[2 * slots * own :, :]).astype(bf16)
+        keep_one[slots * half :, :] = vectors
+        send_one[slots * half :, :] = vectors
+
+
+def fold_first(spot, mine, got, own):
+    width = mine.shape[1]
+    extra = mine.shape[0] - 2 * width
+    rows = width // own * (own // 2)
+    first, second = ((rows + extra, width), bf16), ((rows, width), bf16)
+    return fold_call(
+        functools.partial(fold_first_kernel, own, extra), "fold_first", spot, (mine, got),
+        (first, first, second, second),
+    )
+
+
+def fold_second_kernel(
+    half, extra, spot, keep_a, got_a, keep_b, got_b, keep_one, send_one, keep_two, send_two
+):
+    high, side = spot[0], spot[3]
+    slots = keep_two.shape[0] // half
+
+    def take(keep, got, place):
+        rows = pl.ds(pl.multiple_of(place * half, 16), half)
+        return added(keep[rows, :], got[rows, :]).astype(bf16)
+
+    for slot in range(slots):
+        rows = pl.ds(slot * half, half)
+        keep_one[rows, :] = take(keep_a, got_a, 2 * slot + side)
+        send_one[rows, :] = take(keep_a, got_a, 2 * slot + 1 - side)
+        keep_two[rows, :] = take(keep_b, got_b, high * slots + slot)
+        send_two[rows, :] = take(keep_b, got_b, (1 - high) * slots + slot)
+    if extra:
+        low = 2 * slots * half
+        vectors = added(keep_a[low:, :], got_a[low:, :]).astype(bf16)
+        keep_one[slots * half :, :] = vectors
+        send_one[slots * half :, :] = vectors
+
+
+def fold_second(spot, keep_a, got_a, keep_b, got_b, own):
+    rows, width = keep_b.shape
+    extra = keep_a.shape[0] - rows
+    first, second = ((rows // 2 + extra, width), bf16), ((rows // 2, width), bf16)
+    return fold_call(
+        functools.partial(fold_second_kernel, own // 2, extra), "fold_second", spot,
+        (keep_a, got_a, keep_b, got_b), (first, first, second, second),
+    )
+
+
+def fold_third_kernel(half, extra, spot, keep_a, got_a, keep_b, got_b, *parts):
+    depth = spot[2]
+    slots = keep_b.shape[0] // half
+    for step, part in enumerate(parts):
+        rows = pl.ds(pl.multiple_of((depth + step) % slots * half, 16), half)
+        part[:half, :] = added(keep_a[rows, :], got_a[rows, :]).astype(bf16)
+        part[half : 2 * half, :] = added(keep_b[rows, :], got_b[rows, :]).astype(bf16)
+        if extra:
+            low = slots * half
+            part[2 * half :, :] = added(keep_a[low:, :], got_a[low:, :]).astype(bf16)
+
+
+def fold_third(spot, keep_a, got_a, keep_b, got_b, own):
+    rows, width = keep_b.shape
+    extra = keep_a.shape[0] - rows
+    part = ((own + extra, width), bf16)
+    return fold_call(
+        functools.partial(fold_third_kernel, own // 2, extra), "fold_third", spot,
+        (keep_a, got_a, keep_b, got_b), (part,) * (rows // (own // 2)),
+    )
+
+
+def sources(spot, sent, got):
+    high, core = spot[0], spot[1]
+    rows = sent.shape[0] // 2
+    return [
+        (2 * y + c, ref, pl.ds(low, rows))
+        for c, ref in ((core, sent), (1 - core, got))
+        for y, low in ((high, 0), (1 - high, rows))
+    ]
+
+
+def finish_early_kernel(own, spot, sent, got, in_ref, out_ref, first_ref, rest_ref):
+    width = sent.shape[1]
+    for place, ref, rows in sources(spot, sent, got):
+        low = rows.start
+        in_ref[:, pl.ds(pl.multiple_of(place * width, width), width)] = ref[low : low + own, :].astype(f32)
+        out_ref[pl.ds(pl.multiple_of(place * own, 8), own), :] = ref[low + own : low + 2 * own, :].astype(f32)
+        unit = ref[low + 2 * own : low + 3 * own, :].astype(f32)
+
+        @pl.when(place == 0)
+        def _(unit=unit):
+            first_ref[...] = unit
+
+        @pl.when(place != 0)
+        def _(unit=unit, place=place):
+            rest_ref[place - 1] = unit
+
+
+def finish_early(spot, sent, got, own):
+    width = sent.shape[1]
+    return fold_call(
+        functools.partial(finish_early_kernel, own), "finish_early", spot, (sent, got),
+        (((own, 4 * width), f32), ((4 * own, width), f32), ((own, width), f32), ((3, own, width), f32)),
+    )
+
+
+def finish_late_kernel(spot, sent, got, rest_ref, last_ref):
+    for place, ref, rows in sources(spot, sent, got):
+        unit = ref[rows, :].astype(f32)
+
+        @pl.when(place == 3)
+        def _(unit=unit):
+            last_ref[...] = unit
+
+        @pl.when(place != 3)
+        def _(unit=unit, place=place):
+            rest_ref[place] = unit
+
+
+def finish_late(spot, sent, got):
+    rows, width = sent.shape
+    return fold_call(
+        finish_late_kernel, "finish_late", spot, (sent, got),
+        (((3, rows // 2, width), f32), ((rows // 2, width), f32)),
+    )
+
+
 def wide(array):
     return array.astype(f32)
 
@@ -893,20 +1052,20 @@
         info, query_cross, key_cross, value_cross, dc_cross, context_cross, stats_cross
     )
     dz1, do_self, dc_self, sums_first = first_back(info, dz2, dq_cross, total_first, mid, vectors)
+    grads = self_attend_back(info, queries, keys, values, dc_self, context_self, stats_self)
+    memory, *grads = lax.optimization_barrier((memory, *grads))
     *grad_mid, sum_value = mid_weights(
         info, memory, dk_cross, dv_cross, (first_low, dq_cross, context_self, do_self)
     )
-    self_inputs = (queries, keys, values, dc_self, context_self, stats_self)
     cross = (context_cross, do_cross)
     sums = (sums_first, sum_value, sums_ffn, sums_wide)
-    return output, grad_ffn, grad_mid, dz1, self_inputs, dk_cross, dv_cross, cross, sums, mid
+    return output, grad_ffn, grad_mid, dz1, grads, dk_cross, dv_cross, cross, sums, mid
 
 
 def forward_back(target, memory, cotangent, info, pieces, head, mid, tail, vectors):
-    output, grad_ffn, grad_mid, dz1, self_inputs, dk_cross, dv_cross, cross, sums, mid = forward(
+    output, grad_ffn, grad_mid, dz1, grads, dk_cross, dv_cross, cross, sums, mid = forward(
         target, memory, cotangent, info, pieces, head, mid, tail, vectors
     )
-    grads = self_attend_back(info, *self_inputs)
     grad_self = self_weights(info, target, grads, cross, sums)
     target_grad = target_back(info, dz1, grads, head)
     memory_grad = memory_back(info, dk_cross, dv_cross, mid, 0, memory.shape[0])
@@ -1014,19 +1173,19 @@
     head, mid = fence(join_depth(head, depth), mid)
     one, two = cut(head)
     one, two = join_pair(one, 1, side, "fsdp", 1), join_pair(two, 1, high, "dp", 2)
-    one, two, mid, ffn_in, ffn_out = fence(one, two, mid, ffn_in, ffn_out)
+    one, two, mid = fence(one, two, mid)
     one, two = join_pair(one, 2, high, "dp", 2), join_pair(two, 1, side, "fsdp", 1)
+    half = own // 2
+    mine = jnp.concatenate([one, two[:, :, :, :half]], 3).reshape(pieces, 2, own, width)
+    mine, mid, ffn_in, ffn_out = fence(mine, join_depth(mid, depth), ffn_in, ffn_out)
+    got = pair_swap(mine, "dp", 1)
+    vectors = gather_vectors(two[:, :, 0, half:].reshape(pieces, 8, width), own)
+    three, four = cut(mid)
     in_cols = pick(ffn_in.reshape(own, 4, width), 1, dp)
     out_rows = pick(ffn_out.reshape(4, own, width), 0, dp)
     tail = lax.all_gather(
         jnp.concatenate([in_cols, out_rows], 0), ("dp", "fsdp"), axis=0, tiled=True
     ).reshape(4, pieces, 2 * own, width)
-    half = own // 2
-    mine = jnp.concatenate([one, two[:, :, :, :half]], 3).reshape(pieces, 2, own, width)
-    mine, mid = fence(mine, join_depth(mid, depth))
-    got = pair_swap(mine, "dp", 1)
-    vectors = gather_vectors(two[:, :, 0, half:].reshape(pieces, 8, width), own)
-    three, four = cut(mid)
     parts = (three, pair_swap(three, "fsdp", 1), four, pair_swap(four, "dp", 2))
 
     def mid_step(queries, parts):
@@ -1041,98 +1200,71 @@
         return context, (mine, pair_swap(mine, "dp", 1))
 
     head = (mine, got)
-    output, grad_ffn, grad_mid, dz1, self_inputs, dk_cross, dv_cross, cross, sums, mid = forward(
+    output, grad_ffn, grad_mid, dz1, grads, dk_cross, dv_cross, cross, sums, mid = forward(
         target, memory, cotangent, info, pieces, head, parts, tail, vectors, mid_step, mid_last
     )
     sum_ffn = lax.psum_scatter(
         grad_ffn.reshape(-1, width), ("dp", "fsdp"), scatter_dimension=0, tiled=True
     )
-    pairs = width // PAIR
-    by_owner = lambda rows: rows[: 2 * width].reshape(2, 4, 2, own, width)
-    mine, other, queries = fence(*grad_mid, self_inputs[0])
+    spot = jnp.stack([high, core, depth, side])
+    mine, other, target_late = fence(*grad_mid, target)
     got = pair_swap(other, "dp", 1)
-    grads = self_attend_back(info, queries, *self_inputs[1:], first=0, count=pairs // 2)
-    got, *grads = fence(got, *grads)
-    one, two = cut(by_owner(add(mine, got)))
-    one, two, queries = fence(one, two, queries)
-    got_one = pair_swap(pick(one, 0, 1 - high), "dp", 2)
-    got_two = pair_swap(pick(two, 2, 1 - side), "fsdp", 1)
-    grads = self_attend_back(
-        info, queries, *self_inputs[1:], first=pairs // 2, count=pairs // 2, start=tuple(grads)
-    )
-    got_one, got_two, *grads = fence(got_one, got_two, *grads)
-    one, two = add(pick(one, 0, high), got_one), add(pick(two, 2, side), got_two)
-    one, two, target_late = fence(one, two, target)
-    got_one = pair_swap(pick(one, 1, 1 - side), "fsdp", 1)
-    got_two = pair_swap(pick(two, 0, 1 - high), "dp", 2)
-    mine, other = self_weights(info, target_late, grads, cross, sums)
-    got_one, got_two, mine, other = fence(got_one, got_two, mine, other)
-    one, two = add(pick(one, 1, side), got_one), add(pick(two, 0, high), got_two)
-    both = jnp.concatenate([one, two], 1)
-    both, other, dz1 = fence(both, other, dz1)
+    own_part, other = self_weights(info, target_late, grads, cross, sums)
+    got, own_part, other = fence(got, own_part, other)
+    keep_one, send_one, keep_two, send_two = fold_first(spot, mine, got, own)
+    send_one, send_two, other, dz1 = fence(send_one, send_two, other, dz1)
+    got_one, got_two = pair_swap(send_one, "dp", 2), pair_swap(send_two, "fsdp", 1)
     got = pair_swap(other, "dp", 1)
-    rings = [ring(pick(both, 0, (depth + step) % 4), "fsdp", 2 * step) for step in (1, 2, 3)]
     target_grad = target_back(info, dz1, grads, head)
-    got, *rings, target_grad = fence(got, *rings, target_grad)
-    sum_mid = wide(pick(both, 0, depth))
-    for item in rings:
-        sum_mid = sum_mid + wide(item)
-    total = add(mine, got)
-    one, two = cut(by_owner(total))
-    shape = one.shape
-    flat = lambda item: item.reshape(-1, width)
-    vectors = total[2 * width :]
-    keep, send, vectors, two, dk_cross = fence(
-        flat(pick(one, 0, high)), flat(pick(one, 0, 1 - high)), vectors, two, dk_cross
-    )
-    got_one = pair_swap(jnp.concatenate([send, vectors], 0), "dp", 2)
-    got_two = pair_swap(pick(two, 2, 1 - side), "fsdp", 1)
+    got_one, got_two, got, target_grad = fence(got_one, got_two, got, target_grad)
+    keep_one, send_one, keep_two, send_two = fold_second(spot, keep_one, got_one, keep_two, got_two, own)
+    keep_three, send_three, keep_four, send_four = fold_first(spot, own_part, got, own)
+    send_one, send_two, send_three, send_four, dk_cross = fence(
+        send_one, send_two, send_three, send_four, dk_cross
+    )
+    got_one, got_two = pair_swap(send_one, "fsdp", 1), pair_swap(send_two, "dp", 2)
+    got_three, got_four = pair_swap(send_three, "dp", 2), pair_swap(send_four, "fsdp", 1)
     memory_grad = memory_back(info, dk_cross, dv_cross, mid, 0, count // 2)
-    got_one, got_two, memory_grad = fence(got_one, got_two, memory_grad)
-    one = add(keep, got_one[:-VECTORS]).reshape(4, 2, -1, width)
-    vectors = add(vectors, got_one[-VECTORS:])
-    two = add(pick(two, 2, side), got_two)
-    keep, send, vectors, two, dk_cross = fence(
-        flat(pick(one, 1, side)), flat(pick(one, 1, 1 - side)), vectors, two, dk_cross
-    )
-    got_one = pair_swap(jnp.concatenate([send, vectors], 0), "fsdp", 1)
-    got_two = pair_swap(pick(two, 0, 1 - high), "dp", 2)
+    got_one, got_two, got_three, got_four, memory_grad = fence(
+        got_one, got_two, got_three, got_four, memory_grad
+    )
+    sum_mid, *sends = fold_third(spot, keep_one, got_one, keep_two, got_two, own)
+    keep_three, send_three, keep_four, send_four = fold_second(
+        spot, keep_three, got_three, keep_four, got_four, own
+    )
+    *sends, send_three, send_four, dk_cross = fence(*sends, send_three, send_four, dk_cross)
+    rings = [ring(item, "fsdp", 2 * step) for step, item in zip((1, 2, 3), sends)]
+    got_three, got_four = pair_swap(send_three, "fsdp", 1), pair_swap(send_four, "dp", 2)
     memory_grad = memory_back(
         info, dk_cross, dv_cross, mid, count // 2, count - count // 2, start=(memory_grad,)
     )
-    got_one, got_two, memory_grad = fence(got_one, got_two, memory_grad)
-    one = add(keep, got_one[:-VECTORS]).reshape(4, -1, width)
-    vectors = add(vectors, got_one[-VECTORS:])
-    two = add(pick(two, 0, high), got_two)
-    both = jnp.concatenate([one, two], 1)
-    early = jnp.concatenate([sum_ffn, sum_mid.astype(bf16)], 0)
-    both, vectors, early = fence(both, vectors, early)
-    rings = [
-        ring(jnp.concatenate([pick(both, 0, (depth + step) % 4), vectors], 0), "fsdp", 2 * step)
-        for step in (1, 2, 3)
-    ]
-    early = join_pair(early, 0, high, "dp", 2)
-    early, *rings = fence(early, *rings)
-    late = jnp.concatenate([pick(both, 0, depth), vectors], 0)
-    late = wide(late)
-    for item in rings:
-        late = late + wide(item)
-    vectors = late[-VECTORS:][:17]
-    late = join_pair(late[:-VECTORS].astype(bf16), 0, high, "dp", 2)
-    early = join_pair(early, 1, core, "dp", 1)
+    got_three, got_four, memory_grad, *rings = fence(got_three, got_four, memory_grad, *rings)
+    sum_mid = added(sum_mid, *rings).astype(bf16)
+    early = jnp.concatenate([sum_ffn, sum_mid], 0)
+    sum_self, *sends = fold_third(spot, keep_three, got_three, keep_four, got_four, own)
+    *sends, early = fence(*sends, early)
+    rings = [ring(item, "fsdp", 2 * step) for step, item in zip((1, 2, 3), sends)]
+    got = pair_swap(early, "dp", 2)
+    got, *rings = fence(got, *rings)
+    late = added(sum_self, *rings)
+    vectors = late[-VECTORS:]
+    late = late[:-VECTORS].astype(bf16)
+    early = jnp.concatenate([early, got], 0)
     early, late = fence(early, late)
-    late = join_pair(late, 1, core, "dp", 1)
-    early = wide(early.reshape((4,) + early.shape[2:]))
-    late = wide(late.reshape((4,) + late.shape[2:]))
-    grad_in = jnp.swapaxes(early[:, :own], 0, 1).reshape(own, 4 * width)
-    grad_out = early[:, own : 2 * own].reshape(4 * own, width)
-    mid = early[:, 2 * own :]
+    got_early = pair_swap(early, "dp", 1)
+    got = pair_swap(late, "dp", 2)
+    late = jnp.concatenate([late, got], 0)
+    late, got_early = fence(late, got_early)
+    got = pair_swap(late, "dp", 1)
+    grad_in, grad_out, grad_self_out, grad_cross_qkv = finish_early(spot, early, got_early, own)
     place = lax.axis_index("fsdp")
     hidden = pick(vectors[6:10].reshape(pieces, 4 * own), 0, place)
     vectors = lax.dynamic_slice_in_dim(vectors, place * own, own, 1)
+    got, grad_in, hidden, vectors = fence(got, grad_in, hidden, vectors)
+    grad_self_qkv, grad_cross_out = finish_late(spot, late, got)
     return (
-        output, target_grad, memory_grad, late[:3], mid[0], vectors[:3], mid[1:], late[3], vectors[3:6],
-        grad_in, hidden, grad_out, vectors[10], vectors[11:14], vectors[14:17],
+        output, target_grad, memory_grad, grad_self_qkv, grad_self_out, vectors[:3], grad_cross_qkv,
+        grad_cross_out, vectors[3:6], grad_in, hidden, grad_out, vectors[10], vectors[11:14], vectors[14:17],
     )
 
 

time: 432 us -> 428 us (level)
  Pallas kernels: 249 us -> 269 us
  starting transfers between devices: 44.4 us -> 33 us
  other arithmetic: 16 us -> 6.67 us
    pallas_call x10 -> x18, Pallas kernels: 149 us -> 165 us  [row_call(): pl.pallas_call(kernel, grid_spec=pltpu.PrefetchScalarGridSpec(num_scalar_...]
    ppermute x24, starting transfers between devices: 31 us -> 22.2 us  [pair_swap(): lax.ppermute(array, axis, [(place, place ^ bit) for place in range(count)])]
    convert_element_type x13 -> x1, other arithmetic: 7.72 us -> 0.08 us  [fast_layer(): sum_mid = added(sum_mid, *rings).astype(bf16)]
    pallas_call x5 -> x4, Pallas kernels: 85.7 us -> 88.9 us  [attend_call(): pl.pallas_call(functools.partial(kernel, len(start)), grid_spec=pltpu.Pre...]
  transfers between devices with their start and end apart: 38 -> 38, of which waited for: 23 -> 21; matrix products, arithmetic and copies ran while one was open for 5% -> 1% of each run, Pallas kernels for 46% -> 51%
where the time goes in v3:
time: 428 us; the launch traced here: 423 us
  Pallas kernels  269 us (63%)
  waiting for transfers between devices  85.1 us (20%)
  starting transfers between devices  33 us (8%)
  between operations  15.6 us (4%)
  local copies, waits for them, and re-layouts  14.1 us (3%)
  other arithmetic  6.67 us (2%)
    pallas_call x18, Pallas kernels, row_call(): pl.pallas_call(kernel, grid_spec=pltpu.PrefetchScalarGridSpec(num_scalar_...  165 us
    pallas_call x4, Pallas kernels, attend_call(): pl.pallas_call(functools.partial(kernel, len(start)), grid_spec=pltpu.Pre...  88.9 us
    ppermute x12, waiting for transfers between devices, ring(): lax.ppermute(array, axis, [(place, (place + shift) % count) for place in...  42.7 us
    ppermute x24, waiting for transfers between devices, pair_swap(): lax.ppermute(array, axis, [(place, place ^ bit) for place in range(count)])  42.3 us
    ppermute x24, starting transfers between devices, pair_swap(): lax.ppermute(array, axis, [(place, place ^ bit) for place in range(count)])  22.2 us
    pallas_call x1, Pallas kernels, ffn_weights(): pl.pallas_call(ffn_weights_kernel, grid=(blocks,), in_specs=[whole, part,...  14.6 us
    ppermute x12, starting transfers between devices, ring(): lax.ppermute(array, axis, [(place, (place + shift) % count) for place in...  10.6 us
  transfers between devices with their start and end apart: 38, of which 21 were waited for; matrix products, arithmetic and copies ran while one was open for 1% of the time, Pallas kernels for 51%

profile of v3, /device:TPU:9, one launch (start us, length us, event | category | flops | bytes accessed | tf_op | source)
XLA Modules:
  0.0 423.1 jit_solution(10840979872035910885)
XLA Ops:
  17.6 9.3 %collective-permute-done.1 = bf16[104,768]{1,0:T(8,128)(2,1)S(1)} collective-permute-done((bf16[104,768]{1,0:T(8,128)(2,1)S(1)}, bf16[104,768]{1,0:T(8,128)(2,1)S(1)}, u32[]{:S(2)}, u32[]{:S(2)}) %collective-permute-start.1) | collective-permute-done | bytes 159776 | tf_op jit(solution)/shard_map/ppermute | solution.py:1082
  32.4 5.5 %collective-permute-done.3 = bf16[4,48,768]{2,1,0:T(8,128)(2,1)S(1)} collective-permute-done((bf16[4,48,768]{2,1,0:T(8,128)(2,1)S(1)}, bf16[4,48,768]{2,1,0:T(8,128)(2,1)S(1)}, u32[]{:S(2)}, u32[]{:S(2)}) %collective-permute-start.3) | collective-permute-done | bytes 294944 | tf_op jit(solution)/shard_map/ppermute | solution.py:1077
  47.1 7.5 %collective-permute-done.9 = bf16[96,768]{1,0:T(8,128)(2,1)S(1)} collective-permute-done((bf16[96,768]{1,0:T(8,128)(2,1)S(1)}, bf16[96,768]{1,0:T(8,128)(2,1)S(1)}, u32[]{:S(2)}, u32[]{:S(2)}) %collective-permute-start.9) | collective-permute-done | bytes 147488 | tf_op jit(solution)/shard_map/ppermute | solution.py:1082
  69.3 8.8 %project_self.1 = (bf16[1024,768]{1,0:T(8,128)(2,1)}, bf16[1024,768]{1,0:T(8,128)(2,1)}, bf16[1024,768]{1,0:T(8,128)(2,1)}) custom-call(s32[6]{0:T(128)} %pad_add_fusion.info, bf16[1024,768]{1,0:T(8,128)(2,1)} %x_hbm, bf16[8,2,96,768]{3,2,1,0:T(8,128)(2,1)} %bitcast.101, bf16[8,2,96,768]{3,2,1,0:T(8,128)(2,1)} %collective-permute-done.10.got, ...), custom_call_target="tpu_custom_call" | custom-call | flops 4831838208 | bytes 8388608 | tf_op jit(solution)/shard_map/project_self/pallas_call | solution.py:398
  79.9 9.5 %self_attend.1 = (bf16[1024,768]{1,0:T(8,128)(2,1)}, f32[6,4,1,512]{3,2,1,0:T(1,128)}) custom-call(s32[6]{0:T(128)} %pad_add_fusion.info, bf16[1024,768]{1,0:T(8,128)(2,1)} %get-tuple-element.165.q_ref, bf16[1024,768]{1,0:T(8,128)(2,1)} %get-tuple-element.166.k_ref, bf16[1024,768]{1,0:T(8,128)(2,1)} %get-tuple-element.167.v_ref), custom_call_target="tpu_custom_call" | custom-call | flops 19327352832 | bytes 8388608 | tf_op jit(solution)/shard_map/self_attend/pallas_call | solution.py:288
  97.7 4.3 %collective-permute-done.15.got = bf16[8,2,96,768]{3,2,1,0:T(8,128)(2,1)} collective-permute-done((bf16[8,2,96,768]{3,2,1,0:T(8,128)(2,1)S(1)}, bf16[8,2,96,768]{3,2,1,0:T(8,128)(2,1)}, u32[]{:S(2)}, u32[]{:S(2)}) %collective-permute-start.15) | collective-permute-done | bytes 2359328 | tf_op jit(solution)/shard_map/ppermute | solution.py:1077
  102.0 9.5 %first_norm.1 = (f32[1024,768]{1,0:T(8,128)}, bf16[1024,768]{1,0:T(8,128)(2,1)}, bf16[1024,768]{1,0:T(8,128)(2,1)}) custom-call(s32[6]{0:T(128)} %pad_add_fusion.info, bf16[1024,768]{1,0:T(8,128)(2,1)} %x_hbm, bf16[1024,768]{1,0:T(8,128)(2,1)} %get-tuple-element.173.c_ref.o_ref.self_ref, bf16[8,2,96,768]{3,2,1,0:T(8,128)(2,1)} %bitcast.94, ...), custom_call_target="tpu_custom_call" | custom-call | flops 4831838208 | bytes 8388608 | tf_op jit(solution)/shard_map/first_norm/pallas_call | solution.py:398
  111.5 16.3 %project_memory.1 = (bf16[4,1024,768]{2,1,0:T(8,128)(2,1)}, bf16[4,1024,768]{2,1,0:T(8,128)(2,1)}) custom-call(s32[6]{0:T(128)} %pad_add_fusion.info, bf16[4,1024,768]{2,1,0:T(8,128)(2,1)} %m_ref.2, bf16[8,2,96,768]{3,2,1,0:T(8,128)(2,1)} %bitcast.95, bf16[8,2,96,768]{3,2,1,0:T(8,128)(2,1)} %collective-permute-done.15.got, ...), custom_call_target="tpu_custom_call" | custom-call | flops 9663676416 | bytes 8388608 | tf_op jit(solution)/shard_map/project_memory/pallas_call | solution.py:398
  127.8 29.0 %cross_attend.1 = (bf16[1024,768]{1,0:T(8,128)(2,1)}, f32[6,4,1,512]{3,2,1,0:T(1,128)}) custom-call(s32[6]{0:T(128)} %pad_add_fusion.info, bf16[1024,768]{1,0:T(8,128)(2,1)} %get-tuple-element.179.q_ref, bf16[4,1024,768]{2,1,0:T(8,128)(2,1)} %get-tuple-element.180.k_ref, bf16[4,1024,768]{2,1,0:T(8,128)(2,1)} %get-tuple-element.181.v_ref), custom_call_target="tpu_custom_call" | custom-call | flops 19327352832 | bytes 8388608 | tf_op jit(solution)/shard_map/cross_attend/pallas_call | solution.py:288
  156.8 38.5 %ffn_block.1 = (bf16[1024,768]{1,0:T(8,128)(2,1)}, bf16[1024,768]{1,0:T(8,128)(2,1)}, bf16[1024,3072]{1,0:T(8,128)(2,1)}, bf16[1024,3072]{1,0:T(8,128)(2,1)}, bf...) custom-call(s32[6]{0:T(128)} %pad_add_fusion.info, ...), custom_call_target="tpu_custom_call" | custom-call | flops 38654705664 | bytes 8388608 | tf_op jit(solution)/shard_map/ffn_block/pallas_call | solution.py:398
  195.3 14.6 %ffn_weights.1 = bf16[4,8,192,768]{3,2,1,0:T(8,128)(2,1)} custom-call(bf16[1024,768]{1,0:T(8,128)(2,1)} %get-tuple-element.268.h_ref, bf16[1024,3072]{1,0:T(8,128)(2,1)} %get-tuple-element.269.du_ref, bf16[1024,3072]{1,0:T(8,128)(2,1)} %get-tuple-element.270.a_ref, bf16[1024,768]{1,0:T(8,128)(2,1)} %get-tuple-element.271.df_ref), custom_call_target="tpu_custom_call" | custom-call | flops 9663676416 | bytes 8388608 | tf_op jit(solution)/shard_map/ffn_weights/pallas_call | solution.py:854
  209.9 37.5 %cross_attend_back.1 = (bf16[1024,768]{1,0:T(8,128)(2,1)}, bf16[4,1024,768]{2,1,0:T(8,128)(2,1)}, bf16[4,1024,768]{2,1,0:T(8,128)(2,1)}) custom-call(s32[6]{0:T(128)} %pad_add_fusion.info, bf16[1024,768]{1,0:T(8,128)(2,1)} %get-tuple-element.179.q_ref, bf16[4,1024,768]{2,1,0:T(8,128)(2,1)} %get-tuple-element.180.k_ref, ...), custom_call_target="tpu_custom_call" | custom-call | flops 38654705664 | bytes 8388608 | tf_op jit(solution)/shard_map/cross_attend_back/pallas_call | solution.py:288
  247.4 10.4 %first_back.1 = (f32[1024,768]{1,0:T(8,128)}, bf16[1024,768]{1,0:T(8,128)(2,1)}, bf16[1024,768]{1,0:T(8,128)(2,1)}, f32[8,768]{1,0:T(8,128)}) custom-call(s32[6]{0:T(128)} %pad_add_fusion.info, f32[1024,768]{1,0:T(8,128)} %get-tuple-element.186.dz2_ref, bf16[1024,768]{1,0:T(8,128)(2,1)} %get-tuple-element.189.dq_ref, f32[1024,768]{1,0:T(8,128)} %get-tuple-element.178.z_ref, ...), custom_call_target="tpu_custom_call" | custom-call | flops 4831838208 | bytes 8388608 | tf_op jit(solution)/shard_map/first_back/pallas_call | solution.py:398
  257.8 12.9 %self_attend_back.1 = (bf16[1024,768]{1,0:T(8,128)(2,1)}, bf16[1024,768]{1,0:T(8,128)(2,1)}, bf16[1024,768]{1,0:T(8,128)(2,1)}) custom-call(s32[6]{0:T(128)} %pad_add_fusion.info, bf16[1024,768]{1,0:T(8,128)(2,1)} %get-tuple-element.165.q_ref, bf16[1024,768]{1,0:T(8,128)(2,1)} %get-tuple-element.166.k_ref, bf16[1024,768]{1,0:T(8,128)(2,1)} %get-tuple-element.167.v_ref, ...), custom_call_target="tpu_custom_call" | custom-call | flops 38654705664 | bytes 8388608 | tf_op jit(solution)/shard_map/self_attend_back/pallas_call | solution.py:288
  270.7 21.9 %mid_weights.1 = (bf16[1536,768]{1,0:T(8,128)(2,1)}, bf16[1536,768]{1,0:T(8,128)(2,1)}, f32[1,768]{1,0:T(1,128)}) custom-call(s32[6]{0:T(128)} %pad_add_fusion.info, bf16[4,1024,768]{2,1,0:T(8,128)(2,1)} %m_ref.2, bf16[4,1024,768]{2,1,0:T(8,128)(2,1)} %get-tuple-element.255.dk_ref, bf16[4,1024,768]{2,1,0:T(8,128)(2,1)} %get-tuple-element.197.dv_ref, ...), custom_call_target="tpu_custom_call" | custom-call | flops 9663676416 | bytes 8388608 | tf_op jit(solution)/shard_map/mid_weights/pallas_call | solution.py:398
  292.8 11.9 %self_weights.1 = (bf16[1568,768]{1,0:T(8,128)(2,1)}, bf16[1568,768]{1,0:T(8,128)(2,1)}) custom-call(s32[6]{0:T(128)} %pad_add_fusion.info, bf16[1024,768]{1,0:T(8,128)(2,1)} %x_hbm, bf16[1024,768]{1,0:T(8,128)(2,1)} %get-tuple-element.205.q_hbm.q_ref, bf16[1024,768]{1,0:T(8,128)(2,1)} %get-tuple-element.206.k_hbm.k_ref, ...), custom_call_target="tpu_custom_call" | custom-call | flops 4831838208 | bytes 8388608 | tf_op jit(solution)/shard_map/self_weights/pallas_call | solution.py:398
  309.7 10.1 %target_back.1 = f32[1024,768]{1,0:T(8,128)} custom-call(s32[6]{0:T(128)} %pad_add_fusion.info, f32[1024,768]{1,0:T(8,128)} %get-tuple-element.223.z_ref, bf16[1024,768]{1,0:T(8,128)(2,1)} %get-tuple-element.205.q_hbm.q_ref, bf16[1024,768]{1,0:T(8,128)(2,1)} %get-tuple-element.206.k_hbm.k_ref, bf16[1024,768]{1,0:T(8,128)(2,1)} %get-tuple-element.207.v_hbm.v_ref, ...), custom_call_target="tpu_custom_call" | custom-call | flops 4831838208 | bytes 8388608 | tf_op jit(solution)/shard_map/target_back/pallas_call | solution.py:398
  319.8 10.0 %collective-permute-done.17.got_a = bf16[384,768]{1,0:T(8,128)(2,1)S(1)} collective-permute-done((bf16[384,768]{1,0:T(8,128)(2,1)}, bf16[384,768]{1,0:T(8,128)(2,1)S(1)}, u32[]{:S(2)}, u32[]{:S(2)}) %collective-permute-start.17) | collective-permute-done | bytes 589856 | tf_op jit(solution)/shard_map/ppermute | solution.py:1077
  340.0 10.4 %memory_back.2.refs_0_ = f32[4,1024,768]{2,1,0:T(8,128)} custom-call(s32[6]{0:T(128)} %pad_add_fusion.info, bf16[4,1024,768]{2,1,0:T(8,128)(2,1)} %get-tuple-element.255.dk_ref, bf16[4,1024,768]{2,1,0:T(8,128)(2,1)} %get-tuple-element.197.dv_ref, bf16[8,2,96,768]{3,2,1,0:T(8,128)(2,1)} %bitcast.97, bf16[8,2,96,768]{3,2,1,0:T(8,128)(2,1)} %collective-permute-done.15.got), custom_call_target="tpu_custom_call" | custom-call | flops 4831838208 | bytes 8388608 | tf_op jit(solution)/shard_map/memory_back/pallas_call | solution.py:398
  350.5 9.7 %collective-permute-done.20.got_a = bf16[192,768]{1,0:T(8,128)(2,1)S(1)} collective-permute-done((bf16[192,768]{1,0:T(8,128)(2,1)S(1)}, bf16[192,768]{1,0:T(8,128)(2,1)S(1)}, u32[]{:S(2)}, u32[]{:S(2)}) %collective-permute-start.20) | collective-permute-done | bytes 294944 | tf_op jit(solution)/shard_map/ppermute | solution.py:1077
  368.5 10.6 %memory_back.3 = f32[4,1024,768]{2,1,0:T(8,128)} custom-call(s32[6]{0:T(128)} %pad_add_fusion.info, bf16[4,1024,768]{2,1,0:T(8,128)(2,1)} %get-tuple-element.255.dk_ref, bf16[4,1024,768]{2,1,0:T(8,128)(2,1)} %get-tuple-element.197.dv_ref, bf16[8,2,96,768]{3,2,1,0:T(8,128)(2,1)} %bitcast.98, ...), custom_call_target="tpu_custom_call", output_to_operand_aliasing={{}: (5, {})} | custom-call | flops 4831838208 | bytes 8388608 | tf_op jit(solution)/shard_map/memory_back/pallas_call | solution.py:398
  388.2 10.7 %collective-permute-done.31 = bf16[128,768]{1,0:T(8,128)(2,1)S(1)} collective-permute-done((bf16[128,768]{1,0:T(8,128)(2,1)S(1)}, bf16[128,768]{1,0:T(8,128)(2,1)S(1)}, u32[]{:S(2)}, u32[]{:S(2)}) %collective-permute-start.31) | collective-permute-done | bytes 196640 | tf_op jit(solution)/shard_map/ppermute | solution.py:1082
  399.0 3.8 collective-permute-done.32
  404.3 4.7 %collective-permute-done.33 = bf16[96,768]{1,0:T(8,128)(2,1)S(1)} collective-permute-done((bf16[96,768]{1,0:T(8,128)(2,1)S(1)}, bf16[96,768]{1,0:T(8,128)(2,1)S(1)}, u32[]{:S(2)}, u32[]{:S(2)}) %collective-permute-start.33) | collective-permute-done | bytes 147488 | tf_op jit(solution)/shard_map/ppermute | solution.py:1077
  (180 shorter events, 89.8 us)
Async XLA Ops:
  7.2 149.6 %all-gather.2.cloned.1.call-start = ((), (), s32[]{:S(2)}) async-start(), calls=%async_computation.1 | async-start | bytes 9732096 | tf_op jit(solution)/shard_map/all_gather | solution.py:1186
  13.9 13.0 %collective-permute-start.1 = (bf16[104,768]{1,0:T(8,128)(2,1)S(1)}, bf16[104,768]{1,0:T(8,128)(2,1)S(1)}, u32[]{:S(2)}, u32[]{:S(2)}) collective-permute-start(bf16[104,768]{1,0:T(8,128)(2,1)S(1)} %fusion.3), channel_id=1, source_target_pairs={{0,4},{1,5},{2,6},{3,7},{4,0},{5,1},{6,2},{7,3},{8,12},{9,13},{10,... | collective-permute-start | bytes 479240 | tf_op jit(solution)/shard_map/ppermute | solution.py:1082
  15.0 14.8 %collective-permute-start.2 = (bf16[104,768]{1,0:T(8,128)(2,1)S(1)}, bf16[104,768]{1,0:T(8,128)(2,1)S(1)}, u32[]{:S(2)}, u32[]{:S(2)}) collective-permute-start(bf16[104,768]{1,0:T(8,128)(2,1)S(1)} %fusion.3), channel_id=1, source_target_pairs={{0,6},{1,7},{2,0},{3,1},{4,2},{5,3},{6,4},{7,5},{8,14},{9,15},{10,... | collective-permute-start | bytes 479240 | tf_op jit(solution)/shard_map/ppermute | solution.py:1082
  40.3 14.3 %collective-permute-start.9 = (bf16[96,768]{1,0:T(8,128)(2,1)S(1)}, bf16[96,768]{1,0:T(8,128)(2,1)S(1)}, u32[]{:S(2)}, u32[]{:S(2)}) collective-permute-start(bf16[96,768]{1,0:T(8,128)(2,1)S(1)} %fusion.5), channel_id=1, source_target_pairs={{0,6},{1,7},{2,0},{3,1},{4,2},{5,3},{6,4},{7,5},{8,14},{9,15},{10,... | collective-permute-start | bytes 442376 | tf_op jit(solution)/shard_map/ppermute | solution.py:1082
  41.6 14.1 %collective-permute-start.6 = (bf16[4,2,56,768]{3,2,0,1:T(8,128)(2,1)S(1)}, bf16[4,2,56,768]{3,2,0,1:T(8,128)(2,1)S(1)}, u32[]{:S(2)}, u32[]{:S(2)}) collective-permute-start(bf16[4,2,56,768]{3,2,0,1:T(8,128)(2,1)S(1)} %pad_maximum_fusion.2), channel_id=1, source_target_pairs={{0,1},{1,0},{2,3},{3,2},{4,5},{5,4},{6,7},{7,6},{8,9},{9,8},{10,11... | collective-permute-start | bytes 2064392 | tf_op jit(solution)/shard_map/ppermute | solution.py:1077
  41.9 12.7 %collective-permute-start.5 = (bf16[4,2,48,768]{3,2,1,0:T(8,128)(2,1)S(1)}, bf16[4,2,48,768]{3,2,1,0:T(8,128)(2,1)S(1)}, u32[]{:S(2)}, u32[]{:S(2)}) collective-permute-start(bf16[4,2,48,768]{3,2,1,0:T(8,128)(2,1)S(1)} %pad_maximum_fusion.3), channel_id=1, source_target_pairs={{0,16},{8,24},{16,0},{24,8},{1,17},{9,25},{17,1},{25,9},{2,18},{10... | collective-permute-start | bytes 1769480 | tf_op jit(solution)/shard_map/ppermute | solution.py:1077
  60.7 320.5 %reduce-scatter.2.cloned.1.call-start = ((), (), s32[]{:S(2)}) async-start(), calls=%async_computation.2 | async-start | bytes 9732096 | tf_op jit(solution)/shard_map/reduce_scatter | solution.py:1206
  78.3 14.6 %collective-permute-start.14 = (bf16[4,2,48,768]{3,2,0,1:T(8,128)(2,1)S(1)}, bf16[4,2,48,768]{3,2,0,1:T(8,128)(2,1)S(1)}, u32[]{:S(2)}, u32[]{:S(2)}) collective-permute-start(bf16[4,2,48,768]{3,2,0,1:T(8,128)(2,1)S(1)} %pad_maximum_fusion.5), channel_id=1, source_target_pairs={{0,1},{1,0},{2,3},{3,2},{4,5},{5,4},{6,7},{7,6},{8,9},{9,8},{10,11... | collective-permute-start | bytes 1769480 | tf_op jit(solution)/shard_map/ppermute | solution.py:1077
  79.4 14.0 %collective-permute-start.13 = (bf16[4,2,48,768]{3,2,0,1:T(8,128)(2,1)S(1)}, bf16[4,2,48,768]{3,2,0,1:T(8,128)(2,1)S(1)}, u32[]{:S(2)}, u32[]{:S(2)}) collective-permute-start(bf16[4,2,48,768]{3,2,0,1:T(8,128)(2,1)S(1)} %pad_maximum_fusion.4), channel_id=1, source_target_pairs={{0,16},{8,24},{16,0},{24,8},{1,17},{9,25},{17,1},{25,9},{2,18},{10... | collective-permute-start | bytes 1769480 | tf_op jit(solution)/shard_map/ppermute | solution.py:1077
  292.6 12.1 %collective-permute-start.16 = (bf16[1536,768]{1,0:T(8,128)(2,1)}, bf16[1536,768]{1,0:T(8,128)(2,1)}, u32[]{:S(2)}, u32[]{:S(2)}) collective-permute-start(bf16[1536,768]{1,0:T(8,128)(2,1)} %get-tuple-element.203), channel_id=1, source_target_pairs={{0,8},{8,0},{16,24},{24,16},{1,9},{9,1},{17,25},{25,17},{2,10},{10... | collective-permute-start | bytes 7077896 | tf_op jit(solution)/shard_map/ppermute | solution.py:1077
  309.2 21.5 %collective-permute-start.19 = (bf16[1568,768]{1,0:T(8,128)(2,1)}, bf16[1568,768]{1,0:T(8,128)(2,1)}, u32[]{:S(2)}, u32[]{:S(2)}) collective-permute-start(bf16[1568,768]{1,0:T(8,128)(2,1)} %get-tuple-element.222), channel_id=1, source_target_pairs={{0,8},{8,0},{16,24},{24,16},{1,9},{9,1},{17,25},{25,17},{2,10},{10... | collective-permute-start | bytes 7225352 | tf_op jit(solution)/shard_map/ppermute | solution.py:1077
  309.7 20.2 %collective-permute-start.17 = (bf16[384,768]{1,0:T(8,128)(2,1)}, bf16[384,768]{1,0:T(8,128)(2,1)S(1)}, u32[]{:S(2)}, u32[]{:S(2)}) collective-permute-start(bf16[384,768]{1,0:T(8,128)(2,1)} %get-tuple-element.220), channel_id=1, source_target_pairs={{0,16},{8,24},{16,0},{24,8},{1,17},{9,25},{17,1},{25,9},{2,18},{10... | collective-permute-start | bytes 1769480 | tf_op jit(solution)/shard_map/ppermute | solution.py:1077
  309.7 21.0 %collective-permute-start.18 = (bf16[384,768]{1,0:T(8,128)(2,1)}, bf16[384,768]{1,0:T(8,128)(2,1)}, u32[]{:S(2)}, u32[]{:S(2)}) collective-permute-start(bf16[384,768]{1,0:T(8,128)(2,1)} %get-tuple-element.221), channel_id=1, source_target_pairs={{0,1},{1,0},{2,3},{3,2},{4,5},{5,4},{6,7},{7,6},{8,9},{9,8},{10,11... | collective-permute-start | bytes 1769480 | tf_op jit(solution)/shard_map/ppermute | solution.py:1077
  337.1 24.7 %collective-permute-start.22 = (bf16[416,768]{1,0:T(8,128)(2,1)}, bf16[416,768]{1,0:T(8,128)(2,1)S(1)}, u32[]{:S(2)}, u32[]{:S(2)}) collective-permute-start(bf16[416,768]{1,0:T(8,128)(2,1)} %get-tuple-element.238), channel_id=1, source_target_pairs={{0,16},{8,24},{16,0},{24,8},{1,17},{9,25},{17,1},{25,9},{2,18},{10... | collective-permute-start | bytes 1916936 | tf_op jit(solution)/shard_map/ppermute | solution.py:1077
  337.4 24.4 %collective-permute-start.23 = (bf16[384,768]{1,0:T(8,128)(2,1)}, bf16[384,768]{1,0:T(8,128)(2,1)S(1)}, u32[]{:S(2)}, u32[]{:S(2)}) collective-permute-start(bf16[384,768]{1,0:T(8,128)(2,1)} %get-tuple-element.239), channel_id=1, source_target_pairs={{0,1},{1,0},{2,3},{3,2},{4,5},{5,4},{6,7},{7,6},{8,9},{9,8},{10,11... | collective-permute-start | bytes 1769480 | tf_op jit(solution)/shard_map/ppermute | solution.py:1077
  337.4 22.7 %collective-permute-start.20 = (bf16[192,768]{1,0:T(8,128)(2,1)S(1)}, bf16[192,768]{1,0:T(8,128)(2,1)S(1)}, u32[]{:S(2)}, u32[]{:S(2)}) collective-permute-start(bf16[192,768]{1,0:T(8,128)(2,1)S(1)} %get-tuple-element.236), channel_id=1, source_target_pairs={{0,1},{1,0},{2,3},{3,2},{4,5},{5,4},{6,7},{7,6},{8,9},{9,8},{10,11... | collective-permute-start | bytes 884744 | tf_op jit(solution)/shard_map/ppermute | solution.py:1077
  338.9 22.2 %collective-permute-start.21 = (bf16[192,768]{1,0:T(8,128)(2,1)S(1)}, bf16[192,768]{1,0:T(8,128)(2,1)S(1)}, u32[]{:S(2)}, u32[]{:S(2)}) collective-permute-start(bf16[192,768]{1,0:T(8,128)(2,1)S(1)} %get-tuple-element.237), channel_id=1, source_target_pairs={{0,16},{8,24},{16,0},{24,8},{1,17},{9,25},{17,1},{25,9},{2,18},{10... | collective-permute-start | bytes 884744 | tf_op jit(solution)/shard_map/ppermute | solution.py:1077
  364.1 16.3 %collective-permute-start.24 = (bf16[224,768]{1,0:T(8,128)(2,1)}, bf16[224,768]{1,0:T(8,128)(2,1)S(1)}, u32[]{:S(2)}, u32[]{:S(2)}) collective-permute-start(bf16[224,768]{1,0:T(8,128)(2,1)} %get-tuple-element.253), channel_id=1, source_target_pairs={{0,1},{1,0},{2,3},{3,2},{4,5},{5,4},{6,7},{7,6},{8,9},{9,8},{10,11... | collective-permute-start | bytes 1032200 | tf_op jit(solution)/shard_map/ppermute | solution.py:1077
  364.2 16.2 %collective-permute-start.25 = (bf16[192,768]{1,0:T(8,128)(2,1)}, bf16[192,768]{1,0:T(8,128)(2,1)S(1)}, u32[]{:S(2)}, u32[]{:S(2)}) collective-permute-start(bf16[192,768]{1,0:T(8,128)(2,1)} %get-tuple-element.254), channel_id=1, source_target_pairs={{0,16},{8,24},{16,0},{24,8},{1,17},{9,25},{17,1},{25,9},{2,18},{10... | collective-permute-start | bytes 884744 | tf_op jit(solution)/shard_map/ppermute | solution.py:1077
  364.7 14.5 %collective-permute-start.26 = (bf16[96,768]{1,0:T(8,128)(2,1)S(1)}, bf16[96,768]{1,0:T(8,128)(2,1)S(1)}, u32[]{:S(2)}, u32[]{:S(2)}) collective-permute-start(bf16[96,768]{1,0:T(8,128)(2,1)S(1)} %get-tuple-element.257), channel_id=1, source_target_pairs={{0,2},{1,3},{2,4},{3,5},{4,6},{5,7},{6,0},{7,1},{8,10},{9,11},{10,... | collective-permute-start | bytes 442376 | tf_op jit(solution)/shard_map/ppermute | solution.py:1082
  366.4 12.8 %collective-permute-start.27 = (bf16[96,768]{1,0:T(8,128)(2,1)S(1)}, bf16[96,768]{1,0:T(8,128)(2,1)S(1)}, u32[]{:S(2)}, u32[]{:S(2)}) collective-permute-start(bf16[96,768]{1,0:T(8,128)(2,1)S(1)} %get-tuple-element.258), channel_id=1, source_target_pairs={{0,4},{1,5},{2,6},{3,7},{4,0},{5,1},{6,2},{7,3},{8,12},{9,13},{10,... | collective-permute-start | bytes 442376 | tf_op jit(solution)/shard_map/ppermute | solution.py:1082
  382.2 20.6 %collective-permute-start.29 = (bf16[288,768]{1,0:T(8,128)(2,1)S(1)}, bf16[288,768]{1,0:T(8,128)(2,1)S(1)}, u32[]{:S(2)}, u32[]{:S(2)}) collective-permute-start(bf16[288,768]{1,0:T(8,128)(2,1)S(1)} %pad_maximum_fusion.6), channel_id=1, source_target_pairs={{0,16},{8,24},{16,0},{24,8},{1,17},{9,25},{17,1},{25,9},{2,18},{10... | collective-permute-start | bytes 1327112 | tf_op jit(solution)/shard_map/ppermute | solution.py:1077
  383.4 15.6 %collective-permute-start.31 = (bf16[128,768]{1,0:T(8,128)(2,1)S(1)}, bf16[128,768]{1,0:T(8,128)(2,1)S(1)}, u32[]{:S(2)}, u32[]{:S(2)}) collective-permute-start(bf16[128,768]{1,0:T(8,128)(2,1)S(1)} %get-tuple-element.278), channel_id=1, source_target_pairs={{0,4},{1,5},{2,6},{3,7},{4,0},{5,1},{6,2},{7,3},{8,12},{9,13},{10,... | collective-permute-start | bytes 589832 | tf_op jit(solution)/shard_map/ppermute | solution.py:1082
  384.8 18.0 %collective-permute-start.32 = (bf16[128,768]{1,0:T(8,128)(2,1)S(1)}, bf16[128,768]{1,0:T(8,128)(2,1)S(1)}, u32[]{:S(2)}, u32[]{:S(2)}) collective-permute-start(bf16[128,768]{1,0:T(8,128)(2,1)S(1)} %get-tuple-element.279), channel_id=1, source_target_pairs={{0,6},{1,7},{2,0},{3,1},{4,2},{5,3},{6,4},{7,5},{8,14},{9,15},{10,... | collective-permute-start | bytes 589832 | tf_op jit(solution)/shard_map/ppermute | solution.py:1082
  (30 other events, 282.2 us)
Sparse Core Ops, SparseCore 0:
  60.8 87.2 all-gather.1
  210.0 144.0 reduce-scatter.1

commit v4 on v3

--- a/solution.py
+++ b/solution.py
@@ -35,12 +35,10 @@
 
 
 def mask_tail(scores, valid):
-    width = scores.shape[0]
-    if width == BLOCK:
+    low = scores.shape[0] - valid.shape[0]
+    if low == 0:
         return jnp.where(valid, scores, very_low)
-    return jnp.concatenate(
-        [scores[: width - BLOCK], jnp.where(valid, scores[width - BLOCK :], very_low)], 0
-    )
+    return jnp.concatenate([scores[:low], jnp.where(valid, scores[low:], very_low)], 0)
 
 
 def stacked(pair):
@@ -180,19 +178,31 @@
     count, mem_len, _ = k_ref.shape
     parts = tokens // BLOCK
 
+    half = mem_len // 2
+
     @pl.when(info[0] == 1)
     def _():
-        def step(row, none):
-            rows = pl.ds(pl.multiple_of(row * BLOCK, BLOCK), BLOCK)
-
-            def run(width, valid):
-                scores = score_tile(q_ref[rows, :], k_ref[row, :width, :], valid(2 * BLOCK))
-                o_ref[rows, :], stat_ref[0, row] = attend_tile(scores, v_ref[row, :width, :])
-
-            by_length(info, row, mem_len, run)
+        def step(pair, none):
+            lengths = [info[1 + 2 * pair], info[2 + 2 * pair]]
+
+            def run(*widths):
+                tiles = []
+                for place, width in enumerate(widths):
+                    row = 2 * pair + place
+                    rows = pl.ds(pl.multiple_of(row * BLOCK, BLOCK), BLOCK)
+                    key = lax.broadcasted_iota(jnp.int32, (half, 2 * BLOCK), 0) + (width - half)
+                    scores = score_tile(q_ref[rows, :], k_ref[row, :width, :], key < lengths[place])
+                    tiles.append((row, rows, width, scores))
+                for row, rows, width, scores in tiles:
+                    o_ref[rows, :], stat_ref[0, row] = attend_tile(scores, v_ref[row, :width, :])
+
+            for one in (False, True):
+                for two in (False, True):
+                    chosen = ((lengths[0] > half) == one) & ((lengths[1] > half) == two)
+                    pl.when(chosen)(functools.partial(run, half << one, half << two))
             return none
 
-        lax.fori_loop(0, count, step, None)
+        lax.fori_loop(0, count // 2, step, None)
 
     @pl.when(info[0] != 1)
     def _():
@@ -322,6 +332,7 @@
 
 epsilon = 1e-05
 VECTORS = 32
+LANES = 128
 
 
 def normalise(total):
@@ -412,7 +423,7 @@
     )(info, *inputs)
 
 
-def first_norm(info, x, context, mid, vectors, rows=256):
+def first_norm(info, x, context, mid, vectors, rows=512):
     tokens, width = x.shape
     block = row_block(rows, width)
     low = jax.ShapeDtypeStruct((tokens, width), bf16)
@@ -556,7 +567,7 @@
     by_core(info, mine, got, run)
 
 
-def first_back(info, dz2, grad_query, z, mid, vectors, rows=256):
+def first_back(info, dz2, grad_query, z, mid, vectors, rows=512):
     tokens, width = z.shape
     block = row_block(rows, width)
     low = jax.ShapeDtypeStruct((tokens, width), bf16)
@@ -623,7 +634,7 @@
         out_ref[...] = jnp.zeros_like(out_ref)
 
 
-def memory_back(info, grad_keys, grad_values, mid, first, count, start=(), rows=512):
+def memory_back(info, grad_keys, grad_values, mid, first, count, start=(), rows=1024):
     length, width = grad_keys.shape[1:]
     block = memory_block(rows, width, first)
     return row_call(
@@ -663,16 +674,20 @@
 
 
 def mid_weights_kernel(
-    rows, info, m_ref, dk_ref, dv_ref, first_ref, dq_ref, self_ref, dself_ref,
-    mine, other, sum_ref, key_sum, value_sum, stage, sent,
+    rows, info, m_ref, dk_ref, dv_ref, first_hbm, dq_hbm, self_hbm, dself_hbm,
+    mine, other, sum_ref, key_sum, value_sum, stage, sent, held, arrived,
 ):
     row, part = pl.program_id(0), pl.program_id(1)
     out = (info, stage, sent, mine, other)
+    fetches = [
+        pltpu.make_async_copy(source, held.at[place], arrived.at[place])
+        for place, source in enumerate((self_hbm, dself_hbm, first_hbm, dq_hbm))
+    ]
 
     @pl.when((row == 0) & (part == 0))
     def _():
-        put_unit(*out, 0, dot_tn(self_ref[...], dself_ref[...]))
-        put_unit(*out, 1, dot_tn(first_ref[...], dq_ref[...]))
+        for fetch in fetches:
+            fetch.start()
         key_sum[...] = jnp.zeros_like(key_sum)
         value_sum[...] = jnp.zeros_like(value_sum)
         sum_ref[...] = jnp.zeros_like(sum_ref)
@@ -688,6 +703,10 @@
     def _():
         put_unit(*out, 2, key_sum[...])
         put_unit(*out, 3, value_sum[...])
+        for fetch in fetches:
+            fetch.wait()
+        put_unit(*out, 0, dot_tn(held[0], held[1]))
+        put_unit(*out, 1, dot_tn(held[2], held[3]))
         end_units(*out)
 
 
@@ -697,11 +716,13 @@
     half = jax.ShapeDtypeStruct((2 * width, width), bf16)
     return row_call(
         functools.partial(mid_weights_kernel, rows), "mid_weights", info, (count, 1),
-        [block] * 3 + [full(None)] * 4,
+        [block] * 3 + [pl.BlockSpec(memory_space=pl.ANY)] * 4,
         [pl.BlockSpec(memory_space=pl.ANY)] * 2 + [pl.BlockSpec((1, width), lambda row, part, info: (0, 0))],
         [half, half, jax.ShapeDtypeStruct((1, width), f32)],
         [(count, rows, width, width)] * 2, (memory, grad_keys, grad_values, *pairs),
-        [pltpu.VMEM((width, width), f32)] * 2 + unit_scratch(width),
+        [pltpu.VMEM((width, width), f32)] * 2
+        + unit_scratch(width)
+        + [pltpu.VMEM((4,) + pairs[0].shape, bf16), pltpu.SemaphoreType.DMA((4,))],
     )
 
 
@@ -738,7 +759,7 @@
     by_core(info, mine, got, run)
 
 
-def target_back(info, dz, grads, head, rows=256):
+def target_back(info, dz, grads, head, rows=512):
     tokens, width = dz.shape
     block = row_block(rows, width)
     return row_call(
@@ -868,6 +889,50 @@
     )(second_low, grad_hidden, active, grad_out)
 
 
+def pack_head_kernel(count, place, units, last, *refs):
+    sources, out_ref, rows_ref, arrived, held = refs[:count], refs[count], refs[count + 1], refs[count + 2], refs[count + 3 :]
+    own = last.shape[0]
+    copies = [
+        pltpu.make_async_copy(source, target, arrived.at[number])
+        for number, (source, target) in enumerate(zip(sources, held))
+    ]
+    for copy in copies:
+        copy.start()
+
+    def unit_copy_by(act):
+        rows = out_ref.at[pl.ds(0, own), :]
+
+        @pl.when(place[0] < 3)
+        def _():
+            act(pltpu.make_async_copy(units.at[jnp.minimum(place[0], 2)], rows, arrived.at[count]))
+
+        @pl.when(place[0] == 3)
+        def _():
+            act(pltpu.make_async_copy(last, rows, arrived.at[count]))
+
+    unit_copy_by(lambda copy: copy.start())
+    rows_ref[...] = jnp.zeros_like(rows_ref)
+    for copy in copies:
+        copy.wait()
+    for number, ref in enumerate(held):
+        rows_ref[: ref.shape[0], number * LANES : number * LANES + own] = ref[...].astype(f32)
+    out_ref[own:, :] = rows_ref[...].astype(bf16)
+    unit_copy_by(lambda copy: copy.wait())
+
+
+def pack_head(place, units, last, vectors):
+    own, width = last.shape
+    count = len(vectors)
+    return row_call(
+        functools.partial(pack_head_kernel, count), "pack_head", place, (),
+        [pl.BlockSpec(memory_space=pl.ANY)] * (2 + count), full(None),
+        jax.ShapeDtypeStruct((own + 8, width), bf16), [], (units, last, *vectors),
+        [pltpu.VMEM((8, width), f32), pltpu.SemaphoreType.DMA((count + 1,))]
+        + [pltpu.VMEM(item.shape, item.dtype) for item in vectors],
+        limit=58 * 2**20,
+    )
+
+
 def fold_call(kernel, name, spot, inputs, outs):
     return row_call(
         kernel, name, spot, (), [full(None)] * len(inputs), [full(None)] * len(outs),
@@ -1140,16 +1205,10 @@
     return out
 
 
-def lay_vectors(items, width):
-    rows = [jnp.pad(item, ((0, 8 - item.shape[0]), (0, 0))) for item in items]
-    row = jnp.concatenate(rows, 1)
-    return jnp.pad(row, ((0, 0), (0, width - row.shape[1])))
-
-
 def gather_vectors(rows, own):
     pieces, _, width = rows.shape
-    groups = width // own
-    rows = rows.reshape(pieces, 8, groups, own)
+    groups = width // LANES
+    rows = rows.reshape(pieces, 8, groups, LANES)[..., :own]
     hidden = rows[:, :4, 2].reshape(4, pieces * own)
     rows = jnp.transpose(rows, (2, 1, 0, 3)).reshape(groups * 8, pieces * own)
     return wide(jnp.concatenate([rows[:16], hidden, rows[20:]], 0))
@@ -1165,10 +1224,12 @@
     own = self_out.shape[0]
     pieces = width // own
     info = jnp.concatenate([bucket, source_len, core[None]])
-    vectors = lay_vectors(
-        (self_bias, cross_bias, ffn_in_bias.reshape(4, own), ffn_out_bias[None], norm_gain, norm_bias), width
-    )
-    head = jnp.concatenate([pick(jnp.concatenate([self_qkv, cross_out[None]], 0), 0, dp), vectors], 0)
+    head = pack_head(
+        dp[None],
+        self_qkv,
+        cross_out,
+        (self_bias, cross_bias, ffn_in_bias.reshape(4, own), ffn_out_bias[None], norm_gain, norm_bias),
+    )
     mid = pick(jnp.concatenate([self_out[None], cross_qkv], 0), 0, dp)
     head, mid = fence(join_depth(head, depth), mid)
     one, two = cut(head)

time: 428 us -> 423 us (0.988)
  Pallas kernels: 269 us -> 262 us
  starting transfers between devices: 33 us -> 38 us
    ppermute x24, starting transfers between devices: 22.2 us -> 29.1 us  [pair_swap(): lax.ppermute(array, axis, [(place, place ^ bit) for place in range(count)])]
    pallas_call x4, Pallas kernels: 88.9 us -> 82.4 us  [attend_call(): pl.pallas_call(functools.partial(kernel, len(start)), grid_spec=pltpu.Pre...]
    pallas_call x18 -> x19, Pallas kernels: 165 us -> 165 us  [row_call(): pl.pallas_call(kernel, grid_spec=pltpu.PrefetchScalarGridSpec(num_scalar_...]
  transfers between devices with their start and end apart: 38 -> 38, of which waited for: 21 -> 19; matrix products, arithmetic and copies ran while one was open for 1% -> 1% of each run, Pallas kernels for 51% -> 49%
where the time goes in v4:
time: 423 us; the launch traced here: 417 us
  Pallas kernels  262 us (62%)
  waiting for transfers between devices  84.5 us (20%)
  starting transfers between devices  38 us (9%)
  between operations  15.5 us (4%)
  local copies, waits for them, and re-layouts  11.8 us (3%)
  other arithmetic  5.67 us (1%)
    pallas_call x19, Pallas kernels, row_call(): pl.pallas_call(kernel, grid_spec=pltpu.PrefetchScalarGridSpec(num_scalar_...  165 us
    pallas_call x4, Pallas kernels, attend_call(): pl.pallas_call(functools.partial(kernel, len(start)), grid_spec=pltpu.Pre...  82.4 us
    ppermute x12, waiting for transfers between devices, ring(): lax.ppermute(array, axis, [(place, (place + shift) % count) for place in...  42.7 us
    ppermute x24, waiting for transfers between devices, pair_swap(): lax.ppermute(array, axis, [(place, place ^ bit) for place in range(count)])  41.8 us
    ppermute x24, starting transfers between devices, pair_swap(): lax.ppermute(array, axis, [(place, place ^ bit) for place in range(count)])  29.1 us
    pallas_call x1, Pallas kernels, ffn_weights(): pl.pallas_call(ffn_weights_kernel, grid=(blocks,), in_specs=[whole, part,...  14.6 us
    ppermute x12, starting transfers between devices, ring(): lax.ppermute(array, axis, [(place, (place + shift) % count) for place in...  8.86 us
  transfers between devices with their start and end apart: 38, of which 19 were waited for; matrix products, arithmetic and copies ran while one was open for 1% of the time, Pallas kernels for 49%

profile of v4, /device:TPU:9, one launch (start us, length us, event | category | flops | bytes accessed | tf_op | source)
XLA Modules:
  0.0 417.4 jit_solution(1124442443356810823)
XLA Ops:
  16.3 8.8 %collective-permute-done.1 = bf16[104,768]{1,0:T(8,128)(2,1)S(1)} collective-permute-done((bf16[104,768]{1,0:T(8,128)(2,1)}, bf16[104,768]{1,0:T(8,128)(2,1)S(1)}, u32[]{:S(2)}, u32[]{:S(2)}) %collective-permute-start.1) | collective-permute-done | bytes 159776 | tf_op jit(solution)/shard_map/ppermute | solution.py:1147
  30.4 5.5 %collective-permute-done.3 = bf16[4,48,768]{2,1,0:T(8,128)(2,1)S(1)} collective-permute-done((bf16[4,48,768]{2,1,0:T(8,128)(2,1)S(1)}, bf16[4,48,768]{2,1,0:T(8,128)(2,1)S(1)}, u32[]{:S(2)}, u32[]{:S(2)}) %collective-permute-start.3) | collective-permute-done | bytes 294944 | tf_op jit(solution)/shard_map/ppermute | solution.py:1142
  45.1 7.5 %collective-permute-done.9 = bf16[96,768]{1,0:T(8,128)(2,1)S(1)} collective-permute-done((bf16[96,768]{1,0:T(8,128)(2,1)S(1)}, bf16[96,768]{1,0:T(8,128)(2,1)S(1)}, u32[]{:S(2)}, u32[]{:S(2)}) %collective-permute-start.9) | collective-permute-done | bytes 147488 | tf_op jit(solution)/shard_map/ppermute | solution.py:1147
  67.1 9.4 %project_self.1 = (bf16[1024,768]{1,0:T(8,128)(2,1)}, bf16[1024,768]{1,0:T(8,128)(2,1)}, bf16[1024,768]{1,0:T(8,128)(2,1)}) custom-call(s32[6]{0:T(128)} %pad_add_fusion.info, bf16[1024,768]{1,0:T(8,128)(2,1)} %x_hbm, bf16[8,2,96,768]{3,2,1,0:T(8,128)(2,1)} %bitcast.99, bf16[8,2,96,768]{3,2,1,0:T(8,128)(2,1)} %collective-permute-done.10.got, ...), custom_call_target="tpu_custom_call" | custom-call | flops 4831838208 | bytes 8388608 | tf_op jit(solution)/shard_map/project_self/pallas_call | solution.py:409
  78.3 9.5 %self_attend.1 = (bf16[1024,768]{1,0:T(8,128)(2,1)}, f32[6,4,1,512]{3,2,1,0:T(1,128)}) custom-call(s32[6]{0:T(128)} %pad_add_fusion.info, bf16[1024,768]{1,0:T(8,128)(2,1)} %get-tuple-element.165.q_ref, bf16[1024,768]{1,0:T(8,128)(2,1)} %get-tuple-element.166.k_ref, bf16[1024,768]{1,0:T(8,128)(2,1)} %get-tuple-element.167.v_ref), custom_call_target="tpu_custom_call" | custom-call | flops 19327352832 | bytes 8388608 | tf_op jit(solution)/shard_map/self_attend/pallas_call | solution.py:298
  95.5 4.3 %collective-permute-done.15.got = bf16[8,2,96,768]{3,2,1,0:T(8,128)(2,1)} collective-permute-done((bf16[8,2,96,768]{3,2,1,0:T(8,128)(2,1)S(1)}, bf16[8,2,96,768]{3,2,1,0:T(8,128)(2,1)}, u32[]{:S(2)}, u32[]{:S(2)}) %collective-permute-start.15) | collective-permute-done | bytes 2359328 | tf_op jit(solution)/shard_map/ppermute | solution.py:1142
  99.8 8.9 %first_norm.1 = (f32[1024,768]{1,0:T(8,128)}, bf16[1024,768]{1,0:T(8,128)(2,1)}, bf16[1024,768]{1,0:T(8,128)(2,1)}) custom-call(s32[6]{0:T(128)} %pad_add_fusion.info, bf16[1024,768]{1,0:T(8,128)(2,1)} %x_hbm, bf16[1024,768]{1,0:T(8,128)(2,1)} %get-tuple-element.173.c_ref.o_ref.self_hbm, bf16[8,2,96,768]{3,2,1,0:T(8,128)(2,1)} %bitcast.92, ...), custom_call_target="tpu_custom_call" | custom-call | flops 4831838208 | bytes 8388608 | tf_op jit(solution)/shard_map/first_norm/pallas_call | solution.py:409
  108.7 16.2 %project_memory.1 = (bf16[4,1024,768]{2,1,0:T(8,128)(2,1)}, bf16[4,1024,768]{2,1,0:T(8,128)(2,1)}) custom-call(s32[6]{0:T(128)} %pad_add_fusion.info, bf16[4,1024,768]{2,1,0:T(8,128)(2,1)} %m_ref.2, bf16[8,2,96,768]{3,2,1,0:T(8,128)(2,1)} %bitcast.93, bf16[8,2,96,768]{3,2,1,0:T(8,128)(2,1)} %collective-permute-done.15.got, ...), custom_call_target="tpu_custom_call" | custom-call | flops 9663676416 | bytes 8388608 | tf_op jit(solution)/shard_map/project_memory/pallas_call | solution.py:409
  124.9 22.8 %cross_attend.1 = (bf16[1024,768]{1,0:T(8,128)(2,1)}, f32[6,4,1,512]{3,2,1,0:T(1,128)}) custom-call(s32[6]{0:T(128)} %pad_add_fusion.info, bf16[1024,768]{1,0:T(8,128)(2,1)} %get-tuple-element.179.q_ref, bf16[4,1024,768]{2,1,0:T(8,128)(2,1)} %get-tuple-element.180.k_ref, bf16[4,1024,768]{2,1,0:T(8,128)(2,1)} %get-tuple-element.181.v_ref), custom_call_target="tpu_custom_call" | custom-call | flops 19327352832 | bytes 8388608 | tf_op jit(solution)/shard_map/cross_attend/pallas_call | solution.py:298
  147.7 38.9 %ffn_block.1 = (bf16[1024,768]{1,0:T(8,128)(2,1)}, bf16[1024,768]{1,0:T(8,128)(2,1)}, bf16[1024,3072]{1,0:T(8,128)(2,1)}, bf16[1024,3072]{1,0:T(8,128)(2,1)}, bf...) custom-call(s32[6]{0:T(128)} %pad_add_fusion.info, ...), custom_call_target="tpu_custom_call" | custom-call | flops 38654705664 | bytes 8388608 | tf_op jit(solution)/shard_map/ffn_block/pallas_call | solution.py:409
  186.6 14.6 %ffn_weights.1 = bf16[4,8,192,768]{3,2,1,0:T(8,128)(2,1)} custom-call(bf16[1024,768]{1,0:T(8,128)(2,1)} %get-tuple-element.268.h_ref, bf16[1024,3072]{1,0:T(8,128)(2,1)} %get-tuple-element.269.du_ref, bf16[1024,3072]{1,0:T(8,128)(2,1)} %get-tuple-element.270.a_ref, bf16[1024,768]{1,0:T(8,128)(2,1)} %get-tuple-element.271.df_ref), custom_call_target="tpu_custom_call" | custom-call | flops 9663676416 | bytes 8388608 | tf_op jit(solution)/shard_map/ffn_weights/pallas_call | solution.py:875
  201.2 37.2 %cross_attend_back.1 = (bf16[1024,768]{1,0:T(8,128)(2,1)}, bf16[4,1024,768]{2,1,0:T(8,128)(2,1)}, bf16[4,1024,768]{2,1,0:T(8,128)(2,1)}) custom-call(s32[6]{0:T(128)} %pad_add_fusion.info, bf16[1024,768]{1,0:T(8,128)(2,1)} %get-tuple-element.179.q_ref, bf16[4,1024,768]{2,1,0:T(8,128)(2,1)} %get-tuple-element.180.k_ref, ...), custom_call_target="tpu_custom_call" | custom-call | flops 38654705664 | bytes 8388608 | tf_op jit(solution)/shard_map/cross_attend_back/pallas_call | solution.py:298
  238.4 10.1 %first_back.1 = (f32[1024,768]{1,0:T(8,128)}, bf16[1024,768]{1,0:T(8,128)(2,1)}, bf16[1024,768]{1,0:T(8,128)(2,1)}, f32[8,768]{1,0:T(8,128)}) custom-call(s32[6]{0:T(128)} %pad_add_fusion.info, f32[1024,768]{1,0:T(8,128)} %get-tuple-element.186.dz2_ref, bf16[1024,768]{1,0:T(8,128)(2,1)} %get-tuple-element.189.dq_ref.dq_hbm, ...), custom_call_target="tpu_custom_call" | custom-call | flops 4831838208 | bytes 8388608 | tf_op jit(solution)/shard_map/first_back/pallas_call | solution.py:409
  248.6 12.9 %self_attend_back.1 = (bf16[1024,768]{1,0:T(8,128)(2,1)}, bf16[1024,768]{1,0:T(8,128)(2,1)}, bf16[1024,768]{1,0:T(8,128)(2,1)}) custom-call(s32[6]{0:T(128)} %pad_add_fusion.info, bf16[1024,768]{1,0:T(8,128)(2,1)} %get-tuple-element.165.q_ref, bf16[1024,768]{1,0:T(8,128)(2,1)} %get-tuple-element.166.k_ref, bf16[1024,768]{1,0:T(8,128)(2,1)} %get-tuple-element.167.v_ref, ...), custom_call_target="tpu_custom_call" | custom-call | flops 38654705664 | bytes 8388608 | tf_op jit(solution)/shard_map/self_attend_back/pallas_call | solution.py:298
  261.5 20.0 %mid_weights.1 = (bf16[1536,768]{1,0:T(8,128)(2,1)}, bf16[1536,768]{1,0:T(8,128)(2,1)}, f32[1,768]{1,0:T(1,128)}) custom-call(s32[6]{0:T(128)} %pad_add_fusion.info, bf16[4,1024,768]{2,1,0:T(8,128)(2,1)} %m_ref.2, bf16[4,1024,768]{2,1,0:T(8,128)(2,1)} %get-tuple-element.255.dk_ref, bf16[4,1024,768]{2,1,0:T(8,128)(2,1)} %get-tuple-element.197.dv_ref, ...), custom_call_target="tpu_custom_call" | custom-call | flops 9663676416 | bytes 8388608 | tf_op jit(solution)/shard_map/mid_weights/pallas_call | solution.py:409
  281.7 12.0 %self_weights.1 = (bf16[1568,768]{1,0:T(8,128)(2,1)}, bf16[1568,768]{1,0:T(8,128)(2,1)}) custom-call(s32[6]{0:T(128)} %pad_add_fusion.info, bf16[1024,768]{1,0:T(8,128)(2,1)} %x_hbm, bf16[1024,768]{1,0:T(8,128)(2,1)} %get-tuple-element.205.q_hbm.q_ref, bf16[1024,768]{1,0:T(8,128)(2,1)} %get-tuple-element.206.k_hbm.k_ref, ...), custom_call_target="tpu_custom_call" | custom-call | flops 4831838208 | bytes 8388608 | tf_op jit(solution)/shard_map/self_weights/pallas_call | solution.py:409
  303.3 9.9 %target_back.1 = f32[1024,768]{1,0:T(8,128)} custom-call(s32[6]{0:T(128)} %pad_add_fusion.info, f32[1024,768]{1,0:T(8,128)} %get-tuple-element.223.z_ref, bf16[1024,768]{1,0:T(8,128)(2,1)} %get-tuple-element.205.q_hbm.q_ref, bf16[1024,768]{1,0:T(8,128)(2,1)} %get-tuple-element.206.k_hbm.k_ref, bf16[1024,768]{1,0:T(8,128)(2,1)} %get-tuple-element.207.v_hbm.v_ref, ...), custom_call_target="tpu_custom_call" | custom-call | flops 4831838208 | bytes 8388608 | tf_op jit(solution)/shard_map/target_back/pallas_call | solution.py:409
  313.2 9.8 %collective-permute-done.17.got_a = bf16[384,768]{1,0:T(8,128)(2,1)S(1)} collective-permute-done((bf16[384,768]{1,0:T(8,128)(2,1)}, bf16[384,768]{1,0:T(8,128)(2,1)S(1)}, u32[]{:S(2)}, u32[]{:S(2)}) %collective-permute-start.17) | collective-permute-done | bytes 589856 | tf_op jit(solution)/shard_map/ppermute | solution.py:1142
  333.9 10.4 %memory_back.2.refs_0_ = f32[4,1024,768]{2,1,0:T(8,128)} custom-call(s32[6]{0:T(128)} %pad_add_fusion.info, bf16[4,1024,768]{2,1,0:T(8,128)(2,1)} %get-tuple-element.255.dk_ref, bf16[4,1024,768]{2,1,0:T(8,128)(2,1)} %get-tuple-element.197.dv_ref, bf16[8,2,96,768]{3,2,1,0:T(8,128)(2,1)} %bitcast.95, bf16[8,2,96,768]{3,2,1,0:T(8,128)(2,1)} %collective-permute-done.15.got), custom_call_target="tpu_custom_call" | custom-call | flops 4831838208 | bytes 8388608 | tf_op jit(solution)/shard_map/memory_back/pallas_call | solution.py:409
  344.4 10.1 %collective-permute-done.20.got_a = bf16[192,768]{1,0:T(8,128)(2,1)S(1)} collective-permute-done((bf16[192,768]{1,0:T(8,128)(2,1)S(1)}, bf16[192,768]{1,0:T(8,128)(2,1)S(1)}, u32[]{:S(2)}, u32[]{:S(2)}) %collective-permute-start.20) | collective-permute-done | bytes 294944 | tf_op jit(solution)/shard_map/ppermute | solution.py:1142
  362.1 10.6 %memory_back.3 = f32[4,1024,768]{2,1,0:T(8,128)} custom-call(s32[6]{0:T(128)} %pad_add_fusion.info, bf16[4,1024,768]{2,1,0:T(8,128)(2,1)} %get-tuple-element.255.dk_ref, bf16[4,1024,768]{2,1,0:T(8,128)(2,1)} %get-tuple-element.197.dv_ref, bf16[8,2,96,768]{3,2,1,0:T(8,128)(2,1)} %bitcast.96, ...), custom_call_target="tpu_custom_call", output_to_operand_aliasing={{}: (5, {})} | custom-call | flops 4831838208 | bytes 8388608 | tf_op jit(solution)/shard_map/memory_back/pallas_call | solution.py:409
  380.4 4.2 %collective-permute-done.30 = bf16[128,768]{1,0:T(8,128)(2,1)S(1)} collective-permute-done((bf16[128,768]{1,0:T(8,128)(2,1)S(1)}, bf16[128,768]{1,0:T(8,128)(2,1)S(1)}, u32[]{:S(2)}, u32[]{:S(2)}) %collective-permute-start.30) | collective-permute-done | bytes 196640 | tf_op jit(solution)/shard_map/ppermute | solution.py:1147
  384.6 9.7 %collective-permute-done.31 = bf16[128,768]{1,0:T(8,128)(2,1)S(1)} collective-permute-done((bf16[128,768]{1,0:T(8,128)(2,1)S(1)}, bf16[128,768]{1,0:T(8,128)(2,1)S(1)}, u32[]{:S(2)}, u32[]{:S(2)}) %collective-permute-start.31) | collective-permute-done | bytes 196640 | tf_op jit(solution)/shard_map/ppermute | solution.py:1147
  398.4 4.9 %collective-permute-done.33 = bf16[96,768]{1,0:T(8,128)(2,1)S(1)} collective-permute-done((bf16[96,768]{1,0:T(8,128)(2,1)S(1)}, bf16[96,768]{1,0:T(8,128)(2,1)S(1)}, u32[]{:S(2)}, u32[]{:S(2)}) %collective-permute-start.33) | collective-permute-done | bytes 147488 | tf_op jit(solution)/shard_map/ppermute | solution.py:1142
  (172 shorter events, 93.5 us)
Async XLA Ops:
  7.2 140.5 %all-gather.2.cloned.1.call-start = ((), (), s32[]{:S(2)}) async-start(), calls=%async_computation.1 | async-start | bytes 9732096 | tf_op jit(solution)/shard_map/all_gather | solution.py:1247
  11.7 13.4 %collective-permute-start.1 = (bf16[104,768]{1,0:T(8,128)(2,1)}, bf16[104,768]{1,0:T(8,128)(2,1)S(1)}, u32[]{:S(2)}, u32[]{:S(2)}) collective-permute-start(bf16[104,768]{1,0:T(8,128)(2,1)} %pack_head.1), channel_id=1, source_target_pairs={{0,4},{1,5},{2,6},{3,7},{4,0},{5,1},{6,2},{7,3},{8,12},{9,13},{10,... | collective-permute-start | bytes 479240 | tf_op jit(solution)/shard_map/ppermute | solution.py:1147
  12.8 15.0 %collective-permute-start.2 = (bf16[104,768]{1,0:T(8,128)(2,1)}, bf16[104,768]{1,0:T(8,128)(2,1)S(1)}, u32[]{:S(2)}, u32[]{:S(2)}) collective-permute-start(bf16[104,768]{1,0:T(8,128)(2,1)} %pack_head.1), channel_id=1, source_target_pairs={{0,6},{1,7},{2,0},{3,1},{4,2},{5,3},{6,4},{7,5},{8,14},{9,15},{10,... | collective-permute-start | bytes 479240 | tf_op jit(solution)/shard_map/ppermute | solution.py:1147
  38.3 14.3 %collective-permute-start.9 = (bf16[96,768]{1,0:T(8,128)(2,1)S(1)}, bf16[96,768]{1,0:T(8,128)(2,1)S(1)}, u32[]{:S(2)}, u32[]{:S(2)}) collective-permute-start(bf16[96,768]{1,0:T(8,128)(2,1)S(1)} %fusion.3), channel_id=1, source_target_pairs={{0,6},{1,7},{2,0},{3,1},{4,2},{5,3},{6,4},{7,5},{8,14},{9,15},{10,... | collective-permute-start | bytes 442376 | tf_op jit(solution)/shard_map/ppermute | solution.py:1147
  39.7 14.1 %collective-permute-start.6 = (bf16[4,2,56,768]{3,2,0,1:T(8,128)(2,1)S(1)}, bf16[4,2,56,768]{3,2,0,1:T(8,128)(2,1)S(1)}, u32[]{:S(2)}, u32[]{:S(2)}) collective-permute-start(bf16[4,2,56,768]{3,2,0,1:T(8,128)(2,1)S(1)} %pad_maximum_fusion.2), channel_id=1, source_target_pairs={{0,1},{1,0},{2,3},{3,2},{4,5},{5,4},{6,7},{7,6},{8,9},{9,8},{10,11... | collective-permute-start | bytes 2064392 | tf_op jit(solution)/shard_map/ppermute | solution.py:1142
  39.9 12.7 %collective-permute-start.5 = (bf16[4,2,48,768]{3,2,1,0:T(8,128)(2,1)S(1)}, bf16[4,2,48,768]{3,2,1,0:T(8,128)(2,1)S(1)}, u32[]{:S(2)}, u32[]{:S(2)}) collective-permute-start(bf16[4,2,48,768]{3,2,1,0:T(8,128)(2,1)S(1)} %pad_maximum_fusion.3), channel_id=1, source_target_pairs={{0,16},{8,24},{16,0},{24,8},{1,17},{9,25},{17,1},{25,9},{2,18},{10... | collective-permute-start | bytes 1769480 | tf_op jit(solution)/shard_map/ppermute | solution.py:1142
  58.7 318.0 %reduce-scatter.2.cloned.1.call-start = ((), (), s32[]{:S(2)}) async-start(), calls=%async_computation.2 | async-start | bytes 9732096 | tf_op jit(solution)/shard_map/reduce_scatter | solution.py:1267
  76.6 14.6 %collective-permute-start.14 = (bf16[4,2,48,768]{3,2,0,1:T(8,128)(2,1)S(1)}, bf16[4,2,48,768]{3,2,0,1:T(8,128)(2,1)S(1)}, u32[]{:S(2)}, u32[]{:S(2)}) collective-permute-start(bf16[4,2,48,768]{3,2,0,1:T(8,128)(2,1)S(1)} %pad_maximum_fusion.5), channel_id=1, source_target_pairs={{0,1},{1,0},{2,3},{3,2},{4,5},{5,4},{6,7},{7,6},{8,9},{9,8},{10,11... | collective-permute-start | bytes 1769480 | tf_op jit(solution)/shard_map/ppermute | solution.py:1142
  77.4 14.0 %collective-permute-start.13 = (bf16[4,2,48,768]{3,2,0,1:T(8,128)(2,1)S(1)}, bf16[4,2,48,768]{3,2,0,1:T(8,128)(2,1)S(1)}, u32[]{:S(2)}, u32[]{:S(2)}) collective-permute-start(bf16[4,2,48,768]{3,2,0,1:T(8,128)(2,1)S(1)} %pad_maximum_fusion.4), channel_id=1, source_target_pairs={{0,16},{8,24},{16,0},{24,8},{1,17},{9,25},{17,1},{25,9},{2,18},{10... | collective-permute-start | bytes 1769480 | tf_op jit(solution)/shard_map/ppermute | solution.py:1142
  298.3 25.5 %collective-permute-start.19 = (bf16[1568,768]{1,0:T(8,128)(2,1)}, bf16[1568,768]{1,0:T(8,128)(2,1)}, u32[]{:S(2)}, u32[]{:S(2)}) collective-permute-start(bf16[1568,768]{1,0:T(8,128)(2,1)} %get-tuple-element.222), channel_id=1, source_target_pairs={{0,8},{8,0},{16,24},{24,16},{1,9},{9,1},{17,25},{25,17},{2,10},{10... | collective-permute-start | bytes 7225352 | tf_op jit(solution)/shard_map/ppermute | solution.py:1142
  298.7 24.3 %collective-permute-start.17 = (bf16[384,768]{1,0:T(8,128)(2,1)}, bf16[384,768]{1,0:T(8,128)(2,1)S(1)}, u32[]{:S(2)}, u32[]{:S(2)}) collective-permute-start(bf16[384,768]{1,0:T(8,128)(2,1)} %get-tuple-element.220), channel_id=1, source_target_pairs={{0,16},{8,24},{16,0},{24,8},{1,17},{9,25},{17,1},{25,9},{2,18},{10... | collective-permute-start | bytes 1769480 | tf_op jit(solution)/shard_map/ppermute | solution.py:1142
  300.6 23.2 %collective-permute-start.18 = (bf16[384,768]{1,0:T(8,128)(2,1)}, bf16[384,768]{1,0:T(8,128)(2,1)}, u32[]{:S(2)}, u32[]{:S(2)}) collective-permute-start(bf16[384,768]{1,0:T(8,128)(2,1)} %get-tuple-element.221), channel_id=1, source_target_pairs={{0,1},{1,0},{2,3},{3,2},{4,5},{5,4},{6,7},{7,6},{8,9},{9,8},{10,11... | collective-permute-start | bytes 1769480 | tf_op jit(solution)/shard_map/ppermute | solution.py:1142
  330.2 25.0 %collective-permute-start.22 = (bf16[416,768]{1,0:T(8,128)(2,1)}, bf16[416,768]{1,0:T(8,128)(2,1)S(1)}, u32[]{:S(2)}, u32[]{:S(2)}) collective-permute-start(bf16[416,768]{1,0:T(8,128)(2,1)} %get-tuple-element.238), channel_id=1, source_target_pairs={{0,16},{8,24},{16,0},{24,8},{1,17},{9,25},{17,1},{25,9},{2,18},{10... | collective-permute-start | bytes 1916936 | tf_op jit(solution)/shard_map/ppermute | solution.py:1142
  331.7 23.5 %collective-permute-start.23 = (bf16[384,768]{1,0:T(8,128)(2,1)}, bf16[384,768]{1,0:T(8,128)(2,1)S(1)}, u32[]{:S(2)}, u32[]{:S(2)}) collective-permute-start(bf16[384,768]{1,0:T(8,128)(2,1)} %get-tuple-element.239), channel_id=1, source_target_pairs={{0,1},{1,0},{2,3},{3,2},{4,5},{5,4},{6,7},{7,6},{8,9},{9,8},{10,11... | collective-permute-start | bytes 1769480 | tf_op jit(solution)/shard_map/ppermute | solution.py:1142
  332.8 21.7 %collective-permute-start.20 = (bf16[192,768]{1,0:T(8,128)(2,1)S(1)}, bf16[192,768]{1,0:T(8,128)(2,1)S(1)}, u32[]{:S(2)}, u32[]{:S(2)}) collective-permute-start(bf16[192,768]{1,0:T(8,128)(2,1)S(1)} %get-tuple-element.236), channel_id=1, source_target_pairs={{0,1},{1,0},{2,3},{3,2},{4,5},{5,4},{6,7},{7,6},{8,9},{9,8},{10,11... | collective-permute-start | bytes 884744 | tf_op jit(solution)/shard_map/ppermute | solution.py:1142
  333.1 21.3 %collective-permute-start.21 = (bf16[192,768]{1,0:T(8,128)(2,1)S(1)}, bf16[192,768]{1,0:T(8,128)(2,1)S(1)}, u32[]{:S(2)}, u32[]{:S(2)}) collective-permute-start(bf16[192,768]{1,0:T(8,128)(2,1)S(1)} %get-tuple-element.237), channel_id=1, source_target_pairs={{0,16},{8,24},{16,0},{24,8},{1,17},{9,25},{17,1},{25,9},{2,18},{10... | collective-permute-start | bytes 884744 | tf_op jit(solution)/shard_map/ppermute | solution.py:1142
  357.5 18.4 %collective-permute-start.24 = (bf16[224,768]{1,0:T(8,128)(2,1)}, bf16[224,768]{1,0:T(8,128)(2,1)S(1)}, u32[]{:S(2)}, u32[]{:S(2)}) collective-permute-start(bf16[224,768]{1,0:T(8,128)(2,1)} %get-tuple-element.253), channel_id=1, source_target_pairs={{0,1},{1,0},{2,3},{3,2},{4,5},{5,4},{6,7},{7,6},{8,9},{9,8},{10,11... | collective-permute-start | bytes 1032200 | tf_op jit(solution)/shard_map/ppermute | solution.py:1142
  359.5 16.4 %collective-permute-start.25 = (bf16[192,768]{1,0:T(8,128)(2,1)}, bf16[192,768]{1,0:T(8,128)(2,1)S(1)}, u32[]{:S(2)}, u32[]{:S(2)}) collective-permute-start(bf16[192,768]{1,0:T(8,128)(2,1)} %get-tuple-element.254), channel_id=1, source_target_pairs={{0,16},{8,24},{16,0},{24,8},{1,17},{9,25},{17,1},{25,9},{2,18},{10... | collective-permute-start | bytes 884744 | tf_op jit(solution)/shard_map/ppermute | solution.py:1142
  360.0 12.7 %collective-permute-start.26 = (bf16[96,768]{1,0:T(8,128)(2,1)S(1)}, bf16[96,768]{1,0:T(8,128)(2,1)S(1)}, u32[]{:S(2)}, u32[]{:S(2)}) collective-permute-start(bf16[96,768]{1,0:T(8,128)(2,1)S(1)} %get-tuple-element.257), channel_id=1, source_target_pairs={{0,2},{1,3},{2,4},{3,5},{4,6},{5,7},{6,0},{7,1},{8,10},{9,11},{10,... | collective-permute-start | bytes 442376 | tf_op jit(solution)/shard_map/ppermute | solution.py:1147
  360.0 12.7 %collective-permute-start.27 = (bf16[96,768]{1,0:T(8,128)(2,1)S(1)}, bf16[96,768]{1,0:T(8,128)(2,1)S(1)}, u32[]{:S(2)}, u32[]{:S(2)}) collective-permute-start(bf16[96,768]{1,0:T(8,128)(2,1)S(1)} %get-tuple-element.258), channel_id=1, source_target_pairs={{0,4},{1,5},{2,6},{3,7},{4,0},{5,1},{6,2},{7,3},{8,12},{9,13},{10,... | collective-permute-start | bytes 442376 | tf_op jit(solution)/shard_map/ppermute | solution.py:1147
  362.1 13.8 %collective-permute-start.28 = (bf16[96,768]{1,0:T(8,128)(2,1)S(1)}, bf16[96,768]{1,0:T(8,128)(2,1)S(1)}, u32[]{:S(2)}, u32[]{:S(2)}) collective-permute-start(bf16[96,768]{1,0:T(8,128)(2,1)S(1)} %get-tuple-element.259), channel_id=1, source_target_pairs={{0,6},{1,7},{2,0},{3,1},{4,2},{5,3},{6,4},{7,5},{8,14},{9,15},{10,... | collective-permute-start | bytes 442376 | tf_op jit(solution)/shard_map/ppermute | solution.py:1147
  377.7 19.4 %collective-permute-start.29 = (bf16[288,768]{1,0:T(8,128)(2,1)S(1)}, bf16[288,768]{1,0:T(8,128)(2,1)S(1)}, u32[]{:S(2)}, u32[]{:S(2)}) collective-permute-start(bf16[288,768]{1,0:T(8,128)(2,1)S(1)} %pad_maximum_fusion.6), channel_id=1, source_target_pairs={{0,16},{8,24},{16,0},{24,8},{1,17},{9,25},{17,1},{25,9},{2,18},{10... | collective-permute-start | bytes 1327112 | tf_op jit(solution)/shard_map/ppermute | solution.py:1142
  378.9 15.3 %collective-permute-start.31 = (bf16[128,768]{1,0:T(8,128)(2,1)S(1)}, bf16[128,768]{1,0:T(8,128)(2,1)S(1)}, u32[]{:S(2)}, u32[]{:S(2)}) collective-permute-start(bf16[128,768]{1,0:T(8,128)(2,1)S(1)} %get-tuple-element.278), channel_id=1, source_target_pairs={{0,4},{1,5},{2,6},{3,7},{4,0},{5,1},{6,2},{7,3},{8,12},{9,13},{10,... | collective-permute-start | bytes 589832 | tf_op jit(solution)/shard_map/ppermute | solution.py:1147
  379.0 18.1 %collective-permute-start.32 = (bf16[128,768]{1,0:T(8,128)(2,1)S(1)}, bf16[128,768]{1,0:T(8,128)(2,1)S(1)}, u32[]{:S(2)}, u32[]{:S(2)}) collective-permute-start(bf16[128,768]{1,0:T(8,128)(2,1)S(1)} %get-tuple-element.279), channel_id=1, source_target_pairs={{0,6},{1,7},{2,0},{3,1},{4,2},{5,3},{6,4},{7,5},{8,14},{9,15},{10,... | collective-permute-start | bytes 589832 | tf_op jit(solution)/shard_map/ppermute | solution.py:1147
  (30 other events, 287.0 us)
Sparse Core Ops, SparseCore 0:
  58.9 87.4 all-gather.1
  201.3 147.0 reduce-scatter.1

commit v5 on v4

--- a/solution.py
+++ b/solution.py
@@ -391,14 +391,12 @@
     )
 
 
-def first_kernel(info, x_ref, c_ref, mine, got, vec_ref, z_ref, low_ref, q_ref):
+def first_kernel(info, x_ref, c_ref, mine, got, vec_ref, z_ref, low_ref):
     def run(even, odd):
-        total = x_ref[...].astype(f32) + dot_nn(c_ref[...], unit(even)) + vec_ref[2 : 3, :]
+        total = x_ref[...].astype(f32) + dot_nn(c_ref[...], unit(odd)) + vec_ref[2:3, :]
         normal, _ = normalise(total)
-        first_low = (normal * vec_ref[32 : 33, :] + vec_ref[40 : 41, :]).astype(bf16)
         z_ref[...] = total
-        low_ref[...] = first_low
-        q_ref[...] = ((dot_nn(first_low, unit(odd)) + vec_ref[8 : 9, :]) * HEAD**-0.5).astype(bf16)
+        low_ref[...] = (normal * vec_ref[32:33, :] + vec_ref[40:41, :]).astype(bf16)
 
     by_core(info, mine, got, run)
 
@@ -423,15 +421,15 @@
     )(info, *inputs)
 
 
-def first_norm(info, x, context, mid, vectors, rows=512):
+def first_norm(info, x, context, head, vectors, rows=512):
     tokens, width = x.shape
     block = row_block(rows, width)
     low = jax.ShapeDtypeStruct((tokens, width), bf16)
     return row_call(
         first_kernel, "first_norm", info, (tokens // rows,),
-        [block, block, unit_block(mid[0], 0), unit_block(mid[1], 0), full(vectors)],
-        [block] * 3, [jax.ShapeDtypeStruct((tokens, width), f32), low, low],
-        [(tokens, width, width)] * 4, (x, context, *mid, vectors),
+        [block, block, unit_block(head[0], 1), unit_block(head[1], 1), full(vectors)],
+        [block] * 2, [jax.ShapeDtypeStruct((tokens, width), f32), low],
+        [(tokens, width, width)] * 2, (x, context, *head, vectors),
     )
 
 
@@ -466,7 +464,7 @@
     @pl.when(pl.program_id(0) == 0)
     def _():
         def load(even, odd):
-            out_w[...] = unit(odd)
+            out_w[...] = unit(even)
 
         by_core(info, mine, got, load)
 
@@ -526,7 +524,7 @@
     dc_ref[...] = dot_nt(grad_low, out_w[...]).astype(bf16)
 
 
-def ffn_block(info, z, context, cotangent, head, tail, vectors, rows=256):
+def ffn_block(info, z, context, cotangent, mid, tail, vectors, rows=256):
     tokens, width = z.shape
     hidden = tail.shape[0] * width
     block = row_block(rows, width)
@@ -535,24 +533,26 @@
     wide_shape = jax.ShapeDtypeStruct((tokens, hidden), bf16)
     return row_call(
         ffn_kernel, "ffn_block", info, (tokens // rows,),
-        [block] * 3 + [unit_block(head[0], 1), unit_block(head[1], 1), full(tail), full(vectors)],
+        [block] * 3 + [unit_block(mid[0], 0), unit_block(mid[1], 0), full(tail), full(vectors)],
         [block, block, wide, wide, block, block, block, block, keep_block(8, width), keep_block(1, hidden)],
         [
             narrow_shape, narrow_shape, wide_shape, wide_shape, narrow_shape, narrow_shape,
             jax.ShapeDtypeStruct((tokens, width), f32), narrow_shape,
             jax.ShapeDtypeStruct((8, width), f32), jax.ShapeDtypeStruct((1, hidden), f32),
         ],
-        [(tokens, width, hidden)] * 8, (z, context, cotangent, *head, tail, vectors),
+        [(tokens, width, hidden)] * 8, (z, context, cotangent, *mid, tail, vectors),
         [pltpu.VMEM((rows, hidden), f32), pltpu.VMEM((width, width), bf16)],
     )
 
 
-def first_back_kernel(info, dz2_ref, dq_ref, z_ref, mine, got, vec_ref, dz_ref, do_ref, dc_ref, sum_ref):
+def first_back_kernel(
+    info, dz2_ref, dq_ref, z_ref, mine, got, head_mine, head_got, vec_ref, dz_ref, do_ref, dc_ref, sum_ref
+):
     start_sums(sum_ref)
 
-    def run(even, odd):
+    def run(query, out):
         grad_query = dq_ref[...]
-        grad_first = dz2_ref[...] + dot_nt(grad_query, unit(odd))
+        grad_first = dz2_ref[...] + dot_nt(grad_query, unit(query))
         normal, scale = normalise(z_ref[...])
         add_rows(sum_ref, 0, grad_first * normal)
         add_rows(sum_ref, 1, grad_first)
@@ -562,21 +562,26 @@
         do_ref[...] = grad_low
         add_rows(sum_ref, 2, grad_low.astype(f32))
         add_rows(sum_ref, 3, grad_query.astype(f32))
-        dc_ref[...] = dot_nt(grad_low, unit(even)).astype(bf16)
-
-    by_core(info, mine, got, run)
-
-
-def first_back(info, dz2, grad_query, z, mid, vectors, rows=512):
+        dc_ref[...] = dot_nt(grad_low, unit(out)).astype(bf16)
+
+    core = info[info.shape[0] - 1]
+    pl.when(core == 0)(lambda: run(got, head_got))
+    pl.when(core != 0)(lambda: run(mine, head_mine))
+
+
+def first_back(info, dz2, grad_query, z, head, mid, vectors, rows=512):
     tokens, width = z.shape
     block = row_block(rows, width)
     low = jax.ShapeDtypeStruct((tokens, width), bf16)
     return row_call(
         first_back_kernel, "first_back", info, (tokens // rows,),
-        [block] * 3 + [unit_block(mid[0], 0), unit_block(mid[1], 0), full(vectors)],
+        [block] * 3
+        + [unit_block(item, 0) for item in mid]
+        + [unit_block(item, 1) for item in head]
+        + [full(vectors)],
         [block] * 3 + [keep_block(8, width)],
         [jax.ShapeDtypeStruct((tokens, width), f32), low, low, jax.ShapeDtypeStruct((8, width), f32)],
-        [(tokens, width, width)] * 4, (dz2, grad_query, z, *mid, vectors),
+        [(tokens, width, width)] * 4, (dz2, grad_query, z, *mid, *head, vectors),
     )
 
 
@@ -590,13 +595,24 @@
     return used, jnp.where(info[0] == 1, jnp.minimum(part, last), jnp.where(row == 0, jnp.minimum(part, last), last))
 
 
-def project_kernel(rows, info, m_ref, mine, got, b_ref, k_ref, v_ref):
-    @pl.when(needed(info, pl.program_id(0), pl.program_id(1), rows))
+def project_kernel(
+    rows, info, m_ref, mine, got, low_ref, query_mine, query_got, vec_ref, k_ref, v_ref, q_ref
+):
+    row, part = pl.program_id(0), pl.program_id(1)
+
+    @pl.when((row == 0) & (part == 0))
+    def _():
+        def query(even, odd):
+            q_ref[...] = ((dot_nn(low_ref[...], unit(odd)) + vec_ref[8:9, :]) * HEAD**-0.5).astype(bf16)
+
+        by_core(info, query_mine, query_got, query)
+
+    @pl.when(needed(info, row, part, rows))
     def _():
         def run(even, odd):
             memory = m_ref[0]
             k_ref[0] = dot_nn(memory, unit(even)).astype(bf16)
-            v_ref[0] = (dot_nn(memory, unit(odd)) + b_ref[9 : 10, :]).astype(bf16)
+            v_ref[0] = (dot_nn(memory, unit(odd)) + vec_ref[9:10, :]).astype(bf16)
 
         by_core(info, mine, got, run)
 
@@ -607,14 +623,19 @@
     )
 
 
-def project_memory(info, memory, mid, vectors, rows=512):
+def project_memory(info, memory, low, mid, vectors, rows=512):
     count, length, width = memory.shape
     block = memory_block(rows, width)
     return row_call(
         functools.partial(project_kernel, rows), "project_memory", info, (count, length // rows),
-        [block, unit_block(mid[0], 1), unit_block(mid[1], 1), full(vectors)], [block] * 2,
-        [jax.ShapeDtypeStruct(memory.shape, bf16)] * 2,
-        [(count, length, width, width)] * 2, (memory, *mid, vectors),
+        [block]
+        + [unit_block(item, 1) for item in mid]
+        + [full(low)]
+        + [unit_block(item, 0) for item in mid]
+        + [full(vectors)],
+        [block] * 2 + [pl.BlockSpec(low.shape, lambda row, part, info: (0, 0))],
+        [jax.ShapeDtypeStruct(memory.shape, bf16)] * 2 + [jax.ShapeDtypeStruct(low.shape, bf16)],
+        [(count, length, width, width)] * 2, (memory, *mid, low, *mid, vectors),
     )
 
 
@@ -1106,17 +1127,17 @@
     queries, mid = mid_step(queries, mid)
     context_self, stats_self = self_attend(info, queries, keys, values)
     context_self, mid = mid_last(context_self, mid)
-    total_first, first_low, query_cross = first_norm(info, target, context_self, mid, vectors)
-    key_cross, value_cross = project_memory(info, memory, mid, vectors)
+    total_first, first_low = first_norm(info, target, context_self, head, vectors)
+    key_cross, value_cross, query_cross = project_memory(info, memory, first_low, mid, vectors)
     context_cross, stats_cross = cross_attend(info, query_cross, key_cross, value_cross)
     output, second_low, active, du, df, do_cross, dz2, dc_cross, sums_ffn, sums_wide = ffn_block(
-        info, total_first, context_cross, cotangent, head, tail, vectors
+        info, total_first, context_cross, cotangent, mid, tail, vectors
     )
     grad_ffn = ffn_weights(second_low, du, active, df, pieces)
     dq_cross, dk_cross, dv_cross = cross_attend_back(
         info, query_cross, key_cross, value_cross, dc_cross, context_cross, stats_cross
     )
-    dz1, do_self, dc_self, sums_first = first_back(info, dz2, dq_cross, total_first, mid, vectors)
+    dz1, do_self, dc_self, sums_first = first_back(info, dz2, dq_cross, total_first, head, mid, vectors)
     grads = self_attend_back(info, queries, keys, values, dc_self, context_self, stats_self)
     memory, *grads = lax.optimization_barrier((memory, *grads))
     *grad_mid, sum_value = mid_weights(
@@ -1227,10 +1248,10 @@
     head = pack_head(
         dp[None],
         self_qkv,
-        cross_out,
+        self_out,
         (self_bias, cross_bias, ffn_in_bias.reshape(4, own), ffn_out_bias[None], norm_gain, norm_bias),
     )
-    mid = pick(jnp.concatenate([self_out[None], cross_qkv], 0), 0, dp)
+    mid = pick(jnp.concatenate([cross_out[None], cross_qkv], 0), 0, dp)
     head, mid = fence(join_depth(head, depth), mid)
     one, two = cut(head)
     one, two = join_pair(one, 1, side, "fsdp", 1), join_pair(two, 1, high, "dp", 2)
@@ -1338,8 +1359,8 @@
     width = target.shape[1]
     blocks = ffn_out.shape[0] * lax.axis_size("fsdp") // width
     split = lambda units: (units[None, 0::2], units[None, 1::2])
-    head = split(jnp.concatenate([gather(self_qkv, 1), gather(cross_out, 0)[None]], 0))
-    mid = split(jnp.concatenate([gather(self_out, 0)[None], gather(cross_qkv, 1)], 0))
+    head = split(jnp.concatenate([gather(self_qkv, 1), gather(self_out, 0)[None]], 0))
+    mid = split(jnp.concatenate([gather(cross_out, 0)[None], gather(cross_qkv, 1)], 0))
     ffn_in_w = jnp.swapaxes(gather(ffn_in, 0).reshape(width, blocks, width), 0, 1)
     tail = jnp.concatenate([ffn_in_w, gather(ffn_out, 0).reshape(blocks, width, width)], 1)[:, None]
     vectors = (

time: 423 us -> 416 us (0.983)
  starting transfers between devices: 38 us -> 33.7 us
    ppermute x24, starting transfers between devices: 29.1 us -> 22 us  [pair_swap(): lax.ppermute(array, axis, [(place, place ^ bit) for place in range(count)])]
  transfers between devices with their start and end apart: 38 -> 38, of which waited for: 19 -> 20; matrix products, arithmetic and copies ran while one was open for 1% -> 1% of each run, Pallas kernels for 49% -> 50%
where the time goes in v5:
time: 416 us; the launch traced here: 411 us
  Pallas kernels  261 us (63%)
  waiting for transfers between devices  82.9 us (20%)
  starting transfers between devices  33.7 us (8%)
  between operations  15.6 us (4%)
  local copies, waits for them, and re-layouts  11.8 us (3%)
  other arithmetic  5.67 us (1%)
    pallas_call x19, Pallas kernels, row_call(): pl.pallas_call(kernel, grid_spec=pltpu.PrefetchScalarGridSpec(num_scalar_...  166 us
    pallas_call x4, Pallas kernels, attend_call(): pl.pallas_call(functools.partial(kernel, len(start)), grid_spec=pltpu.Pre...  80.2 us
    ppermute x12, waiting for transfers between devices, ring(): lax.ppermute(array, axis, [(place, (place + shift) % count) for place in...  40.6 us
    ppermute x24, waiting for transfers between devices, pair_swap(): lax.ppermute(array, axis, [(place, place ^ bit) for place in range(count)])  40.3 us
    ppermute x24, starting transfers between devices, pair_swap(): lax.ppermute(array, axis, [(place, place ^ bit) for place in range(count)])  22 us
    pallas_call x1, Pallas kernels, ffn_weights(): pl.pallas_call(ffn_weights_kernel, grid=(blocks,), in_specs=[whole, part,...  14.6 us
    ppermute x12, starting transfers between devices, ring(): lax.ppermute(array, axis, [(place, (place + shift) % count) for place in...  11.1 us
  transfers between devices with their start and end apart: 38, of which 20 were waited for; matrix products, arithmetic and copies ran while one was open for 1% of the time, Pallas kernels for 50%

profile of v5, /device:TPU:9, one launch (start us, length us, event | category | flops | bytes accessed | tf_op | source)
XLA Modules:
  0.0 410.7 jit_solution(4852275542430950154)
XLA Ops:
  16.3 8.8 %collective-permute-done.1 = bf16[104,768]{1,0:T(8,128)(2,1)S(1)} collective-permute-done((bf16[104,768]{1,0:T(8,128)(2,1)}, bf16[104,768]{1,0:T(8,128)(2,1)S(1)}, u32[]{:S(2)}, u32[]{:S(2)}) %collective-permute-start.1) | collective-permute-done | bytes 159776 | tf_op jit(solution)/shard_map/ppermute | solution.py:1168
  30.4 5.5 %collective-permute-done.3 = bf16[4,48,768]{2,1,0:T(8,128)(2,1)S(1)} collective-permute-done((bf16[4,48,768]{2,1,0:T(8,128)(2,1)S(1)}, bf16[4,48,768]{2,1,0:T(8,128)(2,1)S(1)}, u32[]{:S(2)}, u32[]{:S(2)}) %collective-permute-start.3) | collective-permute-done | bytes 294944 | tf_op jit(solution)/shard_map/ppermute | solution.py:1163
  45.1 7.5 %collective-permute-done.9 = bf16[96,768]{1,0:T(8,128)(2,1)S(1)} collective-permute-done((bf16[96,768]{1,0:T(8,128)(2,1)S(1)}, bf16[96,768]{1,0:T(8,128)(2,1)S(1)}, u32[]{:S(2)}, u32[]{:S(2)}) %collective-permute-start.9) | collective-permute-done | bytes 147488 | tf_op jit(solution)/shard_map/ppermute | solution.py:1168
  59.3 3.8 collective-permute-start.10
  67.6 8.8 %project_self.1 = (bf16[1024,768]{1,0:T(8,128)(2,1)}, bf16[1024,768]{1,0:T(8,128)(2,1)}, bf16[1024,768]{1,0:T(8,128)(2,1)}) custom-call(s32[6]{0:T(128)} %pad_add_fusion.info, bf16[1024,768]{1,0:T(8,128)(2,1)} %x_hbm, bf16[8,2,96,768]{3,2,1,0:T(8,128)(2,1)} %bitcast.100, bf16[8,2,96,768]{3,2,1,0:T(8,128)(2,1)} %collective-permute-done.10.got.head_got, ...), custom_call_target="tpu_custom_call" | custom-call | flops 4831838208 | bytes 8388608 | tf_op jit(solution)/shard_map/project_self/pallas_call | solution.py:407
  78.3 9.5 %self_attend.1 = (bf16[1024,768]{1,0:T(8,128)(2,1)}, f32[6,4,1,512]{3,2,1,0:T(1,128)}) custom-call(s32[6]{0:T(128)} %pad_add_fusion.info, bf16[1024,768]{1,0:T(8,128)(2,1)} %get-tuple-element.165.q_ref, bf16[1024,768]{1,0:T(8,128)(2,1)} %get-tuple-element.166.k_ref, bf16[1024,768]{1,0:T(8,128)(2,1)} %get-tuple-element.167.v_ref), custom_call_target="tpu_custom_call" | custom-call | flops 19327352832 | bytes 8388608 | tf_op jit(solution)/shard_map/self_attend/pallas_call | solution.py:298
  92.1 3.7 collective-permute-start.15
  95.8 6.7 %first_norm.1 = (f32[1024,768]{1,0:T(8,128)}, bf16[1024,768]{1,0:T(8,128)(2,1)}) custom-call(s32[6]{0:T(128)} %pad_add_fusion.info, bf16[1024,768]{1,0:T(8,128)(2,1)} %x_hbm, bf16[1024,768]{1,0:T(8,128)(2,1)} %get-tuple-element.173.c_ref.o_ref.self_hbm, bf16[8,2,96,768]{3,2,1,0:T(8,128)(2,1)} %bitcast.101, ...), custom_call_target="tpu_custom_call" | custom-call | flops 2415919104 | bytes 8388608 | tf_op jit(solution)/shard_map/first_norm/pallas_call | solution.py:407
  102.5 19.6 %project_memory.1 = (bf16[4,1024,768]{2,1,0:T(8,128)(2,1)}, bf16[4,1024,768]{2,1,0:T(8,128)(2,1)}, bf16[1024,768]{1,0:T(8,128)(2,1)}) custom-call(s32[6]{0:T(128)} %pad_add_fusion.info, bf16[4,1024,768]{2,1,0:T(8,128)(2,1)} %m_ref.2, bf16[8,2,96,768]{3,2,1,0:T(8,128)(2,1)} %bitcast.92, bf16[8,2,96,768]{3,2,1,0:T(8,128)(2,1)} %collective-permute-done.15.got.query_got, ...), custom_call_target="tpu_custom_call" | custom-call | flops 9663676416 | bytes 8388608 | tf_op jit(solution)/shard_map/project_memory/pallas_call | solution.py:407
  122.1 22.2 %cross_attend.1 = (bf16[1024,768]{1,0:T(8,128)(2,1)}, f32[6,4,1,512]{3,2,1,0:T(1,128)}) custom-call(s32[6]{0:T(128)} %pad_add_fusion.info, bf16[1024,768]{1,0:T(8,128)(2,1)} %get-tuple-element.180.q_ref, bf16[4,1024,768]{2,1,0:T(8,128)(2,1)} %get-tuple-element.181.k_ref, bf16[4,1024,768]{2,1,0:T(8,128)(2,1)} %get-tuple-element.182.v_ref), custom_call_target="tpu_custom_call" | custom-call | flops 19327352832 | bytes 8388608 | tf_op jit(solution)/shard_map/cross_attend/pallas_call | solution.py:298
  146.3 38.9 %ffn_block.1 = (bf16[1024,768]{1,0:T(8,128)(2,1)}, bf16[1024,768]{1,0:T(8,128)(2,1)}, bf16[1024,3072]{1,0:T(8,128)(2,1)}, bf16[1024,3072]{1,0:T(8,128)(2,1)}, bf...) custom-call(s32[6]{0:T(128)} %pad_add_fusion.info, ...), custom_call_target="tpu_custom_call" | custom-call | flops 38654705664 | bytes 8388608 | tf_op jit(solution)/shard_map/ffn_block/pallas_call | solution.py:407
  185.2 14.6 %ffn_weights.1 = bf16[4,8,192,768]{3,2,1,0:T(8,128)(2,1)} custom-call(bf16[1024,768]{1,0:T(8,128)(2,1)} %get-tuple-element.268.h_ref, bf16[1024,3072]{1,0:T(8,128)(2,1)} %get-tuple-element.269.du_ref, bf16[1024,3072]{1,0:T(8,128)(2,1)} %get-tuple-element.270.a_ref, bf16[1024,768]{1,0:T(8,128)(2,1)} %get-tuple-element.271.df_ref), custom_call_target="tpu_custom_call" | custom-call | flops 9663676416 | bytes 8388608 | tf_op jit(solution)/shard_map/ffn_weights/pallas_call | solution.py:896
  199.9 35.4 %cross_attend_back.1 = (bf16[1024,768]{1,0:T(8,128)(2,1)}, bf16[4,1024,768]{2,1,0:T(8,128)(2,1)}, bf16[4,1024,768]{2,1,0:T(8,128)(2,1)}) custom-call(s32[6]{0:T(128)} %pad_add_fusion.info, bf16[1024,768]{1,0:T(8,128)(2,1)} %get-tuple-element.180.q_ref, bf16[4,1024,768]{2,1,0:T(8,128)(2,1)} %get-tuple-element.181.k_ref, ...), custom_call_target="tpu_custom_call" | custom-call | flops 38654705664 | bytes 8388608 | tf_op jit(solution)/shard_map/cross_attend_back/pallas_call | solution.py:298
  235.3 10.9 %first_back.1 = (f32[1024,768]{1,0:T(8,128)}, bf16[1024,768]{1,0:T(8,128)(2,1)}, bf16[1024,768]{1,0:T(8,128)(2,1)}, f32[8,768]{1,0:T(8,128)}) custom-call(s32[6]{0:T(128)} %pad_add_fusion.info, f32[1024,768]{1,0:T(8,128)} %get-tuple-element.187.dz2_ref, bf16[1024,768]{1,0:T(8,128)(2,1)} %get-tuple-element.190.dq_ref.dq_hbm, ...), custom_call_target="tpu_custom_call" | custom-call | flops 4831838208 | bytes 8388608 | tf_op jit(solution)/shard_map/first_back/pallas_call | solution.py:407
  246.2 13.0 %self_attend_back.1 = (bf16[1024,768]{1,0:T(8,128)(2,1)}, bf16[1024,768]{1,0:T(8,128)(2,1)}, bf16[1024,768]{1,0:T(8,128)(2,1)}) custom-call(s32[6]{0:T(128)} %pad_add_fusion.info, bf16[1024,768]{1,0:T(8,128)(2,1)} %get-tuple-element.165.q_ref, bf16[1024,768]{1,0:T(8,128)(2,1)} %get-tuple-element.166.k_ref, bf16[1024,768]{1,0:T(8,128)(2,1)} %get-tuple-element.167.v_ref, ...), custom_call_target="tpu_custom_call" | custom-call | flops 38654705664 | bytes 8388608 | tf_op jit(solution)/shard_map/self_attend_back/pallas_call | solution.py:298
  259.2 20.0 %mid_weights.1 = (bf16[1536,768]{1,0:T(8,128)(2,1)}, bf16[1536,768]{1,0:T(8,128)(2,1)}, f32[1,768]{1,0:T(1,128)}) custom-call(s32[6]{0:T(128)} %pad_add_fusion.info, bf16[4,1024,768]{2,1,0:T(8,128)(2,1)} %m_ref.2, bf16[4,1024,768]{2,1,0:T(8,128)(2,1)} %get-tuple-element.255.dk_ref, bf16[4,1024,768]{2,1,0:T(8,128)(2,1)} %get-tuple-element.198.dv_ref, ...), custom_call_target="tpu_custom_call" | custom-call | flops 9663676416 | bytes 8388608 | tf_op jit(solution)/shard_map/mid_weights/pallas_call | solution.py:407
  279.4 11.9 %self_weights.1 = (bf16[1568,768]{1,0:T(8,128)(2,1)}, bf16[1568,768]{1,0:T(8,128)(2,1)}) custom-call(s32[6]{0:T(128)} %pad_add_fusion.info, bf16[1024,768]{1,0:T(8,128)(2,1)} %x_hbm, bf16[1024,768]{1,0:T(8,128)(2,1)} %get-tuple-element.205.q_hbm.q_ref, bf16[1024,768]{1,0:T(8,128)(2,1)} %get-tuple-element.206.k_hbm.k_ref, ...), custom_call_target="tpu_custom_call" | custom-call | flops 4831838208 | bytes 8388608 | tf_op jit(solution)/shard_map/self_weights/pallas_call | solution.py:407
  296.3 10.0 %target_back.1 = f32[1024,768]{1,0:T(8,128)} custom-call(s32[6]{0:T(128)} %pad_add_fusion.info, f32[1024,768]{1,0:T(8,128)} %get-tuple-element.223.z_ref, bf16[1024,768]{1,0:T(8,128)(2,1)} %get-tuple-element.205.q_hbm.q_ref, bf16[1024,768]{1,0:T(8,128)(2,1)} %get-tuple-element.206.k_hbm.k_ref, bf16[1024,768]{1,0:T(8,128)(2,1)} %get-tuple-element.207.v_hbm.v_ref, ...), custom_call_target="tpu_custom_call" | custom-call | flops 4831838208 | bytes 8388608 | tf_op jit(solution)/shard_map/target_back/pallas_call | solution.py:407
  306.4 11.9 %collective-permute-done.17.got_a = bf16[384,768]{1,0:T(8,128)(2,1)S(1)} collective-permute-done((bf16[384,768]{1,0:T(8,128)(2,1)}, bf16[384,768]{1,0:T(8,128)(2,1)S(1)}, u32[]{:S(2)}, u32[]{:S(2)}) %collective-permute-start.17) | collective-permute-done | bytes 589856 | tf_op jit(solution)/shard_map/ppermute | solution.py:1163
  328.4 10.4 %memory_back.2.refs_0_ = f32[4,1024,768]{2,1,0:T(8,128)} custom-call(s32[6]{0:T(128)} %pad_add_fusion.info, bf16[4,1024,768]{2,1,0:T(8,128)(2,1)} %get-tuple-element.255.dk_ref, bf16[4,1024,768]{2,1,0:T(8,128)(2,1)} %get-tuple-element.198.dv_ref, bf16[8,2,96,768]{3,2,1,0:T(8,128)(2,1)} %bitcast.96, bf16[8,2,96,768]{3,2,1,0:T(8,128)(2,1)} %collective-permute-done.15.got.query_got), custom_call_target="tpu_custom_call" | custom-call | flops 4831838208 | bytes 8388608 | tf_op jit(solution)/shard_map/memory_back/pallas_call | solution.py:407
  338.8 9.7 %collective-permute-done.20.got_a = bf16[192,768]{1,0:T(8,128)(2,1)S(1)} collective-permute-done((bf16[192,768]{1,0:T(8,128)(2,1)S(1)}, bf16[192,768]{1,0:T(8,128)(2,1)S(1)}, u32[]{:S(2)}, u32[]{:S(2)}) %collective-permute-start.20) | collective-permute-done | bytes 294944 | tf_op jit(solution)/shard_map/ppermute | solution.py:1163
  356.7 10.6 %memory_back.3 = f32[4,1024,768]{2,1,0:T(8,128)} custom-call(s32[6]{0:T(128)} %pad_add_fusion.info, bf16[4,1024,768]{2,1,0:T(8,128)(2,1)} %get-tuple-element.255.dk_ref, bf16[4,1024,768]{2,1,0:T(8,128)(2,1)} %get-tuple-element.198.dv_ref, bf16[8,2,96,768]{3,2,1,0:T(8,128)(2,1)} %bitcast.97, ...), custom_call_target="tpu_custom_call", output_to_operand_aliasing={{}: (5, {})} | custom-call | flops 4831838208 | bytes 8388608 | tf_op jit(solution)/shard_map/memory_back/pallas_call | solution.py:407
  376.4 10.6 %collective-permute-done.31 = bf16[128,768]{1,0:T(8,128)(2,1)S(1)} collective-permute-done((bf16[128,768]{1,0:T(8,128)(2,1)S(1)}, bf16[128,768]{1,0:T(8,128)(2,1)S(1)}, u32[]{:S(2)}, u32[]{:S(2)}) %collective-permute-start.31) | collective-permute-done | bytes 196640 | tf_op jit(solution)/shard_map/ppermute | solution.py:1168
  391.5 5.1 %collective-permute-done.33 = bf16[96,768]{1,0:T(8,128)(2,1)S(1)} collective-permute-done((bf16[96,768]{1,0:T(8,128)(2,1)S(1)}, bf16[96,768]{1,0:T(8,128)(2,1)S(1)}, u32[]{:S(2)}, u32[]{:S(2)}) %collective-permute-start.33) | collective-permute-done | bytes 147488 | tf_op jit(solution)/shard_map/ppermute | solution.py:1163
  (172 shorter events, 85.7 us)
Async XLA Ops:
  7.2 139.1 %all-gather.2.cloned.1.call-start = ((), (), s32[]{:S(2)}) async-start(), calls=%async_computation.1 | async-start | bytes 9732096 | tf_op jit(solution)/shard_map/all_gather | solution.py:1268
  11.7 13.4 %collective-permute-start.1 = (bf16[104,768]{1,0:T(8,128)(2,1)}, bf16[104,768]{1,0:T(8,128)(2,1)S(1)}, u32[]{:S(2)}, u32[]{:S(2)}) collective-permute-start(bf16[104,768]{1,0:T(8,128)(2,1)} %pack_head.1), channel_id=1, source_target_pairs={{0,4},{1,5},{2,6},{3,7},{4,0},{5,1},{6,2},{7,3},{8,12},{9,13},{10,... | collective-permute-start | bytes 479240 | tf_op jit(solution)/shard_map/ppermute | solution.py:1168
  12.8 15.0 %collective-permute-start.2 = (bf16[104,768]{1,0:T(8,128)(2,1)}, bf16[104,768]{1,0:T(8,128)(2,1)S(1)}, u32[]{:S(2)}, u32[]{:S(2)}) collective-permute-start(bf16[104,768]{1,0:T(8,128)(2,1)} %pack_head.1), channel_id=1, source_target_pairs={{0,6},{1,7},{2,0},{3,1},{4,2},{5,3},{6,4},{7,5},{8,14},{9,15},{10,... | collective-permute-start | bytes 479240 | tf_op jit(solution)/shard_map/ppermute | solution.py:1168
  38.3 14.3 %collective-permute-start.9 = (bf16[96,768]{1,0:T(8,128)(2,1)S(1)}, bf16[96,768]{1,0:T(8,128)(2,1)S(1)}, u32[]{:S(2)}, u32[]{:S(2)}) collective-permute-start(bf16[96,768]{1,0:T(8,128)(2,1)S(1)} %fusion.3), channel_id=1, source_target_pairs={{0,6},{1,7},{2,0},{3,1},{4,2},{5,3},{6,4},{7,5},{8,14},{9,15},{10,... | collective-permute-start | bytes 442376 | tf_op jit(solution)/shard_map/ppermute | solution.py:1168
  39.7 14.1 %collective-permute-start.6 = (bf16[4,2,56,768]{3,2,0,1:T(8,128)(2,1)S(1)}, bf16[4,2,56,768]{3,2,0,1:T(8,128)(2,1)S(1)}, u32[]{:S(2)}, u32[]{:S(2)}) collective-permute-start(bf16[4,2,56,768]{3,2,0,1:T(8,128)(2,1)S(1)} %pad_maximum_fusion.2), channel_id=1, source_target_pairs={{0,1},{1,0},{2,3},{3,2},{4,5},{5,4},{6,7},{7,6},{8,9},{9,8},{10,11... | collective-permute-start | bytes 2064392 | tf_op jit(solution)/shard_map/ppermute | solution.py:1163
  39.9 12.7 %collective-permute-start.5 = (bf16[4,2,48,768]{3,2,1,0:T(8,128)(2,1)S(1)}, bf16[4,2,48,768]{3,2,1,0:T(8,128)(2,1)S(1)}, u32[]{:S(2)}, u32[]{:S(2)}) collective-permute-start(bf16[4,2,48,768]{3,2,1,0:T(8,128)(2,1)S(1)} %pad_maximum_fusion.3), channel_id=1, source_target_pairs={{0,16},{8,24},{16,0},{24,8},{1,17},{9,25},{17,1},{25,9},{2,18},{10... | collective-permute-start | bytes 1769480 | tf_op jit(solution)/shard_map/ppermute | solution.py:1163
  58.7 310.7 %reduce-scatter.2.cloned.1.call-start = ((), (), s32[]{:S(2)}) async-start(), calls=%async_computation.2 | async-start | bytes 9732096 | tf_op jit(solution)/shard_map/reduce_scatter | solution.py:1288
  76.6 14.6 %collective-permute-start.14 = (bf16[4,2,48,768]{3,2,0,1:T(8,128)(2,1)S(1)}, bf16[4,2,48,768]{3,2,0,1:T(8,128)(2,1)S(1)}, u32[]{:S(2)}, u32[]{:S(2)}) collective-permute-start(bf16[4,2,48,768]{3,2,0,1:T(8,128)(2,1)S(1)} %pad_maximum_fusion.5), channel_id=1, source_target_pairs={{0,1},{1,0},{2,3},{3,2},{4,5},{5,4},{6,7},{7,6},{8,9},{9,8},{10,11... | collective-permute-start | bytes 1769480 | tf_op jit(solution)/shard_map/ppermute | solution.py:1163
  77.4 14.0 %collective-permute-start.13 = (bf16[4,2,48,768]{3,2,0,1:T(8,128)(2,1)S(1)}, bf16[4,2,48,768]{3,2,0,1:T(8,128)(2,1)S(1)}, u32[]{:S(2)}, u32[]{:S(2)}) collective-permute-start(bf16[4,2,48,768]{3,2,0,1:T(8,128)(2,1)S(1)} %pad_maximum_fusion.4), channel_id=1, source_target_pairs={{0,16},{8,24},{16,0},{24,8},{1,17},{9,25},{17,1},{25,9},{2,18},{10... | collective-permute-start | bytes 1769480 | tf_op jit(solution)/shard_map/ppermute | solution.py:1163
  279.2 12.1 %collective-permute-start.16 = (bf16[1536,768]{1,0:T(8,128)(2,1)}, bf16[1536,768]{1,0:T(8,128)(2,1)}, u32[]{:S(2)}, u32[]{:S(2)}) collective-permute-start(bf16[1536,768]{1,0:T(8,128)(2,1)} %get-tuple-element.203), channel_id=1, source_target_pairs={{0,8},{8,0},{16,24},{24,16},{1,9},{9,1},{17,25},{25,17},{2,10},{10... | collective-permute-start | bytes 7077896 | tf_op jit(solution)/shard_map/ppermute | solution.py:1163
  295.8 23.2 %collective-permute-start.19 = (bf16[1568,768]{1,0:T(8,128)(2,1)}, bf16[1568,768]{1,0:T(8,128)(2,1)}, u32[]{:S(2)}, u32[]{:S(2)}) collective-permute-start(bf16[1568,768]{1,0:T(8,128)(2,1)} %get-tuple-element.222), channel_id=1, source_target_pairs={{0,8},{8,0},{16,24},{24,16},{1,9},{9,1},{17,25},{25,17},{2,10},{10... | collective-permute-start | bytes 7225352 | tf_op jit(solution)/shard_map/ppermute | solution.py:1163
  296.3 21.9 %collective-permute-start.17 = (bf16[384,768]{1,0:T(8,128)(2,1)}, bf16[384,768]{1,0:T(8,128)(2,1)S(1)}, u32[]{:S(2)}, u32[]{:S(2)}) collective-permute-start(bf16[384,768]{1,0:T(8,128)(2,1)} %get-tuple-element.220), channel_id=1, source_target_pairs={{0,16},{8,24},{16,0},{24,8},{1,17},{9,25},{17,1},{25,9},{2,18},{10... | collective-permute-start | bytes 1769480 | tf_op jit(solution)/shard_map/ppermute | solution.py:1163
  296.3 22.7 %collective-permute-start.18 = (bf16[384,768]{1,0:T(8,128)(2,1)}, bf16[384,768]{1,0:T(8,128)(2,1)}, u32[]{:S(2)}, u32[]{:S(2)}) collective-permute-start(bf16[384,768]{1,0:T(8,128)(2,1)} %get-tuple-element.221), channel_id=1, source_target_pairs={{0,1},{1,0},{2,3},{3,2},{4,5},{5,4},{6,7},{7,6},{8,9},{9,8},{10,11... | collective-permute-start | bytes 1769480 | tf_op jit(solution)/shard_map/ppermute | solution.py:1163
  325.4 24.7 %collective-permute-start.22 = (bf16[416,768]{1,0:T(8,128)(2,1)}, bf16[416,768]{1,0:T(8,128)(2,1)S(1)}, u32[]{:S(2)}, u32[]{:S(2)}) collective-permute-start(bf16[416,768]{1,0:T(8,128)(2,1)} %get-tuple-element.238), channel_id=1, source_target_pairs={{0,16},{8,24},{16,0},{24,8},{1,17},{9,25},{17,1},{25,9},{2,18},{10... | collective-permute-start | bytes 1916936 | tf_op jit(solution)/shard_map/ppermute | solution.py:1163
  325.8 24.4 %collective-permute-start.23 = (bf16[384,768]{1,0:T(8,128)(2,1)}, bf16[384,768]{1,0:T(8,128)(2,1)S(1)}, u32[]{:S(2)}, u32[]{:S(2)}) collective-permute-start(bf16[384,768]{1,0:T(8,128)(2,1)} %get-tuple-element.239), channel_id=1, source_target_pairs={{0,1},{1,0},{2,3},{3,2},{4,5},{5,4},{6,7},{7,6},{8,9},{9,8},{10,11... | collective-permute-start | bytes 1769480 | tf_op jit(solution)/shard_map/ppermute | solution.py:1163
  325.8 22.7 %collective-permute-start.20 = (bf16[192,768]{1,0:T(8,128)(2,1)S(1)}, bf16[192,768]{1,0:T(8,128)(2,1)S(1)}, u32[]{:S(2)}, u32[]{:S(2)}) collective-permute-start(bf16[192,768]{1,0:T(8,128)(2,1)S(1)} %get-tuple-element.236), channel_id=1, source_target_pairs={{0,1},{1,0},{2,3},{3,2},{4,5},{5,4},{6,7},{7,6},{8,9},{9,8},{10,11... | collective-permute-start | bytes 884744 | tf_op jit(solution)/shard_map/ppermute | solution.py:1163
  327.2 22.2 %collective-permute-start.21 = (bf16[192,768]{1,0:T(8,128)(2,1)S(1)}, bf16[192,768]{1,0:T(8,128)(2,1)S(1)}, u32[]{:S(2)}, u32[]{:S(2)}) collective-permute-start(bf16[192,768]{1,0:T(8,128)(2,1)S(1)} %get-tuple-element.237), channel_id=1, source_target_pairs={{0,16},{8,24},{16,0},{24,8},{1,17},{9,25},{17,1},{25,9},{2,18},{10... | collective-permute-start | bytes 884744 | tf_op jit(solution)/shard_map/ppermute | solution.py:1163
  352.4 16.2 %collective-permute-start.24 = (bf16[224,768]{1,0:T(8,128)(2,1)}, bf16[224,768]{1,0:T(8,128)(2,1)S(1)}, u32[]{:S(2)}, u32[]{:S(2)}) collective-permute-start(bf16[224,768]{1,0:T(8,128)(2,1)} %get-tuple-element.253), channel_id=1, source_target_pairs={{0,1},{1,0},{2,3},{3,2},{4,5},{5,4},{6,7},{7,6},{8,9},{9,8},{10,11... | collective-permute-start | bytes 1032200 | tf_op jit(solution)/shard_map/ppermute | solution.py:1163
  352.5 16.1 %collective-permute-start.25 = (bf16[192,768]{1,0:T(8,128)(2,1)}, bf16[192,768]{1,0:T(8,128)(2,1)S(1)}, u32[]{:S(2)}, u32[]{:S(2)}) collective-permute-start(bf16[192,768]{1,0:T(8,128)(2,1)} %get-tuple-element.254), channel_id=1, source_target_pairs={{0,16},{8,24},{16,0},{24,8},{1,17},{9,25},{17,1},{25,9},{2,18},{10... | collective-permute-start | bytes 884744 | tf_op jit(solution)/shard_map/ppermute | solution.py:1163
  353.1 14.2 %collective-permute-start.26 = (bf16[96,768]{1,0:T(8,128)(2,1)S(1)}, bf16[96,768]{1,0:T(8,128)(2,1)S(1)}, u32[]{:S(2)}, u32[]{:S(2)}) collective-permute-start(bf16[96,768]{1,0:T(8,128)(2,1)S(1)} %get-tuple-element.257), channel_id=1, source_target_pairs={{0,2},{1,3},{2,4},{3,5},{4,6},{5,7},{6,0},{7,1},{8,10},{9,11},{10,... | collective-permute-start | bytes 442376 | tf_op jit(solution)/shard_map/ppermute | solution.py:1168
  355.2 12.1 %collective-permute-start.27 = (bf16[96,768]{1,0:T(8,128)(2,1)S(1)}, bf16[96,768]{1,0:T(8,128)(2,1)S(1)}, u32[]{:S(2)}, u32[]{:S(2)}) collective-permute-start(bf16[96,768]{1,0:T(8,128)(2,1)S(1)} %get-tuple-element.258), channel_id=1, source_target_pairs={{0,4},{1,5},{2,6},{3,7},{4,0},{5,1},{6,2},{7,3},{8,12},{9,13},{10,... | collective-permute-start | bytes 442376 | tf_op jit(solution)/shard_map/ppermute | solution.py:1168
  370.4 19.9 %collective-permute-start.29 = (bf16[288,768]{1,0:T(8,128)(2,1)S(1)}, bf16[288,768]{1,0:T(8,128)(2,1)S(1)}, u32[]{:S(2)}, u32[]{:S(2)}) collective-permute-start(bf16[288,768]{1,0:T(8,128)(2,1)S(1)} %pad_maximum_fusion.6), channel_id=1, source_target_pairs={{0,16},{8,24},{16,0},{24,8},{1,17},{9,25},{17,1},{25,9},{2,18},{10... | collective-permute-start | bytes 1327112 | tf_op jit(solution)/shard_map/ppermute | solution.py:1163
  371.6 15.4 %collective-permute-start.31 = (bf16[128,768]{1,0:T(8,128)(2,1)S(1)}, bf16[128,768]{1,0:T(8,128)(2,1)S(1)}, u32[]{:S(2)}, u32[]{:S(2)}) collective-permute-start(bf16[128,768]{1,0:T(8,128)(2,1)S(1)} %get-tuple-element.278), channel_id=1, source_target_pairs={{0,4},{1,5},{2,6},{3,7},{4,0},{5,1},{6,2},{7,3},{8,12},{9,13},{10,... | collective-permute-start | bytes 589832 | tf_op jit(solution)/shard_map/ppermute | solution.py:1168
  372.3 18.0 %collective-permute-start.32 = (bf16[128,768]{1,0:T(8,128)(2,1)S(1)}, bf16[128,768]{1,0:T(8,128)(2,1)S(1)}, u32[]{:S(2)}, u32[]{:S(2)}) collective-permute-start(bf16[128,768]{1,0:T(8,128)(2,1)S(1)} %get-tuple-element.279), channel_id=1, source_target_pairs={{0,6},{1,7},{2,0},{3,1},{4,2},{5,3},{6,4},{7,5},{8,14},{9,15},{10,... | collective-permute-start | bytes 589832 | tf_op jit(solution)/shard_map/ppermute | solution.py:1168
  (30 other events, 290.9 us)
Sparse Core Ops, SparseCore 0:
  58.9 87.4 all-gather.1
  200.0 142.5 reduce-scatter.1
